TPU v7x, 128 devices: a whole 4x4x4 slice. The times are simulated.
128 devices in a mesh: arc: 64 (over y, z, x_lo, core), circ: 2 (over x_hi).
Axes of the slice: x: 4 (x_hi: 2, x_lo: 2; x = x_hi * 2 + x_lo), y: 4, z: 4, core: 2. Of those that a mesh axis runs over, the one named last changes fastest.
Arguments:
- displacement: float32 [3, 32768, 256], P(None, 'arc', 'circ'), may hold values from -1.2 to 1.2
- velocity: float32 [3, 32768, 256], P(None, 'arc', 'circ'), may hold values from -1.8 to 1.8
- node_mass: float32 [32768, 256], P('arc', 'circ'), may hold values from 0.5 to 2
- wall_stiff: float32 [32768, 256], P('arc', 'circ'), may hold values from 0.5 to 2
- pad_state: float32 [64, 16, 256], P('arc', None, 'circ'), may hold values from 0 to 0.3
- roller_lift: float32 [40], replicated, may hold values from 0.2 to 0.6
- contact_rows: int32 [4, 40, 16], replicated, may hold values from 0 to 32767, as said below
- roller_slot: int32 [40], replicated, may hold values from 0 to 63, as said below
Outputs:
- displacement_out: float32 [3, 32768, 256], P(None, 'arc', 'circ')
- velocity_out: float32 [3, 32768, 256], P(None, 'arc', 'circ')
- pad_out: float32 [64, 16, 256], P('arc', None, 'circ')
Inputs may be any that keep to these rules, and one draw needn't show every extreme that they name: contact_rows[s, r] lie within 20 cycles of cycle r * 32767 // 39, clipped to the pipe; cycles may repeat. `roller_slot`: distinct pad slots; slot t lies on index t // 1 of arc.
All inputs are finite; a program needn't handle non-finite values.
Results may differ from a plain program's by a relative error of at most 0.000084.
Values sent between devices are 32-bit elements; how exact they have to be, the bound alone decides.
No kernel may reach another device: no remote copies, remote signals or barrier semaphores. Data moves between devices by JAX's collectives and lax.ppermute only.
A program may use at most 64 MiB of HBM per device.

v0:
```python
import math

import jax
import jax.numpy as jnp
from jax import lax
from jax.sharding import PartitionSpec as P

STEPS = 4


time_step = 0.1
gravity = 0.2
contact_stiff = 2.0
cradle_curve = 0.5
pad_rate = 0.2
pad_stiff = 1.0


def padded(block, sides, width, periodic):
    for axis, dim in sides:
        count = lax.axis_size(axis)
        forward = [(i, i + 1) for i in range(count - 1)]
        if periodic:
            forward.append((count - 1, 0))
        backward = [(target, source) for source, target in forward]
        low = lax.ppermute(
            lax.slice_in_dim(block, block.shape[dim] - width, None, axis=dim), axis, forward
        )
        high = lax.ppermute(lax.slice_in_dim(block, 0, width, axis=dim), axis, backward)
        block = jnp.concatenate([low, block, high], axis=dim)
    return block


def directions(first_col, count, circ_total):
    columns = (first_col + jnp.arange(count, dtype=jnp.int32)).astype(jnp.float32)
    phases = 2.0 * math.pi * (columns + 0.5) / circ_total
    step_angle = 2.0 * math.pi / circ_total
    chord_len = 2.0 * math.sin(step_angle / 2.0)
    length = math.sqrt(step_angle * step_angle + chord_len * chord_len)
    cos_phase = jnp.cos(phases)
    sin_phase = jnp.sin(phases)
    hoop_dir = (jnp.zeros_like(phases), cos_phase, sin_phase)
    diag_dir = (
        jnp.full_like(phases, step_angle / length),
        chord_len * cos_phase / length,
        chord_len * sin_phase / length,
    )
    anti_dir = (
        jnp.full_like(phases, -step_angle / length),
        chord_len * cos_phase / length,
        chord_len * sin_phase / length,
    )
    return (hoop_dir, diag_dir, anti_dir)


def spring_pull(centre, partner, spring_k, unit_dir):
    stretch = spring_k * (
        unit_dir[0] * (partner[0] - centre[0])
        + unit_dir[1] * (partner[1] - centre[1])
        + unit_dir[2] * (partner[2] - centre[2])
    )
    return jnp.stack([stretch * unit_dir[0], stretch * unit_dir[1], stretch * unit_dir[2]])


def internal_force(ext_shift, ext_k, first_col, circ_total):
    cycle_count = ext_shift.shape[1] - 2
    col_count = ext_shift.shape[2] - 2
    hoop_dir, diag_dir, anti_dir = directions(first_col, col_count + 2, circ_total)
    axial_dir = (1.0, 0.0, 0.0)
    centre = ext_shift[:, 1 : cycle_count + 1, 1 : col_count + 1]

    def neighbour(cycle_step, col_step):
        return ext_shift[
            :,
            1 + cycle_step : cycle_count + 1 + cycle_step,
            1 + col_step : col_count + 1 + col_step,
        ]

    def element_at(cycle_off, col_off):
        return ext_k[cycle_off : cycle_off + cycle_count, col_off : col_off + col_count]

    def pick(vector, col_off):
        return tuple((part_v[col_off : col_off + col_count] for part_v in vector))

    internal = spring_pull(
        centre, neighbour(1, 0), 0.5 * (element_at(1, 0) + element_at(1, 1)), axial_dir
    )
    internal = internal + spring_pull(
        centre, neighbour(-1, 0), 0.5 * (element_at(0, 0) + element_at(0, 1)), axial_dir
    )
    internal = internal + spring_pull(
        centre, neighbour(0, 1), 0.5 * (element_at(1, 1) + element_at(0, 1)), pick(hoop_dir, 1)
    )
    internal = internal + spring_pull(
        centre, neighbour(0, -1), 0.5 * (element_at(1, 0) + element_at(0, 0)), pick(hoop_dir, 0)
    )
    internal = internal + spring_pull(centre, neighbour(1, 1), element_at(1, 1), pick(diag_dir, 1))
    internal = internal + spring_pull(
        centre, neighbour(-1, -1), element_at(0, 0), pick(diag_dir, 0)
    )
    internal = internal + spring_pull(centre, neighbour(1, -1), element_at(1, 0), pick(anti_dir, 0))
    internal = internal + spring_pull(centre, neighbour(-1, 1), element_at(0, 1), pick(anti_dir, 1))
    return internal


def roller_press(lift_up, shift_y, shift_z, pad_now, sin_angle, cos_angle):
    lateral = sin_angle + shift_y
    intrusion = lift_up + cradle_curve * lateral * lateral - (1.0 - cos_angle) - shift_z - pad_now
    contact_load = contact_stiff * jnp.maximum(intrusion, 0.0)
    normal_load = contact_load / jnp.sqrt(
        1.0 + 4.0 * cradle_curve * cradle_curve * lateral * lateral
    )
    return (
        -2.0 * cradle_curve * lateral * normal_load,
        normal_load,
        pad_now + pad_rate * (contact_load - pad_stiff * pad_now),
    )


def extend_field(field_in):
    widened = padded(field_in, (("circ", 2),), 1, True)
    return padded(widened, (("arc", 1),), 1, False)


def match_fold(target_keys, pieces):
    match = (target_keys[:, None] == pieces[1][None, :]).astype(jnp.float32)
    return jnp.dot(match, pieces[0], precision=lax.Precision.HIGHEST)


def local(
    displacement, velocity, node_mass, wall_stiff, pad_state, roller_lift, contact_rows, roller_slot
):
    cycle_dev = displacement.shape[1]
    circ_dev = displacement.shape[2]
    rolls_dev = pad_state.shape[0]
    slot_cap = pad_state.shape[1]
    roller_total = roller_lift.shape[0]
    arc_count = lax.axis_size("arc")
    cycle_total = cycle_dev * arc_count
    circ_total = circ_dev * lax.axis_size("circ")
    cycle_base = lax.axis_index("arc") * cycle_dev
    col_base = lax.axis_index("circ") * circ_dev
    cycle_ids = cycle_base + jnp.arange(cycle_dev, dtype=jnp.int32)
    element_k = jnp.where((cycle_ids < cycle_total - 1)[:, None], wall_stiff, jnp.float32(0.0))
    angles = (
        2.0
        * math.pi
        * (col_base + jnp.arange(circ_dev, dtype=jnp.int32)).astype(jnp.float32)
        / circ_total
    )
    sin_angle = jnp.sin(angles)
    cos_angle = jnp.cos(angles)
    roller_ids = jnp.arange(roller_total, dtype=jnp.int32)
    spacing = (cycle_total - 1) // (roller_total - 1)
    reach = slot_cap + STEPS
    local_most = (cycle_dev + 2 * reach) // spacing + 1
    centres = roller_ids * (cycle_total - 1) // (roller_total - 1)
    first_roll = jnp.sum((centres < cycle_base - reach).astype(jnp.int32))
    local_ids = first_roll + jnp.arange(local_most, dtype=jnp.int32)
    safe_ids = jnp.clip(local_ids, 0, roller_total - 1)
    local_valid = (local_ids < roller_total) & (
        centres[safe_ids] <= cycle_base + cycle_dev - 1 + reach
    )
    local_key = jnp.where(local_valid, local_ids, -2).astype(jnp.float32)
    slot_ids = lax.axis_index("arc") * rolls_dev + jnp.arange(rolls_dev, dtype=jnp.int32)
    own_table = (roller_slot[None, :] == slot_ids[:, None]).astype(jnp.float32)
    assigned = jnp.sum(own_table, axis=1) > 0.5
    assigned_f = assigned.astype(jnp.float32)
    slot_key = (
        jnp.dot(own_table, (roller_ids + 1).astype(jnp.float32), precision=lax.Precision.HIGHEST)
        - 1.0
    )
    lift_own = jnp.dot(own_table, roller_lift, precision=lax.Precision.HIGHEST)
    pad_now = pad_state
    ext_k = element_k
    for step_index in range(STEPS):
        if step_index == 0:
            widened = extend_field(jnp.concatenate([displacement, element_k[None]], axis=0))
            ext_shift = widened[:3]
            ext_k = widened[3]
        else:
            ext_shift = extend_field(displacement)
        internal = internal_force(ext_shift, ext_k, col_base - 1, circ_total)
        cycle_list = contact_rows[step_index][safe_ids]
        local_cycle = cycle_list - cycle_base
        held_mask = ((local_cycle >= 0) & (local_cycle < cycle_dev) & local_valid[:, None]).astype(
            jnp.float32
        )
        local_cycle = jnp.clip(local_cycle, 0, cycle_dev - 1)
        row_major = jnp.transpose(displacement[1:3], (1, 0, 2))
        row_data = row_major[local_cycle] * held_mask[:, :, None, None]
        flat_rows = row_data.reshape(local_most, slot_cap * 2 * circ_dev)
        received = match_fold(
            slot_key,
            (
                lax.all_gather(flat_rows, "arc", axis=0, tiled=True),
                lax.all_gather(local_key, "arc", axis=0, tiled=True),
            ),
        )
        received = received.reshape(rolls_dev, slot_cap, 2, circ_dev)
        force_y, force_z, pad_new = roller_press(
            lift_own[:, None, None],
            received[:, :, 0],
            received[:, :, 1],
            pad_now,
            sin_angle,
            cos_angle,
        )
        own_force = jnp.stack([force_y, force_z], axis=2) * assigned_f[:, None, None, None]
        pad_now = jnp.where(assigned[:, None, None], pad_new, pad_now)
        returned = match_fold(
            local_key,
            (
                lax.all_gather(
                    own_force.reshape(rolls_dev, slot_cap * 2 * circ_dev), "arc", axis=0, tiled=True
                ),
                lax.all_gather(slot_key, "arc", axis=0, tiled=True),
            ),
        )
        row_force = (
            returned.reshape(local_most, slot_cap, 2, circ_dev) * held_mask[:, :, None, None]
        )
        node_force = (
            jnp.zeros((cycle_dev, 2, circ_dev), jnp.float32)
            .at[local_cycle.reshape(-1)]
            .add(row_force.reshape(-1, 2, circ_dev))
        )
        node_force = jnp.transpose(node_force, (1, 0, 2))
        total_force = internal + jnp.stack(
            [jnp.zeros_like(node_mass), node_force[0], node_force[1] - gravity * node_mass]
        )
        velocity = velocity + time_step * total_force / node_mass
        displacement = displacement + time_step * velocity
    return (displacement, velocity, pad_now)


def solution(mesh):
    placed = (
        P(None, "arc", "circ"),
        P(None, "arc", "circ"),
        P("arc", "circ"),
        P("arc", "circ"),
        P("arc", None, "circ"),
        P(),
        P(),
        P(),
    )
    return jax.shard_map(
        local,
        mesh=mesh,
        in_specs=placed,
        out_specs=(P(None, "arc", "circ"), P(None, "arc", "circ"), P("arc", None, "circ")),
        check_vma=False,
    )
```

profile of v0, /device:TPU:0, one launch (start us, length us, event | category | flops | bytes accessed | tf_op | source)
XLA Modules:
  0.0 988.8 jit_solution(6197635722201510432)
XLA Ops:
  12.7 3.2 collective-permute-start
  30.8 147.3 %all-reduce.2 = (f32[64]{0:T(128)S(1)}, f32[64]{0:T(128)S(1)}) all-reduce(f32[64]{0:T(128)S(1)} %dynamic-update-slice.6, f32[64]{0:T(128)S(1)} %dynamic-update-slice.5), channel_id=1, replica_groups=mesh['arc'=64,'circ'=2] {'arc'}, use_global_device_ids=true, to_apply=%add.1 | all-reduce | flops 128 | bytes 1024
  183.6 3.1 reshape.1472
  190.8 3.2 pad_maximum_fusion
  202.9 85.0 %all-gather.19.cloned.1.call-done = f32[64,1,4096]{2,1,0:T(1,128)} async-done(((f32[1,1,4096]{2,1,0:T(1,128)}), f32[64,1,4096]{2,1,0:T(1,128)}) %all-gather.19.cloned.1.call-update) | async-done | bytes 1048592 | tf_op jit(solution)/shard_map/all_gather | solution.py:214
  287.9 2.8 copy.139
  297.1 3.8 multiply_add_fusion.3
  316.9 3.2 collective-permute-start.7
  320.1 83.2 %all-gather.21.cloned.1.call-done = f32[64,1,4096]{2,1,0:T(1,128)} async-done(((f32[1,1,4096]{2,1,0:T(1,128)}), f32[64,1,4096]{2,1,0:T(1,128)}) %all-gather.21.cloned.1.call-update) | async-done | bytes 1048592 | tf_op jit(solution)/shard_map/all_gather | solution.py:196
  403.3 2.8 copy.138
  406.1 3.1 reshape.1473
  424.7 88.6 %all-gather.23.cloned.1.call-done = f32[64,1,4096]{2,1,0:T(1,128)} async-done(((f32[1,1,4096]{2,1,0:T(1,128)}), f32[64,1,4096]{2,1,0:T(1,128)}) %all-gather.23.cloned.1.call-update) | async-done | bytes 1048592 | tf_op jit(solution)/shard_map/all_gather | solution.py:214
  513.3 2.8 copy.137
  516.1 3.1 dot_general.74
  519.2 2.9 fusion.8
  523.6 4.2 multiply_add_fusion.2
  537.6 2.9 collective-permute-done.9
  543.8 3.0 collective-permute-start.11
  546.9 83.3 %all-gather.25.cloned.1.call-done = f32[64,1,4096]{2,1,0:T(1,128)} async-done(((f32[1,1,4096]{2,1,0:T(1,128)}), f32[64,1,4096]{2,1,0:T(1,128)}) %all-gather.25.cloned.1.call-update) | async-done | bytes 1048592 | tf_op jit(solution)/shard_map/all_gather | solution.py:196
  630.2 2.8 copy.136
  633.0 3.1 reshape.1474
  651.6 88.6 %all-gather.27.cloned.1.call-done = f32[64,1,4096]{2,1,0:T(1,128)} async-done(((f32[1,1,4096]{2,1,0:T(1,128)}), f32[64,1,4096]{2,1,0:T(1,128)}) %all-gather.27.cloned.1.call-update) | async-done | bytes 1048592 | tf_op jit(solution)/shard_map/all_gather | solution.py:214
  740.2 2.8 copy.135
  743.0 3.1 dot_general.80
  746.1 2.9 fusion.4
  750.5 4.2 multiply_add_fusion.1
  766.3 2.9 collective-permute-done.13
  772.5 3.0 collective-permute-start.15
  775.6 83.3 %all-gather.29.cloned.1.call-done = f32[64,1,4096]{2,1,0:T(1,128)} async-done(((f32[1,1,4096]{2,1,0:T(1,128)}), f32[64,1,4096]{2,1,0:T(1,128)}) %all-gather.29.cloned.1.call-update) | async-done | bytes 1048592 | tf_op jit(solution)/shard_map/all_gather | solution.py:196
  861.7 3.1 reshape.1475
  880.8 88.7 %all-gather.31.cloned.1.call-done = f32[64,1,4096]{2,1,0:T(1,128)} async-done(((f32[1,1,4096]{2,1,0:T(1,128)}), f32[64,1,4096]{2,1,0:T(1,128)}) %all-gather.31.cloned.1.call-update) | async-done | bytes 1048592 | tf_op jit(solution)/shard_map/all_gather | solution.py:214
  977.7 3.9 multiply_add_fusion
  (253 shorter events, 147.4 us)
Async XLA Ops:
  7.2 173.6 %all-gather.17.cloned.1.call-start = ((), (), s32[]{:S(2)}) async-start(), calls=%async_computation | async-start | bytes 1064960 | tf_op jit(solution)/shard_map/all_gather | solution.py:196
  11.1 6.2 copy-start.17
  11.1 9.2 slice-start
  12.7 10.5 %collective-permute-start = (f32[4,512,1]{1,0,2:T(4,128)S(1)}, f32[4,512,1]{1,0,2:T(4,128)S(1)}, u32[]{:S(2)}, u32[]{:S(2)}) collective-permute-start(f32[4,512,1]{1,0,2:T(4,128)S(1)} %copy.23), channel_id=1, source_target_pairs={{0,1},{1,0},{2,3},{3,2},{4,5},{5,4},{6,7},{7,6},{8,9},{9,8},{10,11... | collective-permute-start | bytes 24584 | tf_op jit(solution)/shard_map/ppermute | solution.py:26
  15.9 6.3 copy-start.18
  15.9 6.3 copy-start.19
  16.2 7.4 collective-permute-start.1
  20.3 3.6 copy-start
  22.1 265.8 %all-gather.19.cloned.1.call-start = ((), (), s32[]{:S(2)}) async-start(), calls=%async_computation.1 | async-start | bytes 1064960 | tf_op jit(solution)/shard_map/all_gather | solution.py:214
  23.9 154.2 %copy-start.1 = (f32[4,512,1]{2,1,0:T(8,128)}, f32[4,512,1]{2,1,0:T(8,128)S(1)}, u32[]{:S(2)}) copy-start(f32[4,512,1]{2,1,0:T(8,128)S(1)} %copy.26) | copy-start | bytes 24580
  24.1 154.1 %collective-permute-start.2 = (f32[4,1,130]{2,1,0:T(1,128)S(1)}, f32[4,1,130]{2,1,0:T(1,128)S(1)}, u32[]{:S(2)}, u32[]{:S(2)}) collective-permute-start(f32[4,1,130]{2,1,0:T(1,128)S(1)} %get-tuple-element.155), channel_id=1, source_target_pairs={{0,2},{2,4},{4,6},{6,8},{8,10},{10,12},{12,14},{14,16},{16,18},{18... | collective-permute-start | bytes 6248 | tf_op jit(solution)/shard_map/ppermute | solution.py:26
  25.3 152.8 %collective-permute-start.3 = (f32[4,1,130]{2,1,0:T(1,128)S(1)}, f32[4,1,130]{2,1,0:T(1,128)S(1)}, u32[]{:S(2)}, u32[]{:S(2)}) collective-permute-start(f32[4,1,130]{2,1,0:T(1,128)S(1)} %get-tuple-element.154), channel_id=1, source_target_pairs={{2,0},{4,2},{6,4},{8,6},{10,8},{12,10},{14,12},{16,14},{18,16},{20... | collective-permute-start | bytes 6248 | tf_op jit(solution)/shard_map/ppermute | solution.py:29
  183.6 5.3 copy-start.16
  190.3 213.1 %all-gather.21.cloned.1.call-start = ((), (), s32[]{:S(2)}) async-start(), calls=%async_computation.2 | async-start | bytes 1064960 | tf_op jit(solution)/shard_map/all_gather | solution.py:196
  292.8 3.6 copy-start.3
  302.6 210.7 %all-gather.23.cloned.1.call-start = ((), (), s32[]{:S(2)}) async-start(), calls=%async_computation.3 | async-start | bytes 1064960 | tf_op jit(solution)/shard_map/all_gather | solution.py:214
  305.4 5.2 collective-permute-start.4
  308.4 5.2 collective-permute-start.5
  315.6 97.2 %collective-permute-start.6 = (f32[3,1,130]{2,1,0:T(1,128)S(1)}, f32[3,1,130]{2,1,0:T(1,128)S(1)}, u32[]{:S(2)}, u32[]{:S(2)}) collective-permute-start(f32[3,1,130]{2,1,0:T(1,128)S(1)} %get-tuple-element.178), channel_id=1, source_target_pairs={{2,0},{4,2},{6,4},{8,6},{10,8},{12,10},{14,12},{16,14},{18,16},{20... | collective-permute-start | bytes 4688 | tf_op jit(solution)/shard_map/ppermute | solution.py:29
  316.9 95.9 %collective-permute-start.7 = (f32[3,1,130]{2,1,0:T(1,128)S(1)}, f32[3,1,130]{2,1,0:T(1,128)S(1)}, u32[]{:S(2)}, u32[]{:S(2)}) collective-permute-start(f32[3,1,130]{2,1,0:T(1,128)S(1)} %get-tuple-element.179), channel_id=1, source_target_pairs={{0,2},{2,4},{4,6},{6,8},{8,10},{10,12},{12,14},{14,16},{16,18},{18... | collective-permute-start | bytes 4688 | tf_op jit(solution)/shard_map/ppermute | solution.py:26
  412.7 217.5 %all-gather.25.cloned.1.call-start = ((), (), s32[]{:S(2)}) async-start(), calls=%async_computation.4 | async-start | bytes 1064960 | tf_op jit(solution)/shard_map/all_gather | solution.py:196
  529.5 210.7 %all-gather.27.cloned.1.call-start = ((), (), s32[]{:S(2)}) async-start(), calls=%async_computation.5 | async-start | bytes 1064960 | tf_op jit(solution)/shard_map/all_gather | solution.py:214
  532.2 5.2 collective-permute-start.8
  535.1 5.4 collective-permute-start.9
  542.5 97.2 %collective-permute-start.10 = (f32[3,1,130]{2,1,0:T(1,128)S(1)}, f32[3,1,130]{2,1,0:T(1,128)S(1)}, u32[]{:S(2)}, u32[]{:S(2)}) collective-permute-start(f32[3,1,130]{2,1,0:T(1,128)S(1)} %get-tuple-element.174), channel_id=1, source_target_pairs={{2,0},{4,2},{6,4},{8,6},{10,8},{12,10},{14,12},{16,14},{18,16},{20... | collective-permute-start | bytes 4688 | tf_op jit(solution)/shard_map/ppermute | solution.py:29
  543.8 95.9 %collective-permute-start.11 = (f32[3,1,130]{2,1,0:T(1,128)S(1)}, f32[3,1,130]{2,1,0:T(1,128)S(1)}, u32[]{:S(2)}, u32[]{:S(2)}) collective-permute-start(f32[3,1,130]{2,1,0:T(1,128)S(1)} %get-tuple-element.175), channel_id=1, source_target_pairs={{0,2},{2,4},{4,6},{6,8},{8,10},{10,12},{12,14},{14,16},{16,18},{18... | collective-permute-start | bytes 4688 | tf_op jit(solution)/shard_map/ppermute | solution.py:26
  639.6 219.3 %all-gather.29.cloned.1.call-start = ((), (), s32[]{:S(2)}) async-start(), calls=%async_computation.6 | async-start | bytes 1064960 | tf_op jit(solution)/shard_map/all_gather | solution.py:196
  758.3 211.3 %all-gather.31.cloned.1.call-start = ((), (), s32[]{:S(2)}) async-start(), calls=%async_computation.7 | async-start | bytes 1064960 | tf_op jit(solution)/shard_map/all_gather | solution.py:214
  760.9 5.2 collective-permute-start.12
  763.8 5.4 collective-permute-start.13
  771.2 97.7 %collective-permute-start.14 = (f32[3,1,130]{2,1,0:T(1,128)S(1)}, f32[3,1,130]{2,1,0:T(1,128)S(1)}, u32[]{:S(2)}, u32[]{:S(2)}) collective-permute-start(f32[3,1,130]{2,1,0:T(1,128)S(1)} %get-tuple-element.170), channel_id=1, source_target_pairs={{2,0},{4,2},{6,4},{8,6},{10,8},{12,10},{14,12},{16,14},{18,16},{20... | collective-permute-start | bytes 4688 | tf_op jit(solution)/shard_map/ppermute | solution.py:29
  772.5 96.4 %collective-permute-start.15 = (f32[3,1,130]{2,1,0:T(1,128)S(1)}, f32[3,1,130]{2,1,0:T(1,128)S(1)}, u32[]{:S(2)}, u32[]{:S(2)}) collective-permute-start(f32[3,1,130]{2,1,0:T(1,128)S(1)} %get-tuple-element.171), channel_id=1, source_target_pairs={{0,2},{2,4},{4,6},{6,8},{8,10},{10,12},{12,14},{14,16},{16,18},{18... | collective-permute-start | bytes 4688 | tf_op jit(solution)/shard_map/ppermute | solution.py:26
  (14 other events, 32.8 us)
Sparse Core Ops, SparseCore 0:
  22.2 103.9 all-gather.16
  190.4 97.4 all-gather.18
  302.8 100.5 all-gather.20
  412.9 100.4 all-gather.22
  529.7 100.4 all-gather.24
  639.7 100.4 all-gather.26
  758.4 100.4 all-gather.28
  869.0 100.4 all-gather.30
where the time goes:
time: 997 us; the launch traced here: 989 us
  waiting for transfers between devices  612 us (61%)
  blocking collectives  147 us (15%)
  other arithmetic  88.5 us (9%)
  local copies, waits for them, and re-layouts  74.1 us (7%)
  starting transfers between devices  31.4 us (3%)
  matrix products  18.1 us (2%)
  between operations  17.5 us (2%)
    all_gather x4, waiting for transfers between devices, local(): lax.all_gather(own_force.reshape(rolls_dev, slot_cap * 2 * circ_dev), 'ar...  351 us
    all_gather x4, waiting for transfers between devices, local(): lax.all_gather(flat_rows, 'arc', axis=0, tiled=True)  250 us
    unnamed x1, blocking collectives  147 us
    another operation x33, other arithmetic, spring_pull(): jnp.stack([stretch * unit_dir[0], stretch * unit_dir[1], stretch * unit_d...  37.6 us
    unnamed x56, local copies, waits for them, and re-layouts  26.4 us
    ppermute x8, starting transfers between devices, padded(): lax.ppermute(lax.slice_in_dim(block, block.shape[dim] - width, None, axis...  21.8 us
  transfers between devices with their start and end apart: 24, of which 13 were waited for; matrix products, arithmetic and copies ran while one was open for 11% of the time, Pallas kernels for 0%

commit v1 on v0

v1 whole, which is shorter than its diff:
```python
import functools
import math

import jax
import jax.numpy as jnp
import numpy as np
from jax import lax
from jax.experimental import pallas as pl
from jax.experimental.pallas import tpu as pltpu
from jax.sharding import PartitionSpec as P

STEPS = 4
REACH = 20
TIME_STEP = 0.1
GRAVITY = 0.2
CONTACT_STIFF = 2.0
CRADLE_CURVE = 0.5
PAD_RATE = 0.2
PAD_STIFF = 1.0

LANES = 128
EDGE = 4
HALO = 48
WIN = 64
CHUNKS = 4
SIZES = (4, 4, 2, 2)


def arc_digits(index):
    return (index // 16, (index // 4) % 4, (index // 2) % 2, index % 2)


def arc_index(y, z, x, c):
    return (((y % 4) * 4 + z % 4) * 2 + x % 2) * 2 + c % 2


def pairs(shift):
    out = []
    for i in range(64):
        y, z, x, c = arc_digits(i)
        out.append((i, arc_index(y + shift[0], z + shift[1], x + shift[2], c + shift[3])))
    return out


def column_table(circ_total):
    step = 2.0 * math.pi / circ_total
    chord = 2.0 * math.sin(step / 2.0)
    length = math.sqrt(step * step + chord * chord)
    rows = []
    for half in range(2):
        cols = (half * LANES + np.arange(2 * LANES)) % circ_total
        phase = step * (cols + 0.5)
        before = step * (cols - 0.5)
        theta = step * cols
        parts = [
            chord / length * np.cos(phase),
            chord / length * np.sin(phase),
            chord / length * np.cos(before),
            chord / length * np.sin(before),
            np.sin(theta),
            np.cos(theta),
            np.zeros_like(theta),
            np.zeros_like(theta),
        ]
        rows.append(np.concatenate([p.reshape(2, LANES) for p in parts], axis=0))
    axial = step / length
    hoop_gain = 1.0 / (chord / length) ** 2
    return np.stack(rows).astype(np.float32), axial, hoop_gain


def prep_kernel(cycle_total, base_ref, disp, vel, mass, stiff, low, high, ext, pack):
    own = disp.shape[1]
    halo = low.shape[1]
    total = own + 2 * halo
    half = total // 2
    base = base_ref[0] - halo

    def put(row, count, raw):
        ids = base + row + lax.broadcasted_iota(jnp.int32, (count, LANES), 0)
        for a in range(3):
            ext[a, row : row + count, :] = raw(a)
        for a in range(3, 6):
            ext[a, row : row + count, :] = raw(a) * TIME_STEP
        m = raw(6)
        ext[6, row : row + count, :] = (TIME_STEP * TIME_STEP) / jnp.where(m > 0.0, m, 1.0)
        inside = (ids >= 0) & (ids < cycle_total - 1)
        ext[7, row : row + count, :] = jnp.where(inside, raw(7), 0.0)

    put(0, halo, lambda a: low[a])
    put(halo + own, halo, lambda a: high[a])
    for row in range(0, own, 64):
        span = slice(row, row + 64)

        def raw(a, span=span):
            if a < 3:
                return disp[a, span, :]
            if a < 6:
                return vel[a - 3, span, :]
            return mass[span, :] if a == 6 else stiff[span, :]

        put(halo + row, 64, raw)
    lane = lax.broadcasted_iota(jnp.int32, (8, LANES), 1) // (2 * EDGE)

    def body(b, carry):
        r = pl.multiple_of(b * 8, 8)
        packed = jnp.zeros((8, LANES), jnp.float32)
        for part in range(2):
            for a in range(8):
                value = ext[a, pl.ds(pl.multiple_of(r + part * half, 8), 8), :]
                moved = pltpu.roll(value, (8 * a + EDGE + 64 * part) % LANES, 1)
                packed = jnp.where(lane == a + 8 * part, moved, packed)
        pack[pl.ds(r, 8), :] = packed
        return carry

    lax.fori_loop(0, half // 8, body, 0)


def ring_left(tiles, last):
    a, b = (pltpu.roll(t, LANES - 1, 1) for t in tiles)
    return jnp.where(last, b, a), jnp.where(last, a, b)


def ring_right(tiles, first):
    a, b = (pltpu.roll(t, 1, 1) for t in tiles)
    return jnp.where(first, b, a), jnp.where(first, a, b)


def unpack_block(pack, row, half, a, keep):
    upper = row >= half
    at = pl.multiple_of(jnp.where(upper, row - half, row), 8)
    shift = jnp.where(upper, (2 * LANES - 8 * a - EDGE - 64) % LANES, (2 * LANES - 8 * a - EDGE) % LANES)
    return jnp.where(keep, pltpu.roll(pack[pl.ds(at, 8), :], shift, 1), 0.0)


def load_state(source, pack, first_row, rows, half, state, vels, coef):
    lane = lax.broadcasted_iota(jnp.int32, (8, LANES), 1)
    sub = lax.broadcasted_iota(jnp.int32, (8, LANES), 0)
    keep = (lane < EDGE) | (lane >= LANES - EDGE)
    first = lane == 0
    top = sub == 0

    def body(b, carry):
        r = pl.multiple_of(b * 8, 8)
        e = first_row + r
        span = pl.ds(r, 8)
        for a in range(3):
            state[0, a, 0, span, :] = source(a, r)
            state[0, a, 1, span, :] = unpack_block(pack, e, half, a, keep)
            vels[a, 0, span, :] = source(3 + a, r)
            vels[a, 1, span, :] = unpack_block(pack, e, half, 3 + a, keep)
        coef[0, 0, span, :] = source(6, r)
        coef[0, 1, span, :] = unpack_block(pack, e, half, 6, keep)
        k = (source(7, r), unpack_block(pack, e, half, 7, keep))
        kr = ring_right(k, first)
        new = []
        for t in range(2):
            down = pltpu.roll(k[t], 1, 0)
            coef[1, t, span, :] = k[t]
            coef[2, t, span, :] = 0.5 * (k[t] + kr[t])
            coef[3, t, span, :] = (0.5 * HOOP_GAIN) * (k[t] + jnp.where(top, carry[t], down))
            new.append(down)
        return tuple(new)

    zero = jnp.zeros((8, LANES), jnp.float32)
    lax.fori_loop(0, rows // 8, body, (zero, zero))
    for buf in range(2):
        for a in range(3):
            for t in range(2):
                state[buf, a, t, rows : rows + 8, :] = zero


TABLE, AXIAL, HOOP_GAIN = column_table(2 * LANES)


def advance(table, rows, step, state, vels, coef, push=None):
    now, later = step % 2, (step + 1) % 2
    lane = lax.broadcasted_iota(jnp.int32, (8, LANES), 1)
    top = lax.broadcasted_iota(jnp.int32, (8, LANES), 0) == 0
    first, last = lane == 0, lane == LANES - 1

    def const(i):
        return [jnp.broadcast_to(table[2 * i + t : 2 * i + t + 1, :], (8, LANES)) for t in range(2)]

    cj, sj, cb, sb = (const(i) for i in range(4))
    two = range(2)

    def body(b, carry):
        r = pl.multiple_of(b * 8, 8)
        span, below = pl.ds(r, 8), pl.ds(r + 1, 8)
        x, y, z = ([state[now, a, t, span, :] for t in two] for a in range(3))
        xn, yn, zn = ([state[now, a, t, below, :] for t in two] for a in range(3))
        p = [cj[t] * y[t] + sj[t] * z[t] for t in two]
        q = [cb[t] * y[t] + sb[t] * z[t] for t in two]
        ax = [AXIAL * x[t] for t in two]
        pn = [cj[t] * yn[t] + sj[t] * zn[t] for t in two]
        qn = [cb[t] * yn[t] + sb[t] * zn[t] for t in two]
        axn = [AXIAL * xn[t] for t in two]
        q_next = ring_left(q, last)
        anti_next = ring_left([q[t] - ax[t] for t in two], last)
        diag_next = ring_left([qn[t] + axn[t] for t in two], last)
        k = [coef[1, t, span, :] for t in two]
        t_d = [k[t] * (diag_next[t] - (p[t] + ax[t])) for t in two]
        t_a = [k[t] * (anti_next[t] - (pn[t] - axn[t])) for t in two]
        t_h = [coef[3, t, span, :] * (q_next[t] - p[t]) for t in two]
        fx = [coef[2, t, span, :] * (xn[t] - x[t]) for t in two]
        d_left = ring_right(t_d, first)
        a_left = ring_right(t_a, first)
        g_left = ring_right([t_a[t] + t_h[t] for t in two], first)
        new = []
        for t in two:
            up = t_d[t] + t_h[t]
            force = [
                fx[t] + AXIAL * (t_d[t] + a_left[t]),
                cj[t] * up - cb[t] * g_left[t],
                sj[t] * up - sb[t] * g_left[t],
            ]
            low = [
                fx[t] + AXIAL * (d_left[t] + t_a[t]),
                cb[t] * d_left[t] - cj[t] * t_a[t],
                sb[t] * d_left[t] - sj[t] * t_a[t],
            ]
            at = (x[t], y[t], z[t])
            inverse = coef[0, t, span, :]
            for a in range(3):
                moved = pltpu.roll(low[a], 1, 0)
                total = force[a] - jnp.where(top, carry[3 * t + a], moved)
                new.append(moved)
                if push is not None and a > 0:
                    total = total + push[a - 1, t, span, :]
                w = vels[a, t, span, :] + inverse * total
                if a == 2:
                    w = w - (GRAVITY * TIME_STEP * TIME_STEP)
                vels[a, t, span, :] = w
                state[later, a, t, span, :] = at[a] + w
        return tuple(new)

    zero = jnp.zeros((8, LANES), jnp.float32)
    lax.fori_loop(0, rows // 8, body, (zero,) * 6)


def window_kernel(
    half, where_ref, list_ref, lift_ref, table, ext, pack, pads, result, pad_out,
    raw, state, vels, coef, push, taken, given, held, sem,
):
    start = pl.multiple_of(where_ref[0], 8)
    copy = pltpu.make_async_copy(ext.at[:, pl.ds(start, WIN), :], raw, sem)
    copy.start()
    copy.wait()
    load_state(lambda a, r: raw[a, pl.ds(r, 8), :], pack, start, WIN, half, state, vels, coef)
    held[...] = pads[...]
    slots = pads.shape[1]
    lift = lift_ref[0]
    for step in range(STEPS):
        now = step % 2
        push[...] = jnp.zeros_like(push)
        for m in range(slots):
            g = list_ref[step, m]
            for a in range(2):
                for t in range(2):
                    taken[a, t, m : m + 1, :] = state[now, a + 1, t, pl.ds(g, 1), :]
        for t in range(2):
            sin_angle, cos_angle = table[8 + t : 9 + t, :], table[10 + t : 11 + t, :]
            lateral = sin_angle + taken[0, t]
            q = held[t]
            intrusion = lift + CRADLE_CURVE * lateral * lateral - (1.0 - cos_angle) - taken[1, t] - q
            load = CONTACT_STIFF * jnp.maximum(intrusion, 0.0)
            normal = load / jnp.sqrt(1.0 + 4.0 * CRADLE_CURVE * CRADLE_CURVE * lateral * lateral)
            given[0, t] = -2.0 * CRADLE_CURVE * lateral * normal
            given[1, t] = normal
            held[t] = q + PAD_RATE * (load - PAD_STIFF * q)
        for m in range(slots):
            g = list_ref[step, m]
            for a in range(2):
                for t in range(2):
                    push[a, t, pl.ds(g, 1), :] += given[a, t, m : m + 1, :]
        advance(table, WIN, step, state, vels, coef, push)
    for a in range(3):
        result[a] = state[STEPS % 2, a, 0, :WIN, :]
        result[3 + a] = vels[a, 0] * (1.0 / TIME_STEP)
    pad_out[0] = held[0]


def bulk_kernel(half, rows, where_ref, table, ext, pack, window, disp_out, vel_out, state, vels, coef):
    chunk = pl.program_id(0)
    count = rows - 16
    first_row = HALO - 8 + chunk * count

    def source(a, r):
        return ext[a, pl.ds(pl.multiple_of(first_row + r, 8), 8), :]

    load_state(source, pack, first_row, rows, half, state, vels, coef)
    for step in range(STEPS):
        advance(table, rows, step, state, vels, coef)
    start = where_ref[1]
    sub = lax.broadcasted_iota(jnp.int32, (8, LANES), 0)

    def body(b, carry):
        r = pl.multiple_of(b * 8, 8)
        inner = pl.ds(pl.multiple_of(r + 8, 8), 8)
        rel = first_row + 8 + r - start
        at = pl.ds(pl.multiple_of(jnp.clip(rel, 0, WIN - 8), 8), 8)
        ids = rel + sub
        use = (ids >= STEPS) & (ids < WIN - STEPS)
        for a in range(3):
            disp_out[a, pl.ds(r, 8), :] = jnp.where(use, window[a, at, :], state[STEPS % 2, a, 0, inner, :])
            vel_out[a, pl.ds(r, 8), :] = jnp.where(
                use, window[3 + a, at, :], vels[a, 0, inner, :] * (1.0 / TIME_STEP)
            )
        return carry

    lax.fori_loop(0, count // 8, body, 0)


def pick(held, index):
    count = held.shape[0]
    out = []
    for i in range(index.shape[0]):
        value = held[0]
        for n in range(1, count):
            value = jnp.where(index[i] == n, held[n], value)
        out.append(value)
    return jnp.stack(out)


def route(value, needs, me, both):
    my_y, my_x, my_c = me // 16, (me // 2) % 2, me % 2
    got = [value]
    for k in range(1, 4):
        got.append(lax.ppermute(value, "arc", pairs((k, 0, 0, 0))))
    held = jnp.stack(got)
    other = lax.ppermute(held, "arc", pairs((0, 0, 0, 1)))
    held = jnp.concatenate([held, other])
    need_y, need_z, need_x, need_c = arc_digits(needs)
    index = (need_c ^ my_c) * 4 + (my_y - need_y) % 4
    chosen = pick(held, index)
    parts = [chosen[0:2]]
    for k in range(1, 4):
        parts.append(lax.ppermute(chosen[2 * k : 2 * k + 2], "arc", pairs((0, k, 0, 0))))
    back = ((me // 4) % 4 - need_z[0:2]) % 4
    mine = []
    for xr in range(2):
        best = parts[0][xr]
        for k in range(1, 4):
            best = jnp.where(back[xr] == k, parts[k][xr], best)
        mine.append(best)
    same = need_x[0] == my_x
    across = pairs((0, 0, 1, 0))
    near = lax.ppermute(mine[1], "arc", across)
    result = jnp.where(same, mine[0], near)
    if not both:
        return result
    swap = [(0, 1), (1, 0)]
    double = [(2 * s + h, 2 * d + 1 - h) for s, d in across for h in range(2)]
    far = lax.ppermute(mine[0], "circ", swap)
    cross = lax.ppermute(mine[1], ("arc", "circ"), double)
    return jnp.stack([result, jnp.where(same, far, cross)])


def static_tables(arc_count, cycle_dev, roller_total):
    cycle_total = arc_count * cycle_dev
    centres = [r * (cycle_total - 1) // (roller_total - 1) for r in range(roller_total)]
    span = REACH + STEPS - 1
    near = np.full(arc_count, -1, np.int32)
    start = np.zeros(arc_count, np.int32)
    for d in range(arc_count):
        base = d * cycle_dev
        touching = [r for r, c in enumerate(centres) if base - span <= c < base + cycle_dev + span]
        assert len(touching) <= 1
        if touching:
            near[d] = touching[0]
            offset = centres[touching[0]] - base - REACH - STEPS - STEPS + 1 + HALO
            start[d] = offset // 8 * 8
            assert 0 <= start[d] <= cycle_dev + 2 * HALO - WIN
    home = np.array([c // cycle_dev for c in centres], np.int32)
    dests = np.zeros((arc_count, 8), np.int32)
    for d in range(arc_count):
        y, z, x, c = arc_digits(d)
        for k in range(4):
            for xr in range(2):
                dests[d, 2 * k + xr] = arc_index(y, z + k, x + xr, c)
    return near, start, home, dests


def local(displacement, velocity, node_mass, wall_stiff, pad_state, roller_lift, contact_rows, roller_slot):
    cycle_dev = displacement.shape[1]
    slots = pad_state.shape[1]
    roller_total = roller_lift.shape[0]
    arc_count = lax.axis_size("arc")
    cycle_total = cycle_dev * arc_count
    total = cycle_dev + 2 * HALO
    half = total // 2
    near, start, home, dests = static_tables(arc_count, cycle_dev, roller_total)
    me = lax.axis_index("arc")
    vmem = pl.BlockSpec(memory_space=pltpu.VMEM)
    smem = pl.BlockSpec(memory_space=pltpu.SMEM)
    params = pltpu.CompilerParams(vmem_limit_bytes=40 * 1024 * 1024)

    roller_ids = jnp.arange(roller_total, dtype=jnp.int32)
    dest_row = jnp.asarray(np.concatenate([dests, near[dests], near[:, None], start[:, None]], axis=1))[me]
    dest_ids, dest_rolls, roll, begin = dest_row[:8], dest_row[8:16], dest_row[16], dest_row[17]
    needs_in = jnp.sum(
        jnp.where(dest_rolls[:, None] == roller_ids[None, :], roller_slot[None, :], 0), axis=1
    )
    matches = roller_slot[None, :] == dest_ids[:, None]
    needs_out = jnp.sum(jnp.where(matches, jnp.asarray(home)[None, :], 0), axis=1)
    used = jnp.any(matches[0])

    def edge(at):
        return jnp.concatenate(
            [displacement[:, at], velocity[:, at], node_mass[None, at], wall_stiff[None, at]], axis=0
        )

    up = [(i, i + 1) for i in range(arc_count - 1)]
    low = lax.ppermute(edge(slice(cycle_dev - HALO, cycle_dev)), "arc", up)
    high = lax.ppermute(edge(slice(0, HALO)), "arc", [(b, a) for a, b in up])

    pads = route(pad_state[0], needs_in, me, True)

    base = jnp.reshape(me * cycle_dev, (1,)).astype(jnp.int32)

    ext, pack = pl.pallas_call(
        functools.partial(prep_kernel, cycle_total),
        out_shape=(
            jax.ShapeDtypeStruct((8, total, LANES), jnp.float32),
            jax.ShapeDtypeStruct((half, LANES), jnp.float32),
        ),
        in_specs=[smem] + [vmem] * 6,
        out_specs=(vmem, vmem),
        compiler_params=params,
        name="prep",
    )(base, displacement, velocity, node_mass, wall_stiff, low, high)
    pack = lax.ppermute(pack, "circ", [(0, 1), (1, 0)])

    safe_roll = jnp.maximum(roll, 0)
    cycles = lax.dynamic_slice(contact_rows, (0, safe_roll, 0), (STEPS, 1, slots))[:, 0]
    rows_in = jnp.clip(cycles - (me * cycle_dev - HALO + begin), 0, WIN - 1)
    lift = jnp.where(roll >= 0, lax.dynamic_slice(roller_lift, (safe_roll,), (1,)), -1e9)
    where = jnp.stack([begin, jnp.where(roll >= 0, begin, -4 * WIN)])
    table = jnp.asarray(TABLE)[lax.axis_index("circ")]

    def scratch(rows):
        return [
            pltpu.VMEM((2, 3, 2, rows + 8, LANES), jnp.float32),
            pltpu.VMEM((3, 2, rows, LANES), jnp.float32),
            pltpu.VMEM((4, 2, rows, LANES), jnp.float32),
        ]

    window, pad_new = pl.pallas_call(
        functools.partial(window_kernel, half),
        out_shape=(
            jax.ShapeDtypeStruct((6, WIN, LANES), jnp.float32),
            jax.ShapeDtypeStruct((1, slots, LANES), jnp.float32),
        ),
        in_specs=[smem, smem, smem, vmem, pl.BlockSpec(memory_space=pl.ANY), vmem, vmem],
        out_specs=(vmem, vmem),
        scratch_shapes=[pltpu.VMEM((8, WIN, LANES), jnp.float32)]
        + scratch(WIN)
        + [
            pltpu.VMEM((2, 2, WIN, LANES), jnp.float32),
            pltpu.VMEM((2, 2, slots, LANES), jnp.float32),
            pltpu.VMEM((2, 2, slots, LANES), jnp.float32),
            pltpu.VMEM((2, slots, LANES), jnp.float32),
            pltpu.SemaphoreType.DMA,
        ],
        compiler_params=params,
        name="window",
    )(where, rows_in, lift, table, ext, pack, pads)

    rows = cycle_dev // CHUNKS + 16
    disp_out, vel_out = pl.pallas_call(
        functools.partial(bulk_kernel, half, rows),
        grid=(CHUNKS,),
        out_shape=(
            jax.ShapeDtypeStruct(displacement.shape, jnp.float32),
            jax.ShapeDtypeStruct(displacement.shape, jnp.float32),
        ),
        in_specs=[smem, vmem, vmem, vmem, vmem],
        out_specs=(
            pl.BlockSpec((3, rows - 16, LANES), lambda i: (0, i, 0)),
            pl.BlockSpec((3, rows - 16, LANES), lambda i: (0, i, 0)),
        ),
        scratch_shapes=scratch(rows),
        compiler_params=params,
        cost_estimate=pl.CostEstimate(flops=30_000_000, bytes_accessed=8_000_000, transcendentals=0),
        name="bulk",
    )(where, table, ext, pack, window)

    returned = route(pad_new[0], needs_out, me, False)
    pad_result = jnp.where(used, returned, pad_state[0])[None]
    return disp_out, vel_out, pad_result


def solution(mesh):
    placed = (
        P(None, "arc", "circ"),
        P(None, "arc", "circ"),
        P("arc", "circ"),
        P("arc", "circ"),
        P("arc", None, "circ"),
        P(),
        P(),
        P(),
    )
    return jax.shard_map(
        local,
        mesh=mesh,
        in_specs=placed,
        out_specs=(P(None, "arc", "circ"), P(None, "arc", "circ"), P("arc", None, "circ")),
        check_vma=False,
    )
```

time: 997 us -> 219 us (0.22)
  waiting for transfers between devices: 612 us -> 6.42 us
  blocking collectives: 147 us -> 0 us
  other arithmetic: 88.5 us -> 11.8 us
  Pallas kernels: 0 us -> 68.4 us
  between operations: 17.5 us -> 82.6 us
  local copies, waits for them, and re-layouts: 74.1 us -> 12.3 us
  matrix products: 18.1 us -> 0 us
    all_gather x8 -> x0, waiting for transfers between devices: 601 us -> none  [the longest x4 351 us: local(): lax.all_gather(own_force.reshape(rolls_dev, slot_cap * 2 * circ_dev), 'ar...]
    unnamed x1 -> x0, blocking collectives: 147 us -> none
    pallas_call x0 -> x3, Pallas kernels: none -> 68.4 us  [the longest x1 57.6 us: local(): pl.pallas_call(functools.partial(bulk_kernel, half, rows), grid=(CHUNKS,)...]
    another operation x44 -> x24, other arithmetic: 39.7 us -> 7.08 us  [the longest x18 4.33 us: pick(): return jnp.stack(out)]
    unnamed x56 -> x36, local copies, waits for them, and re-layouts: 26.4 us -> 5.34 us
    dot_general x8 -> x0, matrix products: 18.1 us -> none  [match_fold(): return jnp.dot(match, pieces[0], precision=lax.Precision.HIGHEST)]
    add x4 -> x0, other arithmetic: 16.1 us -> none  [local(): displacement = displacement + time_step * velocity]
    concatenate x6 -> x2, other arithmetic: 14.3 us -> 0.04 us  [edge(): jnp.concatenate([displacement[:, at], velocity[:, at], node_mass[None, at...]
  transfers between devices with their start and end apart: 24 -> 21, of which waited for: 13 -> 4; matrix products, arithmetic and copies ran while one was open for 11% -> 8% of each run, Pallas kernels for 0% -> 28%
where the time goes in v1:
time: 219 us; the launch traced here: 216 us
  between operations  82.6 us (38%)
  Pallas kernels  68.4 us (31%)
  starting transfers between devices  34.8 us (16%)
  local copies, waits for them, and re-layouts  12.3 us (6%)
  other arithmetic  11.8 us (5%)
  waiting for transfers between devices  6.42 us (3%)
    pallas_call x1, Pallas kernels, local(): pl.pallas_call(functools.partial(bulk_kernel, half, rows), grid=(CHUNKS,)...  57.6 us
    ppermute x6, starting transfers between devices, route(): lax.ppermute(chosen[2 * k:2 * k + 2], 'arc', pairs((0, k, 0, 0)))  10.6 us
    ppermute x6, starting transfers between devices, route(): got.append(lax.ppermute(value, 'arc', pairs((k, 0, 0, 0))))  9.37 us
    pallas_call x1, Pallas kernels, local(): pl.pallas_call(functools.partial(window_kernel, half), out_shape=(jax.Sha...  7.37 us
    unnamed x36, local copies, waits for them, and re-layouts  5.34 us
    ppermute x2, starting transfers between devices, route(): near = lax.ppermute(mine[1], 'arc', across)  4.41 us
  transfers between devices with their start and end apart: 21, of which 4 were waited for; matrix products, arithmetic and copies ran while one was open for 8% of the time, Pallas kernels for 28%

profile of v1, /device:TPU:0, one launch (start us, length us, event | category | flops | bytes accessed | tf_op | source)
XLA Modules:
  0.0 216.3 jit_solution(7487367349989629805)
XLA Ops:
  0.7 1.7 collective-permute-start.3
  2.4 2.9 %collective-permute-start.4 = (f32[16,128]{1,0:T(8,128)}, f32[16,128]{1,0:T(8,128)S(1)}, u32[]{:S(2)}, u32[]{:S(2)}) collective-permute-start(f32[16,128]{1,0:T(8,128)} %bitcast.430), channel_id=1, source_target_pairs={{0,64},{2,66},{4,68},{6,70},{8,72},{10,74},{12,76},{14,78},{16,80}... | collective-permute-start | bytes 24584 | tf_op jit(solution)/shard_map/ppermute | solution.py:329
  5.3 1.3 collective-permute-start.5
  6.7 1.0 fusion.30
  7.7 0.8 slice_bitcast_fusion
  8.5 1.3 collective-permute-start.1
  9.8 3.0 %collective-permute-start = (f32[8,48,128]{2,1,0:T(8,128)S(1)}, f32[8,48,128]{2,1,0:T(8,128)S(1)}, u32[]{:S(2)}, u32[]{:S(2)}) collective-permute-start(f32[8,48,128]{2,1,0:T(8,128)S(1)} %pad_maximum_fusion), channel_id=1, source_target_pairs={{0,2},{2,4},{4,6},{6,8},{8,10},{10,12},{12,14},{14,16},{16,18},{18... | collective-permute-start | bytes 589832 | tf_op jit(solution)/shard_map/ppermute | solution.py:414
  13.7 0.9 select_reduce_fusion
  17.1 1.1 collective-permute-start.6
  46.5 4.1 %collective-permute-start.7 = (f32[2,16,128]{2,1,0:T(8,128)S(1)}, f32[2,16,128]{2,1,0:T(8,128)S(1)}, u32[]{:S(2)}, u32[]{:S(2)}) collective-permute-start(f32[2,16,128]{2,1,0:T(8,128)S(1)} %pad_maximum_fusion.4), channel_id=1, source_target_pairs={{0,24},{2,26},{4,28},{6,30},{8,0},{10,2},{12,4},{14,6},{16,8},{18,... | collective-permute-start | bytes 49160 | tf_op jit(solution)/shard_map/ppermute | solution.py:338
  52.1 0.7 select_bitcast_fusion.8
  53.5 1.3 collective-permute-start.9
  62.6 3.2 %collective-permute-start.10 = (f32[16,128]{1,0:T(8,128)}, f32[16,128]{1,0:T(8,128)S(1)}, u32[]{:S(2)}, u32[]{:S(2)}) collective-permute-start(f32[16,128]{1,0:T(8,128)} %fusion.11), channel_id=1, source_target_pairs={{0,4},{2,6},{4,0},{6,2},{8,12},{10,14},{12,8},{14,10},{16,20},{18,... | collective-permute-start | bytes 24584 | tf_op jit(solution)/shard_map/ppermute | solution.py:348
  74.0 1.4 collective-permute-start.12
  76.0 1.5 collective-permute-start.11
  77.5 0.7 pad_add_fusion.where_ref
  82.4 1.1 copy-done.1
  83.5 0.9 copy-done.3
  84.4 0.9 copy-done.5
  85.4 0.9 copy-done.7
  86.3 3.5 %prep.1 = (f32[8,608,128]{2,1,0:T(8,128)S(1)}, f32[304,128]{1,0:T(8,128)S(1)}) custom-call(s32[1]{0:T(128)} %bitcast.5.base_ref, f32[3,512,128]{2,1,0:T(8,128)S(1)} %copy-done, f32[3,512,128]{2,1,0:T(8,128)S(1)} %copy-done.1, f32[512,128]{1,0:T(8,128)S(1)} %copy-done.2, f32[512,128]{1,0:T(8,128)S(1)} %copy-done.3, f32[8,48,128]{2,1,0:T(8,128)S(1)} %copy-done.7, ...), custom_call_target="tpu_custom_call" | custom-call | tf_op jit(solution)/shard_map/prep/pallas_call | solution.py:421
  89.8 2.1 collective-permute-start.2
  92.7 4.0 %collective-permute-done.2.pack = f32[304,128]{1,0:T(8,128)S(1)} collective-permute-done((f32[304,128]{1,0:T(8,128)S(1)}, f32[304,128]{1,0:T(8,128)S(1)}, u32[]{:S(2)}, u32[]{:S(2)}) %collective-permute-start.2) | collective-permute-done | bytes 155680 | tf_op jit(solution)/shard_map/ppermute | solution.py:432
  96.6 7.4 %window.1 = (f32[6,64,128]{2,1,0:T(8,128)S(1)}, f32[1,16,128]{2,1,0:T(8,128)S(1)}) custom-call(s32[2]{0:T(128)S(1)} %pad_add_fusion.where_ref, s32[4,16]{1,0:T(4,128)S(1)} %clamp_reduce_fusion.list_ref, f32[1]{0:T(128)S(6)} %select_n.897.lift_ref, f32[16,128]{1,0:T(8,128)S(1)} %dynamic-slice_bitcast_fusion.table, f32[8,608,128]{2,1,0:T(8,128)S(1)} %get-tuple-element.9.ext, ...), custom_call_target="tpu_custom_call" | custom-call | tf_op jit(solution)/shard_map/window/pallas_call | solution.py:448
  104.6 2.8 %collective-permute-start.15 = (f32[16,128]{1,0:T(8,128)S(1)}, f32[16,128]{1,0:T(8,128)S(1)}, u32[]{:S(2)}, u32[]{:S(2)}) collective-permute-start(f32[16,128]{1,0:T(8,128)S(1)} %bitcast.428), channel_id=1, source_target_pairs={{0,96},{2,98},{4,100},{6,102},{8,104},{10,106},{12,108},{14,110},{... | collective-permute-start | bytes 24584 | tf_op jit(solution)/shard_map/ppermute | solution.py:329
  107.5 1.5 collective-permute-done.13
  108.9 0.9 collective-permute-done.14
  137.0 2.6 %collective-permute-start.17 = (f32[2,16,128]{2,1,0:T(8,128)S(1)}, f32[2,16,128]{2,1,0:T(8,128)S(1)}, u32[]{:S(2)}, u32[]{:S(2)}) collective-permute-start(f32[2,16,128]{2,1,0:T(8,128)S(1)} %pad_maximum_fusion.8), channel_id=1, source_target_pairs={{0,24},{2,26},{4,28},{6,30},{8,0},{10,2},{12,4},{14,6},{16,8},{18,... | collective-permute-start | bytes 49160 | tf_op jit(solution)/shard_map/ppermute | solution.py:338
  139.7 2.4 %collective-permute-start.18 = (f32[2,16,128]{2,1,0:T(8,128)S(1)}, f32[2,16,128]{2,1,0:T(8,128)S(1)}, u32[]{:S(2)}, u32[]{:S(2)}) collective-permute-start(f32[2,16,128]{2,1,0:T(8,128)S(1)} %pad_maximum_fusion.9), channel_id=1, source_target_pairs={{0,16},{2,18},{4,20},{6,22},{8,24},{10,26},{12,28},{14,30},{16,0},... | collective-permute-start | bytes 49160 | tf_op jit(solution)/shard_map/ppermute | solution.py:338
  149.3 1.2 collective-permute-start.20
  157.6 57.6 %bulk.1 = (f32[3,512,128]{2,1,0:T(8,128)}, f32[3,512,128]{2,1,0:T(8,128)}) custom-call(s32[2]{0:T(128)S(1)} %pad_add_fusion.where_ref, f32[16,128]{1,0:T(8,128)S(1)} %dynamic-slice_bitcast_fusion.table, f32[8,608,128]{2,1,0:T(8,128)S(1)} %get-tuple-element.9.ext, f32[304,128]{1,0:T(8,128)S(1)} %collective-permute-done.2.pack, ...), custom_call_target="tpu_custom_call" | custom-call | flops 30000000 | bytes 8000000 | tf_op jit(solution)/shard_map/bulk/pallas_call | solution.py:470
  215.2 1.2 fusion.8
  (96 shorter events, 15.8 us)
Async XLA Ops:
  0.6 61.3 %copy-start.8 = (f32[1,16,128]{2,1,0:T(8,128)S(1)}, f32[1,16,128]{2,1,0:T(8,128)}, u32[]{:S(2)}) copy-start(f32[1,16,128]{2,1,0:T(8,128)} %param.15) | copy-start | bytes 24580
  0.6 81.7 %copy-start = (f32[3,512,128]{2,1,0:T(8,128)S(1)}, f32[3,512,128]{2,1,0:T(8,128)}, u32[]{:S(2)}) copy-start(f32[3,512,128]{2,1,0:T(8,128)} %disp.1) | copy-start | bytes 2359300
  0.7 81.7 %copy-start.2 = (f32[512,128]{1,0:T(8,128)S(1)}, f32[512,128]{1,0:T(8,128)}, u32[]{:S(2)}) copy-start(f32[512,128]{1,0:T(8,128)} %mass.1) | copy-start | bytes 786436
  0.7 78.8 %copy-start.17 = (f32[40]{0:T(128)S(1)}, f32[40]{0:T(128)}, u32[]{:S(2)}) copy-start(f32[40]{0:T(128)} %param.16) | copy-start | bytes 484
  0.7 80.1 %copy-start.10 = (s32[4,40,16]{1,2,0:T(8,128)S(1)}, s32[4,40,16]{1,2,0:T(8,128)}, u32[]{:S(2)}) copy-start(s32[4,40,16]{1,2,0:T(8,128)} %param.17) | copy-start | bytes 30724
  0.7 15.7 %collective-permute-start.3 = (f32[16,128]{1,0:T(8,128)}, f32[16,128]{1,0:T(8,128)S(1)}, u32[]{:S(2)}, u32[]{:S(2)}) collective-permute-start(f32[16,128]{1,0:T(8,128)} %bitcast.429), channel_id=1, source_target_pairs={{0,32},{2,34},{4,36},{6,38},{8,40},{10,42},{12,44},{14,46},{16,48}... | collective-permute-start | bytes 24584 | tf_op jit(solution)/shard_map/ppermute | solution.py:329
  2.4 14.0 %collective-permute-start.4 = (f32[16,128]{1,0:T(8,128)}, f32[16,128]{1,0:T(8,128)S(1)}, u32[]{:S(2)}, u32[]{:S(2)}) collective-permute-start(f32[16,128]{1,0:T(8,128)} %bitcast.430), channel_id=1, source_target_pairs={{0,64},{2,66},{4,68},{6,70},{8,72},{10,74},{12,76},{14,78},{16,80}... | collective-permute-start | bytes 24584 | tf_op jit(solution)/shard_map/ppermute | solution.py:329
  5.3 11.1 %collective-permute-start.5 = (f32[16,128]{1,0:T(8,128)}, f32[16,128]{1,0:T(8,128)S(1)}, u32[]{:S(2)}, u32[]{:S(2)}) collective-permute-start(f32[16,128]{1,0:T(8,128)} %bitcast.431), channel_id=1, source_target_pairs={{0,96},{2,98},{4,100},{6,102},{8,104},{10,106},{12,108},{14,110},{... | collective-permute-start | bytes 24584 | tf_op jit(solution)/shard_map/ppermute | solution.py:329
  8.5 72.5 %collective-permute-start.1 = (f32[8,48,128]{2,1,0:T(8,128)S(1)}, f32[8,48,128]{2,1,0:T(8,128)S(1)}, u32[]{:S(2)}, u32[]{:S(2)}) collective-permute-start(f32[8,48,128]{2,1,0:T(8,128)S(1)} %pad_maximum_fusion.1), channel_id=1, source_target_pairs={{2,0},{4,2},{6,4},{8,6},{10,8},{12,10},{14,12},{16,14},{18,16},{20... | collective-permute-start | bytes 589832 | tf_op jit(solution)/shard_map/ppermute | solution.py:415
  9.8 71.8 %collective-permute-start = (f32[8,48,128]{2,1,0:T(8,128)S(1)}, f32[8,48,128]{2,1,0:T(8,128)S(1)}, u32[]{:S(2)}, u32[]{:S(2)}) collective-permute-start(f32[8,48,128]{2,1,0:T(8,128)S(1)} %pad_maximum_fusion), channel_id=1, source_target_pairs={{0,2},{2,4},{4,6},{6,8},{8,10},{10,12},{12,14},{14,16},{16,18},{18... | collective-permute-start | bytes 589832 | tf_op jit(solution)/shard_map/ppermute | solution.py:414
  17.1 28.0 %collective-permute-start.6 = (f32[4,16,128]{2,1,0:T(8,128)S(1)}, f32[4,16,128]{2,1,0:T(8,128)S(1)}, u32[]{:S(2)}, u32[]{:S(2)}) collective-permute-start(f32[4,16,128]{2,1,0:T(8,128)S(1)} %pad_maximum_fusion.2), channel_id=1, source_target_pairs={{0,2},{2,0},{4,6},{6,4},{8,10},{10,8},{12,14},{14,12},{16,18},{18,... | collective-permute-start | bytes 98312 | tf_op jit(solution)/shard_map/ppermute | solution.py:331
  46.5 15.4 %collective-permute-start.7 = (f32[2,16,128]{2,1,0:T(8,128)S(1)}, f32[2,16,128]{2,1,0:T(8,128)S(1)}, u32[]{:S(2)}, u32[]{:S(2)}) collective-permute-start(f32[2,16,128]{2,1,0:T(8,128)S(1)} %pad_maximum_fusion.4), channel_id=1, source_target_pairs={{0,24},{2,26},{4,28},{6,30},{8,0},{10,2},{12,4},{14,6},{16,8},{18,... | collective-permute-start | bytes 49160 | tf_op jit(solution)/shard_map/ppermute | solution.py:338
  52.0 9.9 %collective-permute-start.8 = (f32[2,16,128]{2,1,0:T(8,128)S(1)}, f32[2,16,128]{2,1,0:T(8,128)S(1)}, u32[]{:S(2)}, u32[]{:S(2)}) collective-permute-start(f32[2,16,128]{2,1,0:T(8,128)S(1)} %pad_maximum_fusion.5), channel_id=1, source_target_pairs={{0,16},{2,18},{4,20},{6,22},{8,24},{10,26},{12,28},{14,30},{16,0},... | collective-permute-start | bytes 49160 | tf_op jit(solution)/shard_map/ppermute | solution.py:338
  53.5 8.4 %collective-permute-start.9 = (f32[2,16,128]{2,1,0:T(8,128)S(1)}, f32[2,16,128]{2,1,0:T(8,128)S(1)}, u32[]{:S(2)}, u32[]{:S(2)}) collective-permute-start(f32[2,16,128]{2,1,0:T(8,128)S(1)} %pad_maximum_fusion.6), channel_id=1, source_target_pairs={{0,8},{2,10},{4,12},{6,14},{8,16},{10,18},{12,20},{14,22},{16,24},... | collective-permute-start | bytes 49160 | tf_op jit(solution)/shard_map/ppermute | solution.py:338
  62.6 12.8 %collective-permute-start.10 = (f32[16,128]{1,0:T(8,128)}, f32[16,128]{1,0:T(8,128)S(1)}, u32[]{:S(2)}, u32[]{:S(2)}) collective-permute-start(f32[16,128]{1,0:T(8,128)} %fusion.11), channel_id=1, source_target_pairs={{0,4},{2,6},{4,0},{6,2},{8,12},{10,14},{12,8},{14,10},{16,20},{18,... | collective-permute-start | bytes 24584 | tf_op jit(solution)/shard_map/ppermute | solution.py:348
  74.0 17.9 %collective-permute-start.12 = (f32[16,128]{1,0:T(8,128)}, f32[16,128]{1,0:T(8,128)}, u32[]{:S(2)}, u32[]{:S(2)}) collective-permute-start(f32[16,128]{1,0:T(8,128)} %fusion.11), channel_id=1, source_target_pairs={{0,5},{1,4},{2,7},{3,6},{4,1},{5,0},{6,3},{7,2},{8,13},{9,12},{10,... | collective-permute-start | bytes 24584 | tf_op jit(solution)/shard_map/ppermute | solution.py:355
  76.0 16.0 %collective-permute-start.11 = (f32[16,128]{1,0:T(8,128)}, f32[16,128]{1,0:T(8,128)}, u32[]{:S(2)}, u32[]{:S(2)}) collective-permute-start(f32[16,128]{1,0:T(8,128)} %get-tuple-element.18), channel_id=1, source_target_pairs={{0,1},{1,0},{2,3},{3,2},{4,5},{5,4},{6,7},{7,6},{8,9},{9,8},{10,11... | collective-permute-start | bytes 24584 | tf_op jit(solution)/shard_map/ppermute | solution.py:354
  79.5 13.2 %copy-start.11 = (f32[1,16,128]{2,1,0:T(8,128)S(1)}, f32[1,16,128]{2,1,0:T(8,128)}, u32[]{:S(2)}) copy-start(f32[1,16,128]{2,1,0:T(8,128)} %get-tuple-element.17) | copy-start | bytes 24580
  86.3 21.1 %copy-start.14 = (s32[8]{0:T(128)S(1)}, s32[8]{0:T(128)}, u32[]{:S(2)}) copy-start(s32[8]{0:T(128)} %copy-done.13) | copy-start | bytes 100
  86.3 21.1 %copy-start.15 = (s32[40]{0:T(128)S(1)}, s32[40]{0:T(128)}, u32[]{:S(2)}) copy-start(s32[40]{0:T(128)} %param.18) | copy-start | bytes 484
  86.3 55.9 %copy-start.12 = (s32[2]{0:T(128)S(1)}, s32[2]{0:T(128)}, u32[]{:S(2)}) copy-start(s32[2]{0:T(128)} %get-tuple-element.57) | copy-start | bytes 28
  89.8 67.7 %copy-start.16 = (s32[8]{0:T(128)S(1)}, s32[8]{0:T(128)}, u32[]{:S(2)}) copy-start(s32[8]{0:T(128)} %get-tuple-element.27) | copy-start | bytes 100
  89.8 6.8 %collective-permute-start.2 = (f32[304,128]{1,0:T(8,128)S(1)}, f32[304,128]{1,0:T(8,128)S(1)}, u32[]{:S(2)}, u32[]{:S(2)}) collective-permute-start(f32[304,128]{1,0:T(8,128)S(1)} %get-tuple-element.10), channel_id=1, source_target_pairs={{0,1},{1,0},{2,3},{3,2},{4,5},{5,4},{6,7},{7,6},{8,9},{9,8},{10,11... | collective-permute-start | bytes 466952 | tf_op jit(solution)/shard_map/ppermute | solution.py:432
  104.0 111.2 %copy-start.9 = (f32[1,16,128]{2,1,0:T(8,128)S(1)}, f32[1,16,128]{2,1,0:T(8,128)}, u32[]{:S(2)}) copy-start(f32[1,16,128]{2,1,0:T(8,128)} %param.15) | copy-start | bytes 24580
  104.0 4.9 %collective-permute-start.13 = (f32[16,128]{1,0:T(8,128)S(1)}, f32[16,128]{1,0:T(8,128)S(1)}, u32[]{:S(2)}, u32[]{:S(2)}) collective-permute-start(f32[16,128]{1,0:T(8,128)S(1)} %bitcast.426), channel_id=1, source_target_pairs={{0,32},{2,34},{4,36},{6,38},{8,40},{10,42},{12,44},{14,46},{16,48}... | collective-permute-start | bytes 24584 | tf_op jit(solution)/shard_map/ppermute | solution.py:329
  104.6 5.2 %collective-permute-start.14 = (f32[16,128]{1,0:T(8,128)S(1)}, f32[16,128]{1,0:T(8,128)S(1)}, u32[]{:S(2)}, u32[]{:S(2)}) collective-permute-start(f32[16,128]{1,0:T(8,128)S(1)} %bitcast.427), channel_id=1, source_target_pairs={{0,64},{2,66},{4,68},{6,70},{8,72},{10,74},{12,76},{14,78},{16,80}... | collective-permute-start | bytes 24584 | tf_op jit(solution)/shard_map/ppermute | solution.py:329
  104.6 5.2 %collective-permute-start.15 = (f32[16,128]{1,0:T(8,128)S(1)}, f32[16,128]{1,0:T(8,128)S(1)}, u32[]{:S(2)}, u32[]{:S(2)}) collective-permute-start(f32[16,128]{1,0:T(8,128)S(1)} %bitcast.428), channel_id=1, source_target_pairs={{0,96},{2,98},{4,100},{6,102},{8,104},{10,106},{12,108},{14,110},{... | collective-permute-start | bytes 24584 | tf_op jit(solution)/shard_map/ppermute | solution.py:329
  109.9 27.1 %collective-permute-start.16 = (f32[4,16,128]{2,1,0:T(8,128)S(1)}, f32[4,16,128]{2,1,0:T(8,128)S(1)}, u32[]{:S(2)}, u32[]{:S(2)}) collective-permute-start(f32[4,16,128]{2,1,0:T(8,128)S(1)} %pad_maximum_fusion.3), channel_id=1, source_target_pairs={{0,2},{2,0},{4,6},{6,4},{8,10},{10,8},{12,14},{14,12},{16,18},{18,... | collective-permute-start | bytes 98312 | tf_op jit(solution)/shard_map/ppermute | solution.py:331
  137.0 12.3 %collective-permute-start.17 = (f32[2,16,128]{2,1,0:T(8,128)S(1)}, f32[2,16,128]{2,1,0:T(8,128)S(1)}, u32[]{:S(2)}, u32[]{:S(2)}) collective-permute-start(f32[2,16,128]{2,1,0:T(8,128)S(1)} %pad_maximum_fusion.8), channel_id=1, source_target_pairs={{0,24},{2,26},{4,28},{6,30},{8,0},{10,2},{12,4},{14,6},{16,8},{18,... | collective-permute-start | bytes 49160 | tf_op jit(solution)/shard_map/ppermute | solution.py:338
  139.7 9.6 %collective-permute-start.18 = (f32[2,16,128]{2,1,0:T(8,128)S(1)}, f32[2,16,128]{2,1,0:T(8,128)S(1)}, u32[]{:S(2)}, u32[]{:S(2)}) collective-permute-start(f32[2,16,128]{2,1,0:T(8,128)S(1)} %pad_maximum_fusion.9), channel_id=1, source_target_pairs={{0,16},{2,18},{4,20},{6,22},{8,24},{10,26},{12,28},{14,30},{16,0},... | collective-permute-start | bytes 49160 | tf_op jit(solution)/shard_map/ppermute | solution.py:338
  142.1 7.2 %collective-permute-start.19 = (f32[2,16,128]{2,1,0:T(8,128)S(1)}, f32[2,16,128]{2,1,0:T(8,128)S(1)}, u32[]{:S(2)}, u32[]{:S(2)}) collective-permute-start(f32[2,16,128]{2,1,0:T(8,128)S(1)} %pad_maximum_fusion.10), channel_id=1, source_target_pairs={{0,8},{2,10},{4,12},{6,14},{8,16},{10,18},{12,20},{14,22},{16,24},... | collective-permute-start | bytes 49160 | tf_op jit(solution)/shard_map/ppermute | solution.py:338
  149.3 65.8 %collective-permute-start.20 = (f32[16,128]{1,0:T(8,128)S(1)}, f32[16,128]{1,0:T(8,128)S(1)}, u32[]{:S(2)}, u32[]{:S(2)}) collective-permute-start(f32[16,128]{1,0:T(8,128)S(1)} %fusion.2), channel_id=1, source_target_pairs={{0,4},{2,6},{4,0},{6,2},{8,12},{10,14},{12,8},{14,10},{16,20},{18,... | collective-permute-start | bytes 24584 | tf_op jit(solution)/shard_map/ppermute | solution.py:348
  (7 other events, 6.2 us)

commit v2 on v1

v2 whole, which is shorter than its diff:
```python
import functools
import math

import jax
import jax.numpy as jnp
import numpy as np
from jax import lax
from jax.experimental import pallas as pl
from jax.experimental.pallas import tpu as pltpu
from jax.sharding import PartitionSpec as P

STEPS = 4
REACH = 20
TIME_STEP = 0.1
GRAVITY = 0.2
CONTACT_STIFF = 2.0
CRADLE_CURVE = 0.5
PAD_RATE = 0.2
PAD_STIFF = 1.0

LANES = 128
EDGE = 4
HALO = 48
WIN = 64
CHUNKS = 4
GROUP = 6
LOAD_GROUP = 2
LIMIT = 40 * 1024 * 1024
SIZES = (4, 4, 2, 2)


def arc_digits(index):
    return (index // 16, (index // 4) % 4, (index // 2) % 2, index % 2)


def arc_index(y, z, x, c):
    return (((y % 4) * 4 + z % 4) * 2 + x % 2) * 2 + c % 2


def pairs(shift):
    out = []
    for i in range(64):
        y, z, x, c = arc_digits(i)
        out.append((i, arc_index(y + shift[0], z + shift[1], x + shift[2], c + shift[3])))
    return out


def column_table(circ_total):
    step = 2.0 * math.pi / circ_total
    chord = 2.0 * math.sin(step / 2.0)
    length = math.sqrt(step * step + chord * chord)
    rows = []
    for half in range(2):
        cols = (half * LANES + np.arange(2 * LANES)) % circ_total
        phase = step * (cols + 0.5)
        before = step * (cols - 0.5)
        theta = step * cols
        parts = [
            chord / length * np.cos(phase),
            chord / length * np.sin(phase),
            chord / length * np.cos(before),
            chord / length * np.sin(before),
            np.sin(theta),
            np.cos(theta),
            np.zeros_like(theta),
            np.zeros_like(theta),
        ]
        rows.append(np.concatenate([p.reshape(2, LANES) for p in parts], axis=0))
    axial = step / length
    hoop_gain = 1.0 / (chord / length) ** 2
    return np.stack(rows).astype(np.float32), axial, hoop_gain


def start_kernel(
    halo, slot_ref, lift_ref, rows_ref, near_ref, begin_ref, home_ref, disp, vel, mass, stiff,
    low_edge, high_edge, plan, where_ref, list_ref, lift_out, source, sems,
):
    own = disp.shape[1]
    copies = []
    for n, (edge, at) in enumerate(((low_edge, 0), (high_edge, own - halo))):
        span = pl.ds(at, halo)
        copies += [
            pltpu.make_async_copy(disp.at[:, span, :], edge.at[0:3], sems.at[4 * n]),
            pltpu.make_async_copy(vel.at[:, span, :], edge.at[3:6], sems.at[4 * n + 1]),
            pltpu.make_async_copy(mass.at[span, :], edge.at[6], sems.at[4 * n + 2]),
            pltpu.make_async_copy(stiff.at[span, :], edge.at[7], sems.at[4 * n + 3]),
        ]
    for copy in copies:
        copy.start()
    me = lax.axis_index("arc")
    y, z, x, c = arc_digits(me)
    rollers = slot_ref.shape[0]
    roll = near_ref[me]
    begin = begin_ref[me]
    valid = roll >= 0
    safe = jnp.maximum(roll, 0)
    where_ref[0] = begin
    where_ref[1] = jnp.where(valid, begin, -4 * WIN)
    lift_out[0] = jnp.where(valid, lift_ref[safe], -1e9)
    for step in range(STEPS):
        for m in range(list_ref.shape[1]):
            g = rows_ref[step, safe, m] - (me * own - halo + begin)
            list_ref[step, m] = jnp.clip(g, 0, WIN - 1)

    def clear(i, carry):
        source[i] = -1
        return carry

    def note(r, carry):
        source[slot_ref[r]] = home_ref[r]
        return carry

    lax.fori_loop(0, source.shape[0], clear, 0)
    lax.fori_loop(0, rollers, note, 0)

    def line(value):
        return jnp.full((1, LANES), value, jnp.int32)

    for way in range(2):
        at = 16 * way
        for k in range(4):
            for xr in range(2):
                dest = arc_index(y, z + k, x + xr, c)
                if way == 0:
                    need = slot_ref[jnp.maximum(near_ref[dest], 0)]
                else:
                    need = jnp.maximum(source[dest], 0)
                ny, nz, nx, nc = arc_digits(need)
                plan[at + 2 * k + xr : at + 2 * k + xr + 1, :] = line((nc ^ c) * 4 + (y - ny + 4) % 4)
                if k == 0:
                    plan[at + 8 + xr : at + 9 + xr, :] = line((z - nz + 4) % 4)
                if k == 0 and xr == 0:
                    plan[at + 10 : at + 11, :] = line((nx == x).astype(jnp.int32))
        plan[at + 11 : at + 12, :] = line((source[me] >= 0).astype(jnp.int32))
        plan[at + 12 : at + 16, :] = jnp.zeros((4, LANES), jnp.int32)
    for copy in copies:
        copy.wait()


def prep_kernel(disp, vel, mass, stiff, low, high, ext, pack, sems):
    own = disp.shape[1]
    halo = low.shape[1]
    half = (own + 2 * halo) // 2
    span = pl.ds(halo, own)
    copies = [
        pltpu.make_async_copy(disp, ext.at[0:3, span, :], sems.at[0]),
        pltpu.make_async_copy(vel, ext.at[3:6, span, :], sems.at[1]),
        pltpu.make_async_copy(mass, ext.at[6, span, :], sems.at[2]),
        pltpu.make_async_copy(stiff, ext.at[7, span, :], sems.at[3]),
        pltpu.make_async_copy(low, ext.at[:, 0:halo, :], sems.at[4]),
        pltpu.make_async_copy(high, ext.at[:, halo + own : 2 * halo + own, :], sems.at[5]),
    ]
    for copy in copies:
        copy.start()
    for copy in copies:
        copy.wait()
    lane = lax.broadcasted_iota(jnp.int32, (8, LANES), 1) // (2 * EDGE)

    def body(b, carry):
        for u in range(2):
            r = pl.multiple_of(b * 16, 8) + 8 * u
            packed = jnp.zeros((8, LANES), jnp.float32)
            for part in range(2):
                for a in range(8):
                    value = ext[a, pl.ds(r + part * half, 8), :]
                    moved = pltpu.roll(value, (8 * a + EDGE + 64 * part) % LANES, 1)
                    packed = jnp.where(lane == a + 8 * part, moved, packed)
            pack[pl.ds(r, 8), :] = packed
        return carry

    lax.fori_loop(0, half // 16, body, 0)


def ring_left(tiles, last):
    a, b = (pltpu.roll(t, LANES - 1, 1) for t in tiles)
    return jnp.where(last, b, a), jnp.where(last, a, b)


def ring_right(tiles, first):
    a, b = (pltpu.roll(t, 1, 1) for t in tiles)
    return jnp.where(first, b, a), jnp.where(first, a, b)


def unpack_block(pack, row, half, a, keep):
    upper = row >= half
    at = pl.multiple_of(jnp.where(upper, row - half, row), 8)
    shift = jnp.where(upper, (2 * LANES - 8 * a - EDGE - 64) % LANES, (2 * LANES - 8 * a - EDGE) % LANES)
    return jnp.where(keep, pltpu.roll(pack[pl.ds(at, 8), :], shift, 1), 0.0)


def load_state(source, pack, first_row, base, cycle_total, rows, half, state, vels, coef):
    lane = lax.broadcasted_iota(jnp.int32, (8, LANES), 1)
    sub = lax.broadcasted_iota(jnp.int32, (8, LANES), 0)
    keep = (lane < EDGE) | (lane >= LANES - EDGE)
    first = lane == 0
    top = sub == 0

    def body(b, carry):
        r = pl.multiple_of(b * 8, 8)
        e = first_row + r
        span = pl.ds(r, 8)
        for a in range(3):
            state[0, a, 0, span, :] = source(a, r)
            state[0, a, 1, span, :] = unpack_block(pack, e, half, a, keep)
            vels[a, 0, span, :] = TIME_STEP * source(3 + a, r)
            vels[a, 1, span, :] = TIME_STEP * unpack_block(pack, e, half, 3 + a, keep)
        for t, m in enumerate((source(6, r), unpack_block(pack, e, half, 6, keep))):
            coef[0, t, span, :] = (TIME_STEP * TIME_STEP) / jnp.where(m > 0.0, m, 1.0)
        ids = base + e + sub
        inside = (ids >= 0) & (ids < cycle_total - 1)
        k = [
            jnp.where(inside, v, 0.0)
            for v in (source(7, r), unpack_block(pack, e, half, 7, keep))
        ]
        kr = ring_right(k, first)
        new = []
        for t in range(2):
            down = pltpu.roll(k[t], 1, 0)
            coef[1, t, span, :] = k[t]
            coef[2, t, span, :] = 0.5 * (k[t] + kr[t])
            coef[3, t, span, :] = (0.5 * HOOP_GAIN) * (k[t] + jnp.where(top, carry[t], down))
            new.append(down)
        return tuple(new)

    zero = jnp.zeros((8, LANES), jnp.float32)
    group = LOAD_GROUP

    def several(b, carry):
        for u in range(group):
            carry = body(b * group + u, carry)
        return carry

    lax.fori_loop(0, rows // (8 * group), several, (zero, zero))
    for buf in range(2):
        for a in range(3):
            for t in range(2):
                state[buf, a, t, rows : rows + 8, :] = zero


TABLE, AXIAL, HOOP_GAIN = column_table(2 * LANES)


def advance(table, rows, step, state, vels, coef, group, push=None):
    now, later = step % 2, (step + 1) % 2
    lane = lax.broadcasted_iota(jnp.int32, (8, LANES), 1)
    top = lax.broadcasted_iota(jnp.int32, (8, LANES), 0) == 0
    first, last = lane == 0, lane == LANES - 1

    def const(i):
        return [jnp.broadcast_to(table[2 * i + t : 2 * i + t + 1, :], (8, LANES)) for t in range(2)]

    cj, sj, cb, sb = (const(i) for i in range(4))
    two = range(2)

    def block(r, carry):
        span, below = pl.ds(r, 8), pl.ds(r + 1, 8)
        x, y, z = ([state[now, a, t, span, :] for t in two] for a in range(3))
        xn, yn, zn = ([state[now, a, t, below, :] for t in two] for a in range(3))
        p = [cj[t] * y[t] + sj[t] * z[t] for t in two]
        q = [cb[t] * y[t] + sb[t] * z[t] for t in two]
        ax = [AXIAL * x[t] for t in two]
        pn = [cj[t] * yn[t] + sj[t] * zn[t] for t in two]
        qn = [cb[t] * yn[t] + sb[t] * zn[t] for t in two]
        axn = [AXIAL * xn[t] for t in two]
        q_next = ring_left(q, last)
        anti_next = ring_left([q[t] - ax[t] for t in two], last)
        diag_next = ring_left([qn[t] + axn[t] for t in two], last)
        k = [coef[1, t, span, :] for t in two]
        t_d = [k[t] * (diag_next[t] - (p[t] + ax[t])) for t in two]
        t_a = [k[t] * (anti_next[t] - (pn[t] - axn[t])) for t in two]
        t_h = [coef[3, t, span, :] * (q_next[t] - p[t]) for t in two]
        fx = [coef[2, t, span, :] * (xn[t] - x[t]) for t in two]
        d_left = ring_right(t_d, first)
        a_left = ring_right(t_a, first)
        g_left = ring_right([t_a[t] + t_h[t] for t in two], first)
        new = []
        for t in two:
            up = t_d[t] + t_h[t]
            force = [
                fx[t] + AXIAL * (t_d[t] + a_left[t]),
                cj[t] * up - cb[t] * g_left[t],
                sj[t] * up - sb[t] * g_left[t],
            ]
            low = [
                fx[t] + AXIAL * (d_left[t] + t_a[t]),
                cb[t] * d_left[t] - cj[t] * t_a[t],
                sb[t] * d_left[t] - sj[t] * t_a[t],
            ]
            at = (x[t], y[t], z[t])
            inverse = coef[0, t, span, :]
            for a in range(3):
                moved = pltpu.roll(low[a], 1, 0)
                total = force[a] - jnp.where(top, carry[3 * t + a], moved)
                new.append(moved)
                if push is not None and a > 0:
                    total = total + push[a - 1, t, span, :]
                w = vels[a, t, span, :] + inverse * total
                if a == 2:
                    w = w - (GRAVITY * TIME_STEP * TIME_STEP)
                vels[a, t, span, :] = w
                state[later, a, t, span, :] = at[a] + w
        return tuple(new)

    def body(b, carry):
        for u in range(group):
            carry = block(pl.multiple_of(b * (8 * group), 8) + 8 * u, carry)
        return carry

    zero = jnp.zeros((8, LANES), jnp.float32)
    carry = (zero,) * 6
    if group * 8 == rows:
        for u in range(group):
            carry = block(8 * u, carry)
    else:
        lax.fori_loop(0, rows // (8 * group), body, carry)


def window_kernel(
    half, base, cycle_total, where_ref, list_ref, lift_ref, table, plan, ext, pack, mine, near, far, cross,
    result, pad_out, raw, state, vels, coef, push, taken, given, held, sem,
):
    start = pl.multiple_of(where_ref[0], 8)
    copy = pltpu.make_async_copy(ext.at[:, pl.ds(start, WIN), :], raw, sem)
    copy.start()
    copy.wait()
    first_id = base(lax.axis_index("arc"))
    load_state(
        lambda a, r: raw[a, pl.ds(r, 8), :], pack, start, first_id, cycle_total, WIN, half, state, vels, coef
    )
    same = plan[10:11, :] > 0
    held[0] = jnp.where(same, mine[0], near[...])
    held[1] = jnp.where(same, far[...], cross[...])
    slots = near.shape[0]
    lift = lift_ref[0]
    for step in range(STEPS):
        now = step % 2
        push[...] = jnp.zeros_like(push)
        for m in range(slots):
            g = list_ref[step, m]
            for a in range(2):
                for t in range(2):
                    taken[a, t, m : m + 1, :] = state[now, a + 1, t, pl.ds(g, 1), :]
        for t in range(2):
            sin_angle, cos_angle = table[8 + t : 9 + t, :], table[10 + t : 11 + t, :]
            lateral = sin_angle + taken[0, t]
            q = held[t]
            intrusion = lift + CRADLE_CURVE * lateral * lateral - (1.0 - cos_angle) - taken[1, t] - q
            load = CONTACT_STIFF * jnp.maximum(intrusion, 0.0)
            normal = load / jnp.sqrt(1.0 + 4.0 * CRADLE_CURVE * CRADLE_CURVE * lateral * lateral)
            given[0, t] = -2.0 * CRADLE_CURVE * lateral * normal
            given[1, t] = normal
            held[t] = q + PAD_RATE * (load - PAD_STIFF * q)
        for m in range(slots):
            g = list_ref[step, m]
            for a in range(2):
                for t in range(2):
                    push[a, t, pl.ds(g, 1), :] += given[a, t, m : m + 1, :]
        advance(table, WIN, step, state, vels, coef, WIN // 8, push)
    for a in range(3):
        result[a] = state[STEPS % 2, a, 0, :WIN, :]
        result[3 + a] = vels[a, 0] * (1.0 / TIME_STEP)
    pad_out[...] = held[0]


def bulk_kernel(half, base, cycle_total, rows, chunk, where_ref, table, ext, pack, window, *rest):
    disp_out, vel_out, state, vels, coef, result, sems = rest[-7:]
    count = rows - 16
    first_row = HALO - 8 + chunk * count

    def source(a, r):
        return ext[a, pl.ds(pl.multiple_of(first_row + r, 8), 8), :]

    first_id = base(lax.axis_index("arc"))
    load_state(source, pack, first_row, first_id, cycle_total, rows, half, state, vels, coef)
    for step in range(STEPS):
        advance(table, rows, step, state, vels, coef, GROUP)
    start = where_ref[1]
    sub = lax.broadcasted_iota(jnp.int32, (8, LANES), 0)

    def body(b, carry):
        r = pl.multiple_of(b * 8, 8)
        inner = pl.ds(pl.multiple_of(r + 8, 8), 8)
        rel = first_row + 8 + r - start
        at = pl.ds(pl.multiple_of(jnp.clip(rel, 0, WIN - 8), 8), 8)
        ids = rel + sub
        use = (ids >= STEPS) & (ids < WIN - STEPS)
        for a in range(3):
            result[a, pl.ds(r, 8), :] = jnp.where(use, window[a, at, :], state[STEPS % 2, a, 0, inner, :])
            result[3 + a, pl.ds(r, 8), :] = jnp.where(
                use, window[3 + a, at, :], vels[a, 0, inner, :] * (1.0 / TIME_STEP)
            )
        return carry

    lax.fori_loop(0, count // 8, body, 0)
    span = pl.ds(chunk * count, count)
    copies = [
        pltpu.make_async_copy(result.at[0:3], disp_out.at[:, span, :], sems.at[0]),
        pltpu.make_async_copy(result.at[3:6], vel_out.at[:, span, :], sems.at[1]),
    ]
    for copy in copies:
        copy.start()
    for copy in copies:
        copy.wait()


def pick_kernel(way, plan, held, other, *outs):
    parts = [ref[n] for ref in (held, other) for n in range(4)]
    for k in range(4):
        for xr in range(2):
            at = 16 * way + 2 * k + xr
            index = plan[at : at + 1, :]
            value = parts[0]
            for n in range(1, 8):
                value = jnp.where(index == n, parts[n], value)
            outs[k][xr] = value


def join_kernel(way, plan, *refs):
    parts, out = refs[:4], refs[4]
    for xr in range(2):
        at = 16 * way + 8 + xr
        back = plan[at : at + 1, :]
        value = parts[0][xr]
        for k in range(1, 4):
            value = jnp.where(back == k, parts[k][xr], value)
        out[xr] = value


def last_kernel(plan, mine, near, before, out):
    used = plan[27:28, :] > 0
    same = plan[26:27, :] > 0
    out[0] = jnp.where(used, jnp.where(same, mine[0], near[...]), before[0])


def route(value, plan, way):
    shape = value.shape
    vmem = pl.BlockSpec(memory_space=pltpu.VMEM)
    params = pltpu.CompilerParams(vmem_limit_bytes=LIMIT)
    got = [value]
    for k in range(1, 4):
        got.append(lax.ppermute(value, "arc", pairs((k, 0, 0, 0))))
    held = jnp.stack(got)
    other = lax.ppermute(held, "arc", pairs((0, 0, 0, 1)))
    two = jax.ShapeDtypeStruct((2,) + shape, jnp.float32)
    parts = pl.pallas_call(
        functools.partial(pick_kernel, way),
        out_shape=(two,) * 4,
        in_specs=[vmem] * 3,
        out_specs=(vmem,) * 4,
        compiler_params=params,
        name="pick",
    )(plan, held, other)
    parts = [parts[0]] + [lax.ppermute(parts[k], "arc", pairs((0, k, 0, 0))) for k in range(1, 4)]
    return pl.pallas_call(
        functools.partial(join_kernel, way),
        out_shape=two,
        in_specs=[vmem] * 5,
        out_specs=vmem,
        compiler_params=params,
        name="join",
    )(plan, *parts)


def static_tables(arc_count, cycle_dev, roller_total):
    cycle_total = arc_count * cycle_dev
    centres = [r * (cycle_total - 1) // (roller_total - 1) for r in range(roller_total)]
    span = REACH + STEPS - 1
    near = np.full(arc_count, -1, np.int32)
    start = np.zeros(arc_count, np.int32)
    for d in range(arc_count):
        base = d * cycle_dev
        touching = [r for r, c in enumerate(centres) if base - span <= c < base + cycle_dev + span]
        assert len(touching) <= 1
        if touching:
            near[d] = touching[0]
            offset = centres[touching[0]] - base - REACH - STEPS - STEPS + 1 + HALO
            start[d] = offset // 8 * 8
            assert 0 <= start[d] <= cycle_dev + 2 * HALO - WIN
    home = np.array([c // cycle_dev for c in centres], np.int32)
    return near, start, home


def local(displacement, velocity, node_mass, wall_stiff, pad_state, roller_lift, contact_rows, roller_slot):
    cycle_dev = displacement.shape[1]
    slots = pad_state.shape[1]
    roller_total = roller_lift.shape[0]
    arc_count = lax.axis_size("arc")
    cycle_total = cycle_dev * arc_count
    total = cycle_dev + 2 * HALO
    half = total // 2
    near, begin, home = static_tables(arc_count, cycle_dev, roller_total)
    vmem = pl.BlockSpec(memory_space=pltpu.VMEM)
    smem = pl.BlockSpec(memory_space=pltpu.SMEM)
    anywhere = pl.BlockSpec(memory_space=pl.ANY)
    params = pltpu.CompilerParams(vmem_limit_bytes=LIMIT)

    def real(*shape):
        return jax.ShapeDtypeStruct(shape, jnp.float32)

    def whole(*shape):
        return jax.ShapeDtypeStruct(shape, jnp.int32)

    fields = (displacement, velocity, node_mass, wall_stiff)
    low_edge, high_edge, plan, where, rows_in, lift = pl.pallas_call(
        functools.partial(start_kernel, HALO),
        out_shape=(
            real(8, HALO, LANES), real(8, HALO, LANES), whole(32, LANES), whole(2), whole(STEPS, slots), real(1),
        ),
        in_specs=[smem] * 6 + [anywhere] * 4,
        out_specs=(vmem, vmem, vmem, smem, smem, smem),
        scratch_shapes=[pltpu.SMEM((arc_count,), jnp.int32), pltpu.SemaphoreType.DMA((8,))],
        compiler_params=params,
        name="start",
    )(roller_slot, roller_lift, contact_rows, jnp.asarray(near), jnp.asarray(begin), jnp.asarray(home), *fields)

    up = [(i, i + 1) for i in range(arc_count - 1)]
    low = lax.ppermute(high_edge, "arc", up)
    high = lax.ppermute(low_edge, "arc", [(b, a) for a, b in up])

    mine = route(pad_state[0], plan, 0)
    across = pairs((0, 0, 1, 0))
    swap = [(0, 1), (1, 0)]
    double = [(2 * s + h, 2 * d + 1 - h) for s, d in across for h in range(2)]
    near_pad = lax.ppermute(mine[1], "arc", across)
    far_pad = lax.ppermute(mine[0], "circ", swap)
    cross_pad = lax.ppermute(mine[1], ("arc", "circ"), double)

    ext, pack = pl.pallas_call(
        prep_kernel,
        out_shape=(real(8, total, LANES), real(half, LANES)),
        in_specs=[anywhere] * 6,
        out_specs=(vmem, vmem),
        scratch_shapes=[pltpu.SemaphoreType.DMA((6,))],
        compiler_params=params,
        name="prep",
    )(*fields, low, high)
    pack = lax.ppermute(pack, "circ", swap)
    table = jnp.asarray(TABLE)[lax.axis_index("circ")]

    def scratch(rows):
        return [
            pltpu.VMEM((2, 3, 2, rows + 8, LANES), jnp.float32),
            pltpu.VMEM((3, 2, rows, LANES), jnp.float32),
            pltpu.VMEM((4, 2, rows, LANES), jnp.float32),
        ]

    def base(me):
        return me * cycle_dev - HALO

    window, pad_new = pl.pallas_call(
        functools.partial(window_kernel, half, base, cycle_total),
        out_shape=(real(6, WIN, LANES), real(slots, LANES)),
        in_specs=[smem] * 3 + [vmem, vmem, anywhere] + [vmem] * 5,
        out_specs=(vmem, vmem),
        scratch_shapes=[pltpu.VMEM((8, WIN, LANES), jnp.float32)]
        + scratch(WIN)
        + [
            pltpu.VMEM((2, 2, WIN, LANES), jnp.float32),
            pltpu.VMEM((2, 2, slots, LANES), jnp.float32),
            pltpu.VMEM((2, 2, slots, LANES), jnp.float32),
            pltpu.VMEM((2, slots, LANES), jnp.float32),
            pltpu.SemaphoreType.DMA,
        ],
        compiler_params=params,
        name="window",
    )(where, rows_in, lift, table, plan, ext, pack, mine, near_pad, far_pad, cross_pad)

    rows = cycle_dev // CHUNKS + 16
    outs = ()
    for chunk in range(CHUNKS):
        outs = pl.pallas_call(
            functools.partial(bulk_kernel, half, base, cycle_total, rows, chunk),
            out_shape=(real(3, cycle_dev, LANES),) * 2,
            in_specs=[smem] + [vmem] * 4 + [anywhere] * len(outs),
            out_specs=(anywhere, anywhere),
            input_output_aliases={5: 0, 6: 1} if outs else {},
            scratch_shapes=scratch(rows)
            + [pltpu.VMEM((6, rows - 16, LANES), jnp.float32), pltpu.SemaphoreType.DMA((2,))],
            compiler_params=params,
            cost_estimate=pl.CostEstimate(flops=0, bytes_accessed=48_000_000 // CHUNKS, transcendentals=0),
            name="bulk",
        )(where, table, ext, pack, window, *outs)

    back = route(pad_new, plan, 1)
    pad_result = pl.pallas_call(
        last_kernel,
        out_shape=real(1, slots, LANES),
        in_specs=[vmem] * 4,
        out_specs=vmem,
        compiler_params=params,
        name="last",
    )(plan, back, lax.ppermute(back[1], "arc", across), pad_state)
    return outs[0], outs[1], pad_result


def solution(mesh):
    placed = (
        P(None, "arc", "circ"),
        P(None, "arc", "circ"),
        P("arc", "circ"),
        P("arc", "circ"),
        P("arc", None, "circ"),
        P(),
        P(),
        P(),
    )
    return jax.shard_map(
        local,
        mesh=mesh,
        in_specs=placed,
        out_specs=(P(None, "arc", "circ"), P(None, "arc", "circ"), P("arc", None, "circ")),
        check_vma=False,
    )
```

time: 219 us -> 93.8 us (0.43)
  between operations: 82.6 us -> 0.86 us
  Pallas kernels: 68.4 us -> 31.4 us
  waiting for transfers between devices: 6.42 us -> 17.9 us
  other arithmetic: 11.8 us -> 0.7 us
  local copies, waits for them, and re-layouts: 12.3 us -> 8.31 us
    pallas_call x3 -> x12, Pallas kernels: 68.4 us -> 31.4 us  [the longest x4 21.4 us: local(): pl.pallas_call(functools.partial(bulk_kernel, half, base, cycle_total, ro...]
    another operation x22 -> x0, other arithmetic: 6.37 us -> none  [the longest x18 4.33 us: pick(): return jnp.stack(out)]
    ppermute x6, waiting for transfers between devices: 2.41 us -> 7.67 us  [route(): got.append(lax.ppermute(value, 'arc', pairs((k, 0, 0, 0))))]
    ppermute x6, starting transfers between devices: 9.37 us -> 13.9 us  [route(): got.append(lax.ppermute(value, 'arc', pairs((k, 0, 0, 0))))]
    ppermute x13, starting transfers between devices: 24.3 us -> 20.2 us  [the longest x6 8.67 us: route(): lax.ppermute(parts[k], 'arc', pairs((0, k, 0, 0)))]
    slice x6 -> x0, local copies, waits for them, and re-layouts: 4.11 us -> none  [the longest x2 1.35 us: pick(): value = jnp.where(index[i] == n, held[n], value)]
    ppermute x13, waiting for transfers between devices: 4 us -> 7.8 us  [the longest x6 6.08 us: route(): lax.ppermute(parts[k], 'arc', pairs((0, k, 0, 0)))]
    unnamed x36 -> x31, local copies, waits for them, and re-layouts: 5.34 us -> 8.3 us
  transfers between devices with their start and end apart: 21 -> 21, of which waited for: 4 -> 14; matrix products, arithmetic and copies ran while one was open for 8% -> 1% of each run, Pallas kernels for 28% -> 23%
where the time goes in v2:
time: 93.8 us; the launch traced here: 93.2 us
  starting transfers between devices  34 us (36%)
  Pallas kernels  31.4 us (33%)
  waiting for transfers between devices  17.9 us (19%)
  local copies, waits for them, and re-layouts  8.31 us (9%)
    pallas_call x4, Pallas kernels, local(): pl.pallas_call(functools.partial(bulk_kernel, half, base, cycle_total, ro...  21.4 us
    ppermute x6, starting transfers between devices, route(): got.append(lax.ppermute(value, 'arc', pairs((k, 0, 0, 0))))  13.9 us
    ppermute x6, starting transfers between devices, route(): lax.ppermute(parts[k], 'arc', pairs((0, k, 0, 0)))  8.67 us
    unnamed x31, local copies, waits for them, and re-layouts  8.3 us
    ppermute x6, waiting for transfers between devices, route(): got.append(lax.ppermute(value, 'arc', pairs((k, 0, 0, 0))))  7.67 us
    ppermute x6, waiting for transfers between devices, route(): lax.ppermute(parts[k], 'arc', pairs((0, k, 0, 0)))  6.08 us
    ppermute x1, starting transfers between devices, local(): far_pad = lax.ppermute(mine[0], 'circ', swap)  4.23 us
    pallas_call x1, Pallas kernels, local(): pl.pallas_call(functools.partial(start_kernel, HALO), out_shape=(real(8,...  3.94 us
  transfers between devices with their start and end apart: 21, of which 14 were waited for; matrix products, arithmetic and copies ran while one was open for 1% of the time, Pallas kernels for 23%

profile of v2, /device:TPU:0, one launch (start us, length us, event | category | flops | bytes accessed | tf_op | source)
XLA Modules:
  0.0 93.2 jit_solution(13136143863191415796)
XLA Ops:
  1.5 1.1 %copy-done = f32[3,512,128]{2,1,0:T(8,128)S(1)} copy-done((f32[3,512,128]{2,1,0:T(8,128)S(1)}, f32[3,512,128]{2,1,0:T(8,128)}, u32[]{:S(2)}) %copy-start) | copy-done | bytes 786456
  2.6 1.1 %copy-done.2 = f32[3,512,128]{2,1,0:T(8,128)S(1)} copy-done((f32[3,512,128]{2,1,0:T(8,128)S(1)}, f32[3,512,128]{2,1,0:T(8,128)}, u32[]{:S(2)}) %copy-start.2) | copy-done | bytes 786456
  3.7 0.9 %copy-done.4 = f32[512,128]{1,0:T(8,128)S(1)} copy-done((f32[512,128]{1,0:T(8,128)S(1)}, f32[512,128]{1,0:T(8,128)}, u32[]{:S(2)}) %copy-start.4) | copy-done | bytes 262168
  4.7 0.9 %copy-done.6 = f32[512,128]{1,0:T(8,128)S(1)} copy-done((f32[512,128]{1,0:T(8,128)S(1)}, f32[512,128]{1,0:T(8,128)}, u32[]{:S(2)}) %copy-start.6) | copy-done | bytes 262168
  8.9 3.9 %start.1 = (f32[8,48,128]{2,1,0:T(8,128)S(1)}, f32[8,48,128]{2,1,0:T(8,128)S(1)}, s32[32,128]{1,0:T(8,128)S(1)}, s32[2]{0:T(128)S(1)}, s32[4,16]{1,0:T(4,128)S(1)}, /*index=5*/f32[1]{0:T(128)}) custom-call(s32[40]{0:T(128)S(1)} %copy-done.9, f32[40]{0:T(128)S(1)} %copy-done.10, s32[4,40,16]{2,1,0:T(8,128)S(1)} %copy.21.rows_ref, s32[64]{0:T(128)S(1)} %copy-done.13, ...), custom_call_target="tpu_custom_call" | custom-call | tf_op jit(solution)/shard_map/start/pallas_call | solution.py:504
  12.9 1.3 %collective-permute-start = (f32[8,48,128]{2,1,0:T(8,128)S(1)}, f32[8,48,128]{2,1,0:T(8,128)S(1)}, u32[]{:S(2)}, u32[]{:S(2)}) collective-permute-start(f32[8,48,128]{2,1,0:T(8,128)S(1)} %get-tuple-element.30), channel_id=1, source_target_pairs={{0,2},{2,4},{4,6},{6,8},{8,10},{10,12},{12,14},{14,16},{16,18},{18... | collective-permute-start | bytes 589832 | tf_op jit(solution)/shard_map/ppermute | solution.py:517
  14.2 1.3 %collective-permute-start.1 = (f32[8,48,128]{2,1,0:T(8,128)S(1)}, f32[8,48,128]{2,1,0:T(8,128)S(1)}, u32[]{:S(2)}, u32[]{:S(2)}) collective-permute-start(f32[8,48,128]{2,1,0:T(8,128)S(1)} %get-tuple-element.31), channel_id=1, source_target_pairs={{2,0},{4,2},{6,4},{8,6},{10,8},{12,10},{14,12},{16,14},{18,16},{20... | collective-permute-start | bytes 589832 | tf_op jit(solution)/shard_map/ppermute | solution.py:518
  15.5 9.1 %collective-permute-start.5 = (f32[16,128]{1,0:T(8,128)}, f32[16,128]{1,0:T(8,128)S(1)}, u32[]{:S(2)}, u32[]{:S(2)}) collective-permute-start(f32[16,128]{1,0:T(8,128)} %bitcast.16), channel_id=1, source_target_pairs={{0,96},{2,98},{4,100},{6,102},{8,104},{10,106},{12,108},{14,110},{... | collective-permute-start | bytes 24584 | tf_op jit(solution)/shard_map/ppermute | solution.py:441
  25.3 1.0 %collective-permute-start.3 = (f32[16,128]{1,0:T(8,128)}, f32[16,128]{1,0:T(8,128)S(1)}, u32[]{:S(2)}, u32[]{:S(2)}) collective-permute-start(f32[16,128]{1,0:T(8,128)} %bitcast.18), channel_id=1, source_target_pairs={{0,32},{2,34},{4,36},{6,38},{8,40},{10,42},{12,44},{14,46},{16,48}... | collective-permute-start | bytes 24584 | tf_op jit(solution)/shard_map/ppermute | solution.py:441
  26.3 3.8 %collective-permute-done.4 = f32[16,128]{1,0:T(8,128)S(1)} collective-permute-done((f32[16,128]{1,0:T(8,128)}, f32[16,128]{1,0:T(8,128)S(1)}, u32[]{:S(2)}, u32[]{:S(2)}) %collective-permute-start.4) | collective-permute-done | bytes 8224 | tf_op jit(solution)/shard_map/ppermute | solution.py:441
  31.1 1.2 %collective-permute-done.6.other = f32[4,16,128]{2,1,0:T(8,128)S(1)} collective-permute-done((f32[4,16,128]{2,1,0:T(8,128)S(1)}, f32[4,16,128]{2,1,0:T(8,128)S(1)}, u32[]{:S(2)}, u32[]{:S(2)}) %collective-permute-start.6) | collective-permute-done | bytes 32800 | tf_op jit(solution)/shard_map/ppermute | solution.py:443
  32.4 3.4 %collective-permute-start.8 = (f32[2,16,128]{2,1,0:T(8,128)S(1)}, f32[2,16,128]{2,1,0:T(8,128)S(1)}, u32[]{:S(2)}, u32[]{:S(2)}) collective-permute-start(f32[2,16,128]{2,1,0:T(8,128)S(1)} %get-tuple-element.39), channel_id=1, source_target_pairs={{0,16},{2,18},{4,20},{6,22},{8,24},{10,26},{12,28},{14,30},{16,0},... | collective-permute-start | bytes 49160 | tf_op jit(solution)/shard_map/ppermute | solution.py:453
  35.8 1.0 %collective-permute-start.9 = (f32[2,16,128]{2,1,0:T(8,128)S(1)}, f32[2,16,128]{2,1,0:T(8,128)S(1)}, u32[]{:S(2)}, u32[]{:S(2)}) collective-permute-start(f32[2,16,128]{2,1,0:T(8,128)S(1)} %get-tuple-element.40), channel_id=1, source_target_pairs={{0,24},{2,26},{4,28},{6,30},{8,0},{10,2},{12,4},{14,6},{16,8},{18,... | collective-permute-start | bytes 49160 | tf_op jit(solution)/shard_map/ppermute | solution.py:453
  37.7 1.8 %collective-permute-done.9.refs_3_ = f32[2,16,128]{2,1,0:T(8,128)S(1)} collective-permute-done((f32[2,16,128]{2,1,0:T(8,128)S(1)}, f32[2,16,128]{2,1,0:T(8,128)S(1)}, u32[]{:S(2)}, u32[]{:S(2)}) %collective-permute-start.9) | collective-permute-done | bytes 16416 | tf_op jit(solution)/shard_map/ppermute | solution.py:453
  39.6 2.4 %prep.1 = (f32[8,608,128]{2,1,0:T(8,128)S(1)}, f32[304,128]{1,0:T(8,128)S(1)}) custom-call(f32[3,512,128]{2,1,0:T(8,128)S(1)} %copy-done.1, f32[3,512,128]{2,1,0:T(8,128)S(1)} %copy-done.3, f32[512,128]{1,0:T(8,128)S(1)} %copy-done.5, f32[512,128]{1,0:T(8,128)S(1)} %copy-done.7, f32[8,48,128]{2,1,0:T(8,128)S(1)} %collective-permute-done.low, ...), custom_call_target="tpu_custom_call" | custom-call | tf_op jit(solution)/shard_map/prep/pallas_call | solution.py:528
  41.9 3.1 %collective-permute-start.2 = (f32[304,128]{1,0:T(8,128)S(1)}, f32[304,128]{1,0:T(8,128)S(1)}, u32[]{:S(2)}, u32[]{:S(2)}) collective-permute-start(f32[304,128]{1,0:T(8,128)S(1)} %get-tuple-element.33), channel_id=1, source_target_pairs={{0,1},{1,0},{2,3},{3,2},{4,5},{5,4},{6,7},{7,6},{8,9},{9,8},{10,11... | collective-permute-start | bytes 466952 | tf_op jit(solution)/shard_map/ppermute | solution.py:537
  45.5 4.2 %collective-permute-start.11 = (f32[16,128]{1,0:T(8,128)S(1)}, f32[16,128]{1,0:T(8,128)S(1)}, u32[]{:S(2)}, u32[]{:S(2)}) collective-permute-start(f32[16,128]{1,0:T(8,128)S(1)} %get-tuple-element.55), channel_id=1, source_target_pairs={{0,1},{1,0},{2,3},{3,2},{4,5},{5,4},{6,7},{7,6},{8,9},{9,8},{10,11... | collective-permute-start | bytes 24584 | tf_op jit(solution)/shard_map/ppermute | solution.py:525
  49.8 1.7 %collective-permute-done.11.far = f32[16,128]{1,0:T(8,128)S(1)} collective-permute-done((f32[16,128]{1,0:T(8,128)S(1)}, f32[16,128]{1,0:T(8,128)S(1)}, u32[]{:S(2)}, u32[]{:S(2)}) %collective-permute-start.11) | collective-permute-done | bytes 8224 | tf_op jit(solution)/shard_map/ppermute | solution.py:525
  51.5 3.0 %window.1 = (f32[6,64,128]{2,1,0:T(8,128)S(1)}, f32[16,128]{1,0:T(8,128)S(1)}) custom-call(s32[2]{0:T(128)S(1)} %get-tuple-element.29.where_ref, s32[4,16]{1,0:T(4,128)S(1)} %get-tuple-element.34.list_ref, f32[1]{0:T(128)} %get-tuple-element.35.lift_ref, f32[16,128]{1,0:T(8,128)S(1)} %dynamic-slice_bitcast_fusion.table, ...), custom_call_target="tpu_custom_call" | custom-call | tf_op jit(solution)/shard_map/window/pallas_call | solution.py:550
  55.0 1.3 %collective-permute-start.14 = (f32[16,128]{1,0:T(8,128)S(1)}, f32[16,128]{1,0:T(8,128)S(1)}, u32[]{:S(2)}, u32[]{:S(2)}) collective-permute-start(f32[16,128]{1,0:T(8,128)S(1)} %get-tuple-element.50), channel_id=1, source_target_pairs={{0,64},{2,66},{4,68},{6,70},{8,72},{10,74},{12,76},{14,78},{16,80}... | collective-permute-start | bytes 24584 | tf_op jit(solution)/shard_map/ppermute | solution.py:441
  56.3 1.3 %collective-permute-start.13 = (f32[16,128]{1,0:T(8,128)S(1)}, f32[16,128]{1,0:T(8,128)S(1)}, u32[]{:S(2)}, u32[]{:S(2)}) collective-permute-start(f32[16,128]{1,0:T(8,128)S(1)} %get-tuple-element.50), channel_id=1, source_target_pairs={{0,32},{2,34},{4,36},{6,38},{8,40},{10,42},{12,44},{14,46},{16,48}... | collective-permute-start | bytes 24584 | tf_op jit(solution)/shard_map/ppermute | solution.py:441
  58.2 1.9 %collective-permute-done.14 = f32[16,128]{1,0:T(8,128)S(1)} collective-permute-done((f32[16,128]{1,0:T(8,128)S(1)}, f32[16,128]{1,0:T(8,128)S(1)}, u32[]{:S(2)}, u32[]{:S(2)}) %collective-permute-start.14) | collective-permute-done | bytes 8224 | tf_op jit(solution)/shard_map/ppermute | solution.py:441
  60.1 1.1 %collective-permute-done.13 = f32[16,128]{1,0:T(8,128)S(1)} collective-permute-done((f32[16,128]{1,0:T(8,128)S(1)}, f32[16,128]{1,0:T(8,128)S(1)}, u32[]{:S(2)}, u32[]{:S(2)}) %collective-permute-start.13) | collective-permute-done | bytes 8224 | tf_op jit(solution)/shard_map/ppermute | solution.py:441
  61.2 1.2 %collective-permute-done.16.other = f32[4,16,128]{2,1,0:T(8,128)S(1)} collective-permute-done((f32[4,16,128]{2,1,0:T(8,128)S(1)}, f32[4,16,128]{2,1,0:T(8,128)S(1)}, u32[]{:S(2)}, u32[]{:S(2)}) %collective-permute-start.16) | collective-permute-done | bytes 32800 | tf_op jit(solution)/shard_map/ppermute | solution.py:443
  63.3 3.0 %collective-permute-start.18 = (f32[2,16,128]{2,1,0:T(8,128)S(1)}, f32[2,16,128]{2,1,0:T(8,128)S(1)}, u32[]{:S(2)}, u32[]{:S(2)}) collective-permute-start(f32[2,16,128]{2,1,0:T(8,128)S(1)} %get-tuple-element.53), channel_id=1, source_target_pairs={{0,16},{2,18},{4,20},{6,22},{8,24},{10,26},{12,28},{14,30},{16,0},... | collective-permute-start | bytes 49160 | tf_op jit(solution)/shard_map/ppermute | solution.py:453
  66.7 1.0 %collective-permute-done.17.refs_1_ = f32[2,16,128]{2,1,0:T(8,128)S(1)} collective-permute-done((f32[2,16,128]{2,1,0:T(8,128)S(1)}, f32[2,16,128]{2,1,0:T(8,128)S(1)}, u32[]{:S(2)}, u32[]{:S(2)}) %collective-permute-start.17) | collective-permute-done | bytes 16416 | tf_op jit(solution)/shard_map/ppermute | solution.py:453
  68.5 1.5 %collective-permute-done.19.refs_3_ = f32[2,16,128]{2,1,0:T(8,128)S(1)} collective-permute-done((f32[2,16,128]{2,1,0:T(8,128)S(1)}, f32[2,16,128]{2,1,0:T(8,128)S(1)}, u32[]{:S(2)}, u32[]{:S(2)}) %collective-permute-start.19) | collective-permute-done | bytes 16416 | tf_op jit(solution)/shard_map/ppermute | solution.py:453
  70.0 1.1 %collective-permute-start.20 = (f32[16,128]{1,0:T(8,128)S(1)}, f32[16,128]{1,0:T(8,128)S(1)}, u32[]{:S(2)}, u32[]{:S(2)}) collective-permute-start(f32[16,128]{1,0:T(8,128)S(1)} %slice_bitcast_fusion), channel_id=1, source_target_pairs={{0,4},{2,6},{4,0},{6,2},{8,12},{10,14},{12,8},{14,10},{16,20},{18,... | collective-permute-start | bytes 24584 | tf_op jit(solution)/shard_map/ppermute | solution.py:592
  71.1 5.3 %bulk.4 = (f32[3,512,128]{2,1,0:T(8,128)}, f32[3,512,128]{2,1,0:T(8,128)}) custom-call(s32[2]{0:T(128)S(1)} %get-tuple-element.29.where_ref, f32[16,128]{1,0:T(8,128)S(1)} %dynamic-slice_bitcast_fusion.table, f32[8,608,128]{2,1,0:T(8,128)S(1)} %get-tuple-element.32.ext, f32[304,128]{1,0:T(8,128)S(1)} %collective-permute-done.2.pack, ...), custom_call_target="tpu_custom_call" | custom-call | bytes 12000000 | tf_op jit(solution)/shard_map/bulk/pallas_call | solution.py:571
  76.5 5.3 %bulk.5 = (f32[3,512,128]{2,1,0:T(8,128)}, f32[3,512,128]{2,1,0:T(8,128)}) custom-call(s32[2]{0:T(128)S(1)} %get-tuple-element.29.where_ref, f32[16,128]{1,0:T(8,128)S(1)} %dynamic-slice_bitcast_fusion.table, f32[8,608,128]{2,1,0:T(8,128)S(1)} %get-tuple-element.32.ext, ...), custom_call_target="tpu_custom_call", output_to_operand_aliasing={{0}: (5, {}), {1}: (6, {})} | custom-call | bytes 12000000 | tf_op jit(solution)/shard_map/bulk/pallas_call | solution.py:571
  81.8 5.3 %bulk.6 = (f32[3,512,128]{2,1,0:T(8,128)}, f32[3,512,128]{2,1,0:T(8,128)}) custom-call(s32[2]{0:T(128)S(1)} %get-tuple-element.29.where_ref, f32[16,128]{1,0:T(8,128)S(1)} %dynamic-slice_bitcast_fusion.table, f32[8,608,128]{2,1,0:T(8,128)S(1)} %get-tuple-element.32.ext, ...), custom_call_target="tpu_custom_call", output_to_operand_aliasing={{0}: (5, {}), {1}: (6, {})} | custom-call | bytes 12000000 | tf_op jit(solution)/shard_map/bulk/pallas_call | solution.py:571
  87.2 5.3 %bulk.7 = (f32[3,512,128]{2,1,0:T(8,128)}, f32[3,512,128]{2,1,0:T(8,128)}) custom-call(s32[2]{0:T(128)S(1)} %get-tuple-element.29.where_ref, f32[16,128]{1,0:T(8,128)S(1)} %dynamic-slice_bitcast_fusion.table, f32[8,608,128]{2,1,0:T(8,128)S(1)} %get-tuple-element.32.ext, ...), custom_call_target="tpu_custom_call", output_to_operand_aliasing={{0}: (5, {}), {1}: (6, {})} | custom-call | bytes 12000000 | tf_op jit(solution)/shard_map/bulk/pallas_call | solution.py:571
  (58 shorter events, 11.3 us)
Async XLA Ops:
  1.5 1.1 %copy-start = (f32[3,512,128]{2,1,0:T(8,128)S(1)}, f32[3,512,128]{2,1,0:T(8,128)}, u32[]{:S(2)}) copy-start(f32[3,512,128]{2,1,0:T(8,128)} %disp.3) | copy-start | bytes 2359300
  2.6 1.1 %copy-start.2 = (f32[3,512,128]{2,1,0:T(8,128)S(1)}, f32[3,512,128]{2,1,0:T(8,128)}, u32[]{:S(2)}) copy-start(f32[3,512,128]{2,1,0:T(8,128)} %vel.3) | copy-start | bytes 2359300
  3.7 0.9 %copy-start.4 = (f32[512,128]{1,0:T(8,128)S(1)}, f32[512,128]{1,0:T(8,128)}, u32[]{:S(2)}) copy-start(f32[512,128]{1,0:T(8,128)} %mass.3) | copy-start | bytes 786436
  4.7 0.9 %copy-start.6 = (f32[512,128]{1,0:T(8,128)S(1)}, f32[512,128]{1,0:T(8,128)}, u32[]{:S(2)}) copy-start(f32[512,128]{1,0:T(8,128)} %stiff.3) | copy-start | bytes 786436
  5.6 0.7 copy-start.9
  8.9 30.6 %copy-start.1 = (f32[3,512,128]{2,1,0:T(8,128)S(1)}, f32[3,512,128]{2,1,0:T(8,128)}, u32[]{:S(2)}) copy-start(f32[3,512,128]{2,1,0:T(8,128)} %disp.3) | copy-start | bytes 2359300
  8.9 30.6 %copy-start.3 = (f32[3,512,128]{2,1,0:T(8,128)S(1)}, f32[3,512,128]{2,1,0:T(8,128)}, u32[]{:S(2)}) copy-start(f32[3,512,128]{2,1,0:T(8,128)} %vel.3) | copy-start | bytes 2359300
  8.9 30.6 %copy-start.5 = (f32[512,128]{1,0:T(8,128)S(1)}, f32[512,128]{1,0:T(8,128)}, u32[]{:S(2)}) copy-start(f32[512,128]{1,0:T(8,128)} %mass.3) | copy-start | bytes 786436
  8.9 30.6 %copy-start.7 = (f32[512,128]{1,0:T(8,128)S(1)}, f32[512,128]{1,0:T(8,128)}, u32[]{:S(2)}) copy-start(f32[512,128]{1,0:T(8,128)} %stiff.3) | copy-start | bytes 786436
  8.9 40.8 %copy-start.14 = (f32[2,16,128]{2,1,0:T(8,128)S(1)}, f32[2,16,128]{2,1,0:T(8,128)}, u32[]{:S(2)}) copy-start(f32[2,16,128]{2,1,0:T(8,128)} %constant.19.clone) | copy-start | bytes 49156
  12.9 26.6 %collective-permute-start = (f32[8,48,128]{2,1,0:T(8,128)S(1)}, f32[8,48,128]{2,1,0:T(8,128)S(1)}, u32[]{:S(2)}, u32[]{:S(2)}) collective-permute-start(f32[8,48,128]{2,1,0:T(8,128)S(1)} %get-tuple-element.30), channel_id=1, source_target_pairs={{0,2},{2,4},{4,6},{6,8},{8,10},{10,12},{12,14},{14,16},{16,18},{18... | collective-permute-start | bytes 589832 | tf_op jit(solution)/shard_map/ppermute | solution.py:517
  14.2 25.3 %collective-permute-start.1 = (f32[8,48,128]{2,1,0:T(8,128)S(1)}, f32[8,48,128]{2,1,0:T(8,128)S(1)}, u32[]{:S(2)}, u32[]{:S(2)}) collective-permute-start(f32[8,48,128]{2,1,0:T(8,128)S(1)} %get-tuple-element.31), channel_id=1, source_target_pairs={{2,0},{4,2},{6,4},{8,6},{10,8},{12,10},{14,12},{16,14},{18,16},{20... | collective-permute-start | bytes 589832 | tf_op jit(solution)/shard_map/ppermute | solution.py:518
  15.5 10.7 %collective-permute-start.5 = (f32[16,128]{1,0:T(8,128)}, f32[16,128]{1,0:T(8,128)S(1)}, u32[]{:S(2)}, u32[]{:S(2)}) collective-permute-start(f32[16,128]{1,0:T(8,128)} %bitcast.16), channel_id=1, source_target_pairs={{0,96},{2,98},{4,100},{6,102},{8,104},{10,106},{12,108},{14,110},{... | collective-permute-start | bytes 24584 | tf_op jit(solution)/shard_map/ppermute | solution.py:441
  24.6 5.4 %collective-permute-start.4 = (f32[16,128]{1,0:T(8,128)}, f32[16,128]{1,0:T(8,128)S(1)}, u32[]{:S(2)}, u32[]{:S(2)}) collective-permute-start(f32[16,128]{1,0:T(8,128)} %bitcast.17), channel_id=1, source_target_pairs={{0,64},{2,66},{4,68},{6,70},{8,72},{10,74},{12,76},{14,78},{16,80}... | collective-permute-start | bytes 24584 | tf_op jit(solution)/shard_map/ppermute | solution.py:441
  25.3 5.1 %collective-permute-start.3 = (f32[16,128]{1,0:T(8,128)}, f32[16,128]{1,0:T(8,128)S(1)}, u32[]{:S(2)}, u32[]{:S(2)}) collective-permute-start(f32[16,128]{1,0:T(8,128)} %bitcast.18), channel_id=1, source_target_pairs={{0,32},{2,34},{4,36},{6,38},{8,40},{10,42},{12,44},{14,46},{16,48}... | collective-permute-start | bytes 24584 | tf_op jit(solution)/shard_map/ppermute | solution.py:441
  31.0 1.2 %collective-permute-start.6 = (f32[4,16,128]{2,1,0:T(8,128)S(1)}, f32[4,16,128]{2,1,0:T(8,128)S(1)}, u32[]{:S(2)}, u32[]{:S(2)}) collective-permute-start(f32[4,16,128]{2,1,0:T(8,128)S(1)} %pad_maximum_fusion.held), channel_id=1, source_target_pairs={{0,2},{2,0},{4,6},{6,4},{8,10},{10,8},{12,14},{14,12},{16,18},{18,... | collective-permute-start | bytes 98312 | tf_op jit(solution)/shard_map/ppermute | solution.py:443
  32.3 5.0 %collective-permute-start.7 = (f32[2,16,128]{2,1,0:T(8,128)S(1)}, f32[2,16,128]{2,1,0:T(8,128)S(1)}, u32[]{:S(2)}, u32[]{:S(2)}) collective-permute-start(f32[2,16,128]{2,1,0:T(8,128)S(1)} %get-tuple-element.38), channel_id=1, source_target_pairs={{0,8},{2,10},{4,12},{6,14},{8,16},{10,18},{12,20},{14,22},{16,24},... | collective-permute-start | bytes 49160 | tf_op jit(solution)/shard_map/ppermute | solution.py:453
  32.4 5.3 %collective-permute-start.8 = (f32[2,16,128]{2,1,0:T(8,128)S(1)}, f32[2,16,128]{2,1,0:T(8,128)S(1)}, u32[]{:S(2)}, u32[]{:S(2)}) collective-permute-start(f32[2,16,128]{2,1,0:T(8,128)S(1)} %get-tuple-element.39), channel_id=1, source_target_pairs={{0,16},{2,18},{4,20},{6,22},{8,24},{10,26},{12,28},{14,30},{16,0},... | collective-permute-start | bytes 49160 | tf_op jit(solution)/shard_map/ppermute | solution.py:453
  35.8 3.7 %collective-permute-start.9 = (f32[2,16,128]{2,1,0:T(8,128)S(1)}, f32[2,16,128]{2,1,0:T(8,128)S(1)}, u32[]{:S(2)}, u32[]{:S(2)}) collective-permute-start(f32[2,16,128]{2,1,0:T(8,128)S(1)} %get-tuple-element.40), channel_id=1, source_target_pairs={{0,24},{2,26},{4,28},{6,30},{8,0},{10,2},{12,4},{14,6},{16,8},{18,... | collective-permute-start | bytes 49160 | tf_op jit(solution)/shard_map/ppermute | solution.py:453
  41.9 9.5 %collective-permute-start.2 = (f32[304,128]{1,0:T(8,128)S(1)}, f32[304,128]{1,0:T(8,128)S(1)}, u32[]{:S(2)}, u32[]{:S(2)}) collective-permute-start(f32[304,128]{1,0:T(8,128)S(1)} %get-tuple-element.33), channel_id=1, source_target_pairs={{0,1},{1,0},{2,3},{3,2},{4,5},{5,4},{6,7},{7,6},{8,9},{9,8},{10,11... | collective-permute-start | bytes 466952 | tf_op jit(solution)/shard_map/ppermute | solution.py:537
  45.1 6.4 %collective-permute-start.12 = (f32[16,128]{1,0:T(8,128)S(1)}, f32[16,128]{1,0:T(8,128)S(1)}, u32[]{:S(2)}, u32[]{:S(2)}) collective-permute-start(f32[16,128]{1,0:T(8,128)S(1)} %get-tuple-element.56), channel_id=1, source_target_pairs={{0,5},{1,4},{2,7},{3,6},{4,1},{5,0},{6,3},{7,2},{8,13},{9,12},{10,... | collective-permute-start | bytes 24584 | tf_op jit(solution)/shard_map/ppermute | solution.py:526
  45.3 6.2 %collective-permute-start.10 = (f32[16,128]{1,0:T(8,128)S(1)}, f32[16,128]{1,0:T(8,128)S(1)}, u32[]{:S(2)}, u32[]{:S(2)}) collective-permute-start(f32[16,128]{1,0:T(8,128)S(1)} %get-tuple-element.56), channel_id=1, source_target_pairs={{0,4},{2,6},{4,0},{6,2},{8,12},{10,14},{12,8},{14,10},{16,20},{18,... | collective-permute-start | bytes 24584 | tf_op jit(solution)/shard_map/ppermute | solution.py:524
  45.5 5.9 %collective-permute-start.11 = (f32[16,128]{1,0:T(8,128)S(1)}, f32[16,128]{1,0:T(8,128)S(1)}, u32[]{:S(2)}, u32[]{:S(2)}) collective-permute-start(f32[16,128]{1,0:T(8,128)S(1)} %get-tuple-element.55), channel_id=1, source_target_pairs={{0,1},{1,0},{2,3},{3,2},{4,5},{5,4},{6,7},{7,6},{8,9},{9,8},{10,11... | collective-permute-start | bytes 24584 | tf_op jit(solution)/shard_map/ppermute | solution.py:525
  54.5 3.7 %collective-permute-start.15 = (f32[16,128]{1,0:T(8,128)S(1)}, f32[16,128]{1,0:T(8,128)S(1)}, u32[]{:S(2)}, u32[]{:S(2)}) collective-permute-start(f32[16,128]{1,0:T(8,128)S(1)} %get-tuple-element.50), channel_id=1, source_target_pairs={{0,96},{2,98},{4,100},{6,102},{8,104},{10,106},{12,108},{14,110},{... | collective-permute-start | bytes 24584 | tf_op jit(solution)/shard_map/ppermute | solution.py:441
  55.0 5.2 %collective-permute-start.14 = (f32[16,128]{1,0:T(8,128)S(1)}, f32[16,128]{1,0:T(8,128)S(1)}, u32[]{:S(2)}, u32[]{:S(2)}) collective-permute-start(f32[16,128]{1,0:T(8,128)S(1)} %get-tuple-element.50), channel_id=1, source_target_pairs={{0,64},{2,66},{4,68},{6,70},{8,72},{10,74},{12,76},{14,78},{16,80}... | collective-permute-start | bytes 24584 | tf_op jit(solution)/shard_map/ppermute | solution.py:441
  56.3 4.9 %collective-permute-start.13 = (f32[16,128]{1,0:T(8,128)S(1)}, f32[16,128]{1,0:T(8,128)S(1)}, u32[]{:S(2)}, u32[]{:S(2)}) collective-permute-start(f32[16,128]{1,0:T(8,128)S(1)} %get-tuple-element.50), channel_id=1, source_target_pairs={{0,32},{2,34},{4,36},{6,38},{8,40},{10,42},{12,44},{14,46},{16,48}... | collective-permute-start | bytes 24584 | tf_op jit(solution)/shard_map/ppermute | solution.py:441
  61.2 1.2 %collective-permute-start.16 = (f32[4,16,128]{2,1,0:T(8,128)S(1)}, f32[4,16,128]{2,1,0:T(8,128)S(1)}, u32[]{:S(2)}, u32[]{:S(2)}) collective-permute-start(f32[4,16,128]{2,1,0:T(8,128)S(1)} %pad_maximum_fusion.1.held), channel_id=1, source_target_pairs={{0,2},{2,0},{4,6},{6,4},{8,10},{10,8},{12,14},{14,12},{16,18},{18,... | collective-permute-start | bytes 98312 | tf_op jit(solution)/shard_map/ppermute | solution.py:443
  62.5 5.2 %collective-permute-start.17 = (f32[2,16,128]{2,1,0:T(8,128)S(1)}, f32[2,16,128]{2,1,0:T(8,128)S(1)}, u32[]{:S(2)}, u32[]{:S(2)}) collective-permute-start(f32[2,16,128]{2,1,0:T(8,128)S(1)} %get-tuple-element.52), channel_id=1, source_target_pairs={{0,8},{2,10},{4,12},{6,14},{8,16},{10,18},{12,20},{14,22},{16,24},... | collective-permute-start | bytes 49160 | tf_op jit(solution)/shard_map/ppermute | solution.py:453
  63.3 5.2 %collective-permute-start.18 = (f32[2,16,128]{2,1,0:T(8,128)S(1)}, f32[2,16,128]{2,1,0:T(8,128)S(1)}, u32[]{:S(2)}, u32[]{:S(2)}) collective-permute-start(f32[2,16,128]{2,1,0:T(8,128)S(1)} %get-tuple-element.53), channel_id=1, source_target_pairs={{0,16},{2,18},{4,20},{6,22},{8,24},{10,26},{12,28},{14,30},{16,0},... | collective-permute-start | bytes 49160 | tf_op jit(solution)/shard_map/ppermute | solution.py:453
  66.3 3.7 %collective-permute-start.19 = (f32[2,16,128]{2,1,0:T(8,128)S(1)}, f32[2,16,128]{2,1,0:T(8,128)S(1)}, u32[]{:S(2)}, u32[]{:S(2)}) collective-permute-start(f32[2,16,128]{2,1,0:T(8,128)S(1)} %get-tuple-element.54), channel_id=1, source_target_pairs={{0,24},{2,26},{4,28},{6,30},{8,0},{10,2},{12,4},{14,6},{16,8},{18,... | collective-permute-start | bytes 49160 | tf_op jit(solution)/shard_map/ppermute | solution.py:453
  70.0 22.5 %collective-permute-start.20 = (f32[16,128]{1,0:T(8,128)S(1)}, f32[16,128]{1,0:T(8,128)S(1)}, u32[]{:S(2)}, u32[]{:S(2)}) collective-permute-start(f32[16,128]{1,0:T(8,128)S(1)} %slice_bitcast_fusion), channel_id=1, source_target_pairs={{0,4},{2,6},{4,0},{6,2},{8,12},{10,14},{12,8},{14,10},{16,20},{18,... | collective-permute-start | bytes 24584 | tf_op jit(solution)/shard_map/ppermute | solution.py:592
  87.2 5.4 %copy-start.8 = (f32[1,16,128]{2,1,0:T(8,128)S(1)}, f32[1,16,128]{2,1,0:T(8,128)}, u32[]{:S(2)}) copy-start(f32[1,16,128]{2,1,0:T(8,128)} %before.1) | copy-start | bytes 24580
  (4 other events, 2.6 us)

commit v3 on v2

v3 whole, which is shorter than its diff:
```python
import functools
import math

import jax
import jax.numpy as jnp
import numpy as np
from jax import lax
from jax.experimental import pallas as pl
from jax.experimental.pallas import tpu as pltpu
from jax.sharding import PartitionSpec as P

STEPS = 4
REACH = 20
TIME_STEP = 0.1
GRAVITY = 0.2
CONTACT_STIFF = 2.0
CRADLE_CURVE = 0.5
PAD_RATE = 0.2
PAD_STIFF = 1.0

LANES = 128
EDGE = 4
HALO = 48
WIN = 64
CHUNKS = 4
GROUP = 11
PARTS = 3
LOAD_GROUP = 4
LIMIT = 40 * 1024 * 1024
MOST = 60 * 1024 * 1024


def arc_digits(index):
    return (index >> 4, (index >> 2) & 3, (index >> 1) & 1, index & 1)


def arc_index(y, z, x, c):
    return (y << 4) + (z << 2) + (x << 1) + c


def flips(y=0, z=0, x=0, c=0):
    out = []
    for i in range(64):
        iy, iz, ix, ic = arc_digits(i)
        out.append((i, arc_index(iy ^ y, iz ^ z, ix ^ x, ic ^ c)))
    return out


def column_table(circ_total):
    step = 2.0 * math.pi / circ_total
    chord = 2.0 * math.sin(step / 2.0)
    length = math.sqrt(step * step + chord * chord)
    rows = []
    for half in range(2):
        cols = (half * LANES + np.arange(2 * LANES)) % circ_total
        phase = step * (cols + 0.5)
        before = step * (cols - 0.5)
        theta = step * cols
        parts = [
            chord / length * np.cos(phase),
            chord / length * np.sin(phase),
            chord / length * np.cos(before),
            chord / length * np.sin(before),
            np.sin(theta),
            np.cos(theta),
            np.zeros_like(theta),
            np.zeros_like(theta),
        ]
        rows.append(np.concatenate([p.reshape(2, LANES) for p in parts], axis=0))
    axial = step / length
    hoop_gain = 1.0 / (chord / length) ** 2
    return np.stack(rows).astype(np.float32), axial, hoop_gain


def edge_kernel(halo, disp, vel, mass, stiff, field, inner, outer, sems):
    own = disp.shape[1]
    odd = lax.axis_index("arc") & 1
    copies = [
        pltpu.make_async_copy(disp, field.at[0:3], sems.at[8]),
        pltpu.make_async_copy(vel, field.at[3:6], sems.at[9]),
        pltpu.make_async_copy(mass, field.at[6], sems.at[10]),
        pltpu.make_async_copy(stiff, field.at[7], sems.at[11]),
    ]
    for n, (edge, at) in enumerate(((inner, (1 - odd) * (own - halo)), (outer, odd * (own - halo)))):
        span = pl.ds(pl.multiple_of(at, 8), halo)
        copies += [
            pltpu.make_async_copy(disp.at[:, span, :], edge.at[0:3], sems.at[4 * n]),
            pltpu.make_async_copy(vel.at[:, span, :], edge.at[3:6], sems.at[4 * n + 1]),
            pltpu.make_async_copy(mass.at[span, :], edge.at[6], sems.at[4 * n + 2]),
            pltpu.make_async_copy(stiff.at[span, :], edge.at[7], sems.at[4 * n + 3]),
        ]
    for copy in copies:
        copy.start()
    for copy in copies:
        copy.wait()


KEEP, SEND, FROM_Z, FAR_Z, SAME_X, USED, PLAN = 0, 4, 8, 12, 14, 15, 16


def plan_kernel(
    arc_count, own, slot_ref, lift_ref, rows_ref, static_ref, plan, where_ref, list_ref, lift_out, source
):
    me = lax.axis_index("arc")
    y, z, x, c = arc_digits(me)
    rollers = slot_ref.shape[0]
    roll = static_ref[me]
    begin = static_ref[arc_count + me]
    valid = roll >= 0
    safe = jnp.maximum(roll, 0)
    where_ref[0] = begin
    where_ref[1] = jnp.where(valid, begin, -4 * WIN)
    lift_out[0] = jnp.where(valid, lift_ref[safe], -1e9)
    offset = me * own - HALO + begin
    for step in range(STEPS):
        g = rows_ref[step, pl.ds(safe, 1), :] - offset
        list_ref[step : step + 1, :] = jnp.clip(g, 0, WIN - 1)
    for i in range(source.shape[0]):
        source[i] = -1
    for r in range(rollers):
        source[slot_ref[r]] = static_ref[2 * arc_count + r]

    def line(row, value):
        plan[row : row + 1, :] = jnp.full((1, LANES), value, jnp.int32)

    def index(need):
        ny, _, _, nc = arc_digits(need)
        step = jnp.where((ny >> 1) == (y >> 1), ny ^ y, 2 + (ny ^ y ^ 3))
        return 2 * step + (nc ^ c)

    for way in range(2):
        at = PLAN * way
        for zi in range(4):
            for xr in range(2):
                dest = arc_index(y, z ^ (0, 3, 1, 2)[zi], x ^ xr, c)
                if way == 0:
                    need = slot_ref[jnp.maximum(static_ref[dest], 0)]
                else:
                    need = jnp.maximum(source[dest], 0)
                n = 2 * zi + xr
                line(at + KEEP + n, index(need))
                _, nz, nx, _ = arc_digits(need)
                if n < 4:
                    line(at + FROM_Z + n, (nz == (z ^ 1)).astype(jnp.int32))
                if n < 2:
                    line(at + FAR_Z + n, ((nz != z) & (nz != (z ^ 1))).astype(jnp.int32))
                if n < 1:
                    line(at + SAME_X, (nx == x).astype(jnp.int32))
        line(at + USED, (source[me] >= 0).astype(jnp.int32))


def row_block(field, inner, outer, odd, a, row):
    halo = inner.shape[1]
    own = field.shape[1]
    if row < halo:
        span = slice(row, row + 8)
        return jnp.where(odd, inner[a, span, :], outer[a, span, :])
    if row < halo + own:
        return field[a, row - halo : row - halo + 8, :]
    span = slice(row - halo - own, row - halo - own + 8)
    return jnp.where(odd, outer[a, span, :], inner[a, span, :])


def pack_kernel(field, inner, outer, pack):
    half = field.shape[1] // 2 + inner.shape[1]
    odd = (lax.axis_index("arc") & 1) > 0
    lane = lax.broadcasted_iota(jnp.int32, (8, LANES), 1) // (2 * EDGE)
    for r in range(0, half, 8):
        packed = jnp.zeros((8, LANES), jnp.float32)
        for part in range(2):
            for a in range(8):
                value = row_block(field, inner, outer, odd, a, r + part * half)
                moved = pltpu.roll(value, (8 * a + EDGE + 64 * part) % LANES, 1)
                packed = jnp.where(lane == a + 8 * part, moved, packed)
        pack[r : r + 8, :] = packed


def ring_left(tiles, last):
    a, b = (pltpu.roll(t, LANES - 1, 1) for t in tiles)
    return jnp.where(last, b, a), jnp.where(last, a, b)


def ring_right(tiles, first):
    a, b = (pltpu.roll(t, 1, 1) for t in tiles)
    return jnp.where(first, b, a), jnp.where(first, a, b)


def unpack_block(pack, row, half, a, keep):
    upper = row >= half
    at = pl.multiple_of(jnp.where(upper, row - half, row), 8)
    shift = jnp.where(upper, (2 * LANES - 8 * a - EDGE - 64) % LANES, (2 * LANES - 8 * a - EDGE) % LANES)
    return jnp.where(keep, pltpu.roll(pack[pl.ds(at, 8), :], shift, 1), 0.0)


def clear_tail(state, rows):
    for a in range(3):
        for t in range(2):
            state[a, t, rows : rows + 8, :] = jnp.zeros((8, LANES), jnp.float32)


def load_state(group, source, pack, first_row, base, cycle_total, rows, half, state, vels, coef, ends=False):
    lane = lax.broadcasted_iota(jnp.int32, (8, LANES), 1)
    sub = lax.broadcasted_iota(jnp.int32, (8, LANES), 0)
    keep = (lane < EDGE) | (lane >= LANES - EDGE)
    first = lane == 0
    top = sub == 0

    def body(b, carry):
        r = 8 * b if isinstance(b, int) else pl.multiple_of(b * 8, 8)
        e = first_row + r
        span = pl.ds(r, 8)
        for a in range(3):
            state[a, 0, span, :] = source(a, r)
            state[a, 1, span, :] = unpack_block(pack, e, half, a, keep)
            vels[a, 0, span, :] = TIME_STEP * source(3 + a, r)
            vels[a, 1, span, :] = TIME_STEP * unpack_block(pack, e, half, 3 + a, keep)
        for t, m in enumerate((source(6, r), unpack_block(pack, e, half, 6, keep))):
            coef[0, t, span, :] = (TIME_STEP * TIME_STEP) / jnp.where(m > 0.0, m, 1.0)
        ids = base + e + sub
        inside = (ids >= 0) & (ids < cycle_total - 1)
        k = [
            jnp.where(inside, v, 0.0)
            for v in (source(7, r), unpack_block(pack, e, half, 7, keep))
        ]
        kr = ring_right(k, first)
        new = []
        for t in range(2):
            down = pltpu.roll(k[t], 1, 0)
            coef[1, t, span, :] = k[t]
            coef[2, t, span, :] = 0.5 * (k[t] + kr[t])
            coef[3, t, span, :] = (0.5 * HOOP_GAIN) * (k[t] + jnp.where(top, carry[t], down))
            new.append(down)
        return tuple(new)

    zero = jnp.zeros((8, LANES), jnp.float32)

    def several(b, carry):
        for u in range(group):
            carry = body(b * group + u + int(ends), carry)
        return carry

    carry = (zero, zero)
    if ends:
        carry = body(0, carry)
    carry = lax.fori_loop(0, (rows // 8 - 2 * int(ends)) // group, several, carry)
    if ends:
        body(rows // 8 - 1, carry)
    clear_tail(state, rows)


TABLE, AXIAL, HOOP_GAIN = column_table(2 * LANES)


def advance(table, rows, state, vels, coef, later, vels_later, group, push=None, span_of=None):
    lane = lax.broadcasted_iota(jnp.int32, (8, LANES), 1)
    top = lax.broadcasted_iota(jnp.int32, (8, LANES), 0) == 0
    first, last = lane == 0, lane == LANES - 1

    def const(i):
        return [jnp.broadcast_to(table[2 * i + t : 2 * i + t + 1, :], (8, LANES)) for t in range(2)]

    cj, sj, cb, sb = (const(i) for i in range(4))
    two = range(2)

    def block(r, carry, store=True):
        span, below = pl.ds(r, 8), pl.ds(r + 1, 8)
        x, y, z = ([state[a, t, span, :] for t in two] for a in range(3))
        xn, yn, zn = ([state[a, t, below, :] for t in two] for a in range(3))
        p = [cj[t] * y[t] + sj[t] * z[t] for t in two]
        q = [cb[t] * y[t] + sb[t] * z[t] for t in two]
        ax = [AXIAL * x[t] for t in two]
        pn = [cj[t] * yn[t] + sj[t] * zn[t] for t in two]
        qn = [cb[t] * yn[t] + sb[t] * zn[t] for t in two]
        axn = [AXIAL * xn[t] for t in two]
        q_next = ring_left(q, last)
        anti_next = ring_left([q[t] - ax[t] for t in two], last)
        diag_next = ring_left([qn[t] + axn[t] for t in two], last)
        k = [coef[1, t, span, :] for t in two]
        t_d = [k[t] * (diag_next[t] - (p[t] + ax[t])) for t in two]
        t_a = [k[t] * (anti_next[t] - (pn[t] - axn[t])) for t in two]
        t_h = [coef[3, t, span, :] * (q_next[t] - p[t]) for t in two]
        fx = [coef[2, t, span, :] * (xn[t] - x[t]) for t in two]
        d_left = ring_right(t_d, first)
        a_left = ring_right(t_a, first)
        g_left = ring_right([t_a[t] + t_h[t] for t in two], first)
        new = []
        for t in two:
            up = t_d[t] + t_h[t]
            force = [
                fx[t] + AXIAL * (t_d[t] + a_left[t]),
                cj[t] * up - cb[t] * g_left[t],
                sj[t] * up - sb[t] * g_left[t],
            ]
            low = [
                fx[t] + AXIAL * (d_left[t] + t_a[t]),
                cb[t] * d_left[t] - cj[t] * t_a[t],
                sb[t] * d_left[t] - sj[t] * t_a[t],
            ]
            at = (x[t], y[t], z[t])
            inverse = coef[0, t, span, :]
            for a in range(3):
                moved = pltpu.roll(low[a], 1, 0)
                total = force[a] - jnp.where(top, carry[3 * t + a], moved)
                new.append(moved)
                if not store:
                    continue
                if push is not None and a > 0:
                    total = total + push[a - 1, t, span, :]
                w = vels[a, t, span, :] + inverse * total
                if a == 2:
                    w = w - (GRAVITY * TIME_STEP * TIME_STEP)
                vels_later[a, t, span, :] = w
                later[a, t, span, :] = at[a] + w
        return tuple(new)

    def body(b, carry):
        for u in range(group):
            carry = block(pl.multiple_of(b * (8 * group), 8) + 8 * u, carry)
        return carry

    zero = jnp.zeros((8, LANES), jnp.float32)
    carry = (zero,) * 6
    begin, end = span_of or (0, rows)
    if begin > 0:
        carry = block(begin - 8, carry, store=False)
    if group * 8 == rows:
        for u in range(group):
            carry = block(8 * u, carry)
    else:
        lax.fori_loop(begin // (8 * group), end // (8 * group), body, carry)


def pad_edge_kernel(pad, out):
    lane = lax.broadcasted_iota(jnp.int32, (1, LANES), 1) // (2 * EDGE)
    total = jnp.zeros((1, LANES), jnp.float32)
    slots = pad.shape[1]
    for m in range(slots):
        moved = pltpu.roll(pad[0, m : m + 1, :], LANES - EDGE - 2 * EDGE * m, 1)
        total = jnp.where(lane == slots - 1 - m, moved, total)
    out[...] = jnp.broadcast_to(total, out.shape)


def pad_extend_kernel(pad, edges, *rest):
    out = rest[-1]
    slots = pad.shape[1]
    out[0, :slots, :] = pad[0]
    out[0, slots:, :] = edges[...]


def window_load_kernel(half, base, cycle_total, where_ref, field, inner, outer, columns, state, vels, coef):
    start = pl.multiple_of(where_ref[0], 8)
    halo = inner.shape[1]
    own = field.shape[1]
    odd = (lax.axis_index("arc") & 1) > 0

    def source(a, r):
        row = start + r
        mid = field[a, pl.ds(pl.multiple_of(jnp.clip(row - halo, 0, own - 8), 8), 8), :]
        before = row < halo
        at = jnp.where(before, row, jnp.maximum(row - halo - own, 0))
        span = pl.ds(pl.multiple_of(at, 8), 8)
        end = jnp.where(odd == before, inner[a, span, :], outer[a, span, :])
        return jnp.where(before | (row >= halo + own), end, mid)

    first_id = base(lax.axis_index("arc"))
    load_state(4, source, columns, start, first_id, cycle_total, WIN, half, state, vels, coef)


def contact(table, lift, list_ref, step, state, push, taken, given, held):
    slots = held.shape[1]
    push[...] = jnp.zeros_like(push)
    for m in range(slots):
        g = list_ref[step, m]
        for a in range(2):
            for t in range(2):
                taken[a, t, m : m + 1, :] = state[a + 1, t, pl.ds(g, 1), :]
    for t in range(2):
        sin_angle, cos_angle = table[8 + t : 9 + t, :], table[10 + t : 11 + t, :]
        lateral = sin_angle + taken[0, t]
        q = held[t]
        intrusion = lift + CRADLE_CURVE * lateral * lateral - (1.0 - cos_angle) - taken[1, t] - q
        load = CONTACT_STIFF * jnp.maximum(intrusion, 0.0)
        normal = load / jnp.sqrt(1.0 + 4.0 * CRADLE_CURVE * CRADLE_CURVE * lateral * lateral)
        given[0, t] = -2.0 * CRADLE_CURVE * lateral * normal
        given[1, t] = normal
        held[t] = q + PAD_RATE * (load - PAD_STIFF * q)
    for m in range(slots):
        g = list_ref[step, m]
        for a in range(2):
            for t in range(2):
                push[a, t, pl.ds(g, 1), :] += given[a, t, m : m + 1, :]


def window_kernel(
    list_ref, lift_ref, plan, table, state, vels, coef, pads, handed, *rest
):
    state_out, vels_out, push, pad_out, spare, vels_spare, taken, given, held = rest[-9:]
    same = plan[SAME_X : SAME_X + 1, :] > 0
    slots = held.shape[1]
    lane = lax.broadcasted_iota(jnp.int32, (8, LANES), 1)
    keep = (lane < EDGE) | (lane >= LANES - EDGE)
    both = jnp.where(same, pads[0], handed[0])
    held[0] = both[:slots]
    for part in range(2):
        moved = pltpu.roll(both[slots:], EDGE + 64 * part, 1, stride=2 * EDGE, stride_axis=0)
        held[1, 8 * part : 8 * part + 8, :] = jnp.where(keep, moved, 0.0)
    lift = lift_ref[0]
    clear_tail(spare, WIN)
    clear_tail(state_out, WIN)
    now = (state, vels)
    for step in range(STEPS):
        contact(table, lift, list_ref, step, now[0], push, taken, given, held)
        if step < STEPS - 1:
            later = (spare, vels_spare) if (STEPS - step) % 2 else (state_out, vels_out)
            advance(table, WIN, *now, coef, *later, WIN // 8, push)
            now = later
    pad_out[0] = held[0]


def window_last_kernel(table, state, vels, coef, push, result, later, vels_later):
    advance(table, WIN, state, vels, coef, later, vels_later, WIN // 8, push)
    for a in range(3):
        result[a] = later[a, 0, :WIN, :]
        result[3 + a] = vels_later[a, 0] * (1.0 / TIME_STEP)


def bulk_load_kernel(half, base, cycle_total, rows, field, inner, outer, columns, state, vels, coef):
    first_row = HALO - 8
    odd = (lax.axis_index("arc") & 1) > 0

    def source(a, r):
        if isinstance(r, int):
            return row_block(field, inner, outer, odd, a, first_row + r)
        return field[a, pl.ds(pl.multiple_of(r - 8, 8), 8), :]

    first_id = base(lax.axis_index("arc"))
    load_state(
        LOAD_GROUP, source, columns, first_row, first_id, cycle_total, rows, half, state, vels, coef, ends=True
    )


def bulk_step_kernel(rows, part, table, state, vels, coef, *rest):
    later, vels_later = rest[-2:]
    third = rows // PARTS
    advance(table, rows, state, vels, coef, later, vels_later, GROUP, span_of=(part * third, (part + 1) * third))
    if part == 0:
        clear_tail(later, rows)


def bulk_store_kernel(rows, where_ref, state, vels, window, *rest):
    disp_out, vel_out, token, result, sems = rest[-5:]
    token[...] = jnp.zeros_like(token)
    count = (rows - 16) // CHUNKS
    start = where_ref[1]
    sub = lax.broadcasted_iota(jnp.int32, (8, LANES), 0)

    def body(b, carry):
        r = pl.multiple_of(b * 8, 8)
        inner = pl.ds(pl.multiple_of(r + 8, 8), 8)
        rel = HALO + r - start
        at = pl.ds(pl.multiple_of(jnp.clip(rel, 0, WIN - 8), 8), 8)
        ids = rel + sub
        use = (ids >= STEPS) & (ids < WIN - STEPS)
        for a in range(3):
            result[a, pl.ds(r, 8), :] = jnp.where(use, window[a, at, :], state[a, 0, inner, :])
            result[3 + a, pl.ds(r, 8), :] = jnp.where(
                use, window[3 + a, at, :], vels[a, 0, inner, :] * (1.0 / TIME_STEP)
            )
        return carry

    copies = []
    for chunk in range(CHUNKS):
        lax.fori_loop(chunk * count // 8, (chunk + 1) * count // 8, body, 0)
        span = pl.ds(chunk * count, count)
        for n, out in enumerate((disp_out, vel_out)):
            copy = pltpu.make_async_copy(
                result.at[3 * n : 3 * n + 3, span, :], out.at[:, span, :], sems.at[2 * chunk + n]
            )
            copy.start()
            copies.append(copy)
    for copy in copies:
        copy.wait()


def stack_kernel(first, second, *rest):
    count = first.shape[0]
    rest[-1][:count] = first[...]
    rest[-1][count:] = second[...]


def pick_kernel(way, plan, first, second, *rest):
    keep, send = rest[-2:]
    parts = [ref[n] for ref in (first, second) for n in range(4)]
    for out, row in ((keep, KEEP), (send, SEND)):
        for n in range(4):
            at = PLAN * way + row + n
            index = plan[at : at + 1, :]
            value = parts[0]
            for m in range(1, 8):
                value = jnp.where(index == m, parts[m], value)
            out[n] = value


def choose_kernel(way, row, plan, kept, got, *rest):
    keep, send = rest[-2:]
    count = got.shape[0]
    for n in range(count):
        at = PLAN * way + row + n
        value = jnp.where(plan[at : at + 1, :] > 0, got[n], kept[n])
        if n < count // 2:
            keep[n] = value
        else:
            send[n - count // 2] = value


def last_kernel(plan, mine, handed, before, *rest):
    out = rest[-1]
    used = plan[PLAN + USED : PLAN + USED + 1, :] > 0
    same = plan[PLAN + SAME_X : PLAN + SAME_X + 1, :] > 0
    out[0] = jnp.where(used, jnp.where(same, mine[0], handed[0]), before[0])


VMEM = pl.BlockSpec(memory_space=pltpu.VMEM)
SMEM = pl.BlockSpec(memory_space=pltpu.SMEM)
ANY = pl.BlockSpec(memory_space=pl.ANY)
HBM = pl.BlockSpec(memory_space=pltpu.HBM)


def real(*shape):
    return jax.ShapeDtypeStruct(shape, jnp.float32)


def whole(*shape):
    return jax.ShapeDtypeStruct(shape, jnp.int32)


def call(kernel, name, outs, ins, in_specs=None, out_specs=None, scratch=(), micros=0.1, after=(), limit=LIMIT, aliases=()):
    single = not isinstance(outs, tuple)
    shapes = (outs,) if single else outs
    result = pl.pallas_call(
        kernel,
        out_shape=shapes,
        in_specs=list(in_specs or [VMEM] * len(ins)) + [ANY] * len(after),
        out_specs=tuple(out_specs or [VMEM] * len(shapes)),
        scratch_shapes=list(scratch),
        compiler_params=pltpu.CompilerParams(vmem_limit_bytes=limit),
        cost_estimate=pl.CostEstimate(flops=0, bytes_accessed=int(micros * 3.6e6), transcendentals=0),
        input_output_aliases=dict(aliases),
        name=name,
    )(*ins, *after)
    return result[0] if single else result


def route(value, plan, way, between):
    shape = value.shape[1:]
    got = lax.ppermute(value, "arc", flips(c=1))
    held = call(stack_kernel, "stack", real(2, *shape), (value, got), after=between(0, value))
    got = lax.ppermute(held, "arc", flips(y=1))
    held = call(stack_kernel, "stack", real(4, *shape), (held, got), after=between(1, held))
    got = lax.ppermute(held, "arc", flips(y=3))
    keep, send = call(
        functools.partial(pick_kernel, way), "pick", (real(4, *shape),) * 2, (plan, held, got), after=between(2, held)
    )
    got = lax.ppermute(send, "arc", flips(z=1))
    keep, send = call(
        functools.partial(choose_kernel, way, FROM_Z), "choose", (real(2, *shape),) * 2, (plan, keep, got),
        after=between(3, send),
    )
    got = lax.ppermute(send, "arc", flips(z=3))
    keep, send = call(
        functools.partial(choose_kernel, way, FAR_Z), "choose", (real(1, *shape),) * 2, (plan, keep, got),
        after=between(4, send),
    )
    return keep, lax.ppermute(send, "arc", flips(x=1)), between(5, send)


def static_tables(arc_count, cycle_dev, roller_total):
    cycle_total = arc_count * cycle_dev
    centres = [r * (cycle_total - 1) // (roller_total - 1) for r in range(roller_total)]
    span = REACH + STEPS - 1
    near = np.full(arc_count, -1, np.int32)
    start = np.zeros(arc_count, np.int32)
    for d in range(arc_count):
        base = d * cycle_dev
        touching = [r for r, c in enumerate(centres) if base - span <= c < base + cycle_dev + span]
        assert len(touching) <= 1
        if touching:
            near[d] = touching[0]
            offset = centres[touching[0]] - base - REACH - STEPS - STEPS + 1 + HALO
            start[d] = offset // 8 * 8
            assert 0 <= start[d] <= cycle_dev + 2 * HALO - WIN
    home = np.array([c // cycle_dev for c in centres], np.int32)
    return near, start, home


def local(displacement, velocity, node_mass, wall_stiff, pad_state, roller_lift, contact_rows, roller_slot):
    cycle_dev = displacement.shape[1]
    slots = pad_state.shape[1]
    roller_total = roller_lift.shape[0]
    arc_count = lax.axis_size("arc")
    cycle_total = cycle_dev * arc_count
    half = cycle_dev // 2 + HALO
    rows = cycle_dev + 16
    fields = (displacement, velocity, node_mass, wall_stiff)
    static = np.concatenate(static_tables(arc_count, cycle_dev, roller_total)).astype(np.int32)
    swap = [(0, 1), (1, 0)]
    table = jnp.asarray(TABLE)[lax.axis_index("circ")]

    def base(me):
        return me * cycle_dev - HALO

    def buffers(count):
        return real(3, 2, count + 8, LANES), real(3, 2, count, LANES), real(4, 2, count, LANES)

    def room(count):
        return [pltpu.VMEM(shape.shape, jnp.float32) for shape in buffers(count)[:2]]

    pad_edges = call(pad_edge_kernel, "pad_edge", real(8, LANES), (pad_state,))
    pad_edges = lax.ppermute(pad_edges, "circ", swap)
    field, inner, outer = call(
        functools.partial(edge_kernel, HALO), "edge",
        (real(8, cycle_dev, LANES), real(8, HALO, LANES), real(8, HALO, LANES)), fields,
        in_specs=[HBM] * 4, scratch=[pltpu.SemaphoreType.DMA((12,))], micros=2.0, limit=MOST,
    )
    plan, where, rows_in, lift = call(
        functools.partial(plan_kernel, arc_count, cycle_dev), "plan",
        (whole(2 * PLAN, LANES), whole(2), whole(STEPS, slots), real(1)),
        (roller_slot, roller_lift, contact_rows, jnp.asarray(static)),
        in_specs=[SMEM, SMEM, VMEM, SMEM], out_specs=[VMEM, SMEM, VMEM, SMEM],
        scratch=[pltpu.SMEM((arc_count,), jnp.int32)], micros=3.0,
    )

    outward = [pair for i in range(1, arc_count, 2) for pair in ((i, (i + 1) % arc_count), ((i + 1) % arc_count, i))]
    token = inner
    inner = lax.ppermute(inner, "arc", flips(c=1))
    outer = lax.ppermute(outer, "arc", outward)
    pack = call(pack_kernel, "pack", real(half, LANES), (field, inner, outer), micros=2.0)
    columns = lax.ppermute(pack, "circ", swap)
    kept = {"done": 0}

    def load_window():
        return call(
            functools.partial(window_load_kernel, half, base, cycle_total), "window_load", buffers(WIN),
            (where, field, inner, outer, columns), in_specs=[SMEM] + [VMEM] * 4, micros=0.8,
        )

    def load_bulk():
        return call(
            functools.partial(bulk_load_kernel, half, base, cycle_total, rows), "bulk_load", buffers(rows),
            (field, inner, outer, columns), micros=2.0,
        )

    def step_bulk(value, count):
        for _ in range(count):
            step, part = divmod(kept["done"], PARTS)
            state, vels, coef = kept["bulk"]
            before = kept["next"] if part else ()
            kept["next"] = call(
                functools.partial(bulk_step_kernel, rows, part), "bulk_step", buffers(rows)[:2],
                (table, state, vels, coef, *before), micros=2.4 / PARTS, after=(value,),
                aliases={4: 0, 5: 1} if part else {},
            )
            kept["done"] += 1
            if part == PARTS - 1:
                kept["bulk"] = (*kept["next"], coef)
        return kept["next"][:1]

    def store_bulk(value):
        state, vels, _ = kept["bulk"]
        outs = call(
            functools.partial(bulk_store_kernel, rows), "bulk_store",
            (real(3, cycle_dev, LANES), real(3, cycle_dev, LANES), real(8, LANES)),
            (where, state, vels, kept["last"], value),
            in_specs=[SMEM] + [VMEM] * 3 + [ANY], out_specs=[HBM] * 2 + [VMEM],
            scratch=[pltpu.VMEM((6, cycle_dev, LANES), jnp.float32), pltpu.SemaphoreType.DMA((2 * CHUNKS,))],
            micros=2.0,
        )
        kept["outs"] = outs[:2]
        return outs[2:]

    def going(stage, value):
        if stage == 1:
            return (pack,)
        if stage == 3:
            kept["window"] = load_window()
            kept["bulk"] = load_bulk()
            return (kept["window"][0], kept["bulk"][0])
        return step_bulk(value, 2) if stage > 3 else ()

    value = call(
        pad_extend_kernel, "pad_extend", real(1, slots + 8, LANES), (pad_state, pad_edges), after=(plan, token)
    )
    pads, handed, done = route(value, plan, 0, going)

    win_state, win_vels, win_coef = kept["window"]
    win_state, win_vels, push, pad_new = call(
        window_kernel, "window", (*buffers(WIN)[:2], real(2, 2, WIN, LANES), real(1, slots, LANES)),
        (rows_in, lift, plan, table, win_state, win_vels, win_coef, pads, handed),
        after=done,
        in_specs=[SMEM] * 2 + [VMEM] * 7,
        scratch=room(WIN)
        + [
            pltpu.VMEM((2, 2, slots, LANES), jnp.float32),
            pltpu.VMEM((2, 2, slots, LANES), jnp.float32),
            pltpu.VMEM((2, slots, LANES), jnp.float32),
        ],
        micros=2.0,
    )

    def coming(stage, value):
        if stage == 0:
            kept["last"] = call(
                window_last_kernel, "window_last", real(6, WIN, LANES), (table, win_state, win_vels, win_coef, push),
                scratch=room(WIN), micros=0.6,
            )
            return (kept["last"],)
        return store_bulk(value) if stage == 5 else step_bulk(value, 2)

    pads, handed, done = route(pad_new, plan, 1, coming)
    pad_result = call(last_kernel, "last", real(1, slots, LANES), (plan, pads, handed, pad_state), after=done)
    return *kept["outs"], pad_result


def solution(mesh):
    placed = (
        P(None, "arc", "circ"),
        P(None, "arc", "circ"),
        P("arc", "circ"),
        P("arc", "circ"),
        P("arc", None, "circ"),
        P(),
        P(),
        P(),
    )
    return jax.shard_map(
        local,
        mesh=mesh,
        in_specs=placed,
        out_specs=(P(None, "arc", "circ"), P(None, "arc", "circ"), P("arc", None, "circ")),
        check_vma=False,
    )
```

time: 93.8 us -> 75.8 us (0.81)
  starting transfers between devices: 34 us -> 14.1 us
  waiting for transfers between devices: 17.9 us -> 35.8 us
  Pallas kernels: 31.4 us -> 23 us
  local copies, waits for them, and re-layouts: 8.31 us -> 1.71 us
    ppermute x21 -> x16, starting transfers between devices: 34 us -> 14.1 us  [the longest x1 7.6 us: local(): outer = lax.ppermute(outer, 'arc', outward)]
    ppermute x21 -> x16, waiting for transfers between devices: 17.9 us -> 35.8 us  [the longest x2 7.41 us: route(): got = lax.ppermute(held, 'arc', flips(y=3))]
    pallas_call x12 -> x33, Pallas kernels: 31.4 us -> 23 us  [call(): pl.pallas_call(kernel, out_shape=shapes, in_specs=list(in_specs or [VMEM]...]
    unnamed x31 -> x19, local copies, waits for them, and re-layouts: 8.3 us -> 1.71 us
  transfers between devices with their start and end apart: 21 -> 16, of which waited for: 14 -> 14; matrix products, arithmetic and copies ran while one was open for 1% -> 0% of each run, Pallas kernels for 23% -> 21%
where the time goes in v3:
time: 75.8 us; the launch traced here: 75.6 us
  waiting for transfers between devices  35.8 us (47%)
  Pallas kernels  23 us (30%)
  starting transfers between devices  14.1 us (19%)
  local copies, waits for them, and re-layouts  1.71 us (2%)
  between operations  0.94 us (1%)
    pallas_call x33, Pallas kernels, call(): pl.pallas_call(kernel, out_shape=shapes, in_specs=list(in_specs or [VMEM]...  23 us
    ppermute x1, starting transfers between devices, local(): outer = lax.ppermute(outer, 'arc', outward)  7.6 us
    ppermute x2, waiting for transfers between devices, route(): got = lax.ppermute(held, 'arc', flips(y=3))  7.41 us
    ppermute x2, waiting for transfers between devices, route(): got = lax.ppermute(send, 'arc', flips(z=3))  6.41 us
    ppermute x2, waiting for transfers between devices, route(): got = lax.ppermute(held, 'arc', flips(y=1))  5.94 us
    ppermute x1, waiting for transfers between devices, local(): outer = lax.ppermute(outer, 'arc', outward)  4.86 us
    ppermute x2, waiting for transfers between devices, route(): return (keep, lax.ppermute(send, 'arc', flips(x=1)), between(5, send))  3.85 us
    ppermute x2, waiting for transfers between devices, route(): got = lax.ppermute(send, 'arc', flips(z=1))  2.73 us
  transfers between devices with their start and end apart: 16, of which 14 were waited for; matrix products, arithmetic and copies ran while one was open for 0% of the time, Pallas kernels for 21%

profile of v3, /device:TPU:0, one launch (start us, length us, event | category | flops | bytes accessed | tf_op | source)
XLA Modules:
  0.0 75.6 jit_solution(11736164308342714508)
XLA Ops:
  0.7 3.2 %edge.1 = (f32[8,512,128]{2,1,0:T(8,128)}, f32[8,48,128]{2,1,0:T(8,128)}, f32[8,48,128]{2,1,0:T(8,128)}) custom-call(f32[3,512,128]{2,1,0:T(8,128)} %disp.1, f32[3,512,128]{2,1,0:T(8,128)} %vel.1, f32[512,128]{1,0:T(8,128)} %mass.1, f32[512,128]{1,0:T(8,128)} %stiff.1), custom_call_target="tpu_custom_call" | custom-call | bytes 7200000 | tf_op jit(solution)/shard_map/edge/pallas_call | solution.py:540
  4.0 7.6 %collective-permute-start.1 = (f32[8,48,128]{2,1,0:T(8,128)}, f32[8,48,128]{2,1,0:T(8,128)S(1)}, u32[]{:S(2)}, u32[]{:S(2)}) collective-permute-start(f32[8,48,128]{2,1,0:T(8,128)} %get-tuple-element.62), channel_id=1, source_target_pairs={{2,4},{4,2},{6,8},{8,6},{10,12},{12,10},{14,16},{16,14},{18,20},{2... | collective-permute-start | bytes 589832 | tf_op jit(solution)/shard_map/ppermute | solution.py:636
  11.6 4.9 %collective-permute-done.1.outer = f32[8,48,128]{2,1,0:T(8,128)S(1)} collective-permute-done((f32[8,48,128]{2,1,0:T(8,128)}, f32[8,48,128]{2,1,0:T(8,128)S(1)}, u32[]{:S(2)}, u32[]{:S(2)}) %collective-permute-start.1) | collective-permute-done | bytes 196640 | tf_op jit(solution)/shard_map/ppermute | solution.py:636
  16.4 1.6 %copy-done = f32[8,512,128]{2,1,0:T(8,128)S(1)} copy-done((f32[8,512,128]{2,1,0:T(8,128)S(1)}, f32[8,512,128]{2,1,0:T(8,128)}, u32[]{:S(2)}) %copy-start) | copy-done | bytes 2097176
  18.7 2.5 %collective-permute-start.2 = (f32[304,128]{1,0:T(8,128)S(1)}, f32[304,128]{1,0:T(8,128)S(1)}, u32[]{:S(2)}, u32[]{:S(2)}) collective-permute-start(f32[304,128]{1,0:T(8,128)S(1)} %pack.1.rest_0_), channel_id=1, source_target_pairs={{0,1},{1,0},{2,3},{3,2},{4,5},{5,4},{6,7},{7,6},{8,9},{9,8},{10,11... | collective-permute-start | bytes 466952 | tf_op jit(solution)/shard_map/ppermute | solution.py:638
  21.3 1.2 %collective-permute-start.3 = (f32[8,128]{1,0:T(8,128)S(1)}, f32[8,128]{1,0:T(8,128)S(1)}, u32[]{:S(2)}, u32[]{:S(2)}) collective-permute-start(f32[8,128]{1,0:T(8,128)S(1)} %pad_edge.1), channel_id=1, source_target_pairs={{0,1},{1,0},{2,3},{3,2},{4,5},{5,4},{6,7},{7,6},{8,9},{9,8},{10,11... | collective-permute-start | bytes 12296 | tf_op jit(solution)/shard_map/ppermute | solution.py:619
  22.6 1.3 %plan.1 = (s32[32,128]{1,0:T(8,128)S(1)}, s32[2]{0:T(128)S(1)}, s32[4,16]{1,0:T(4,128)S(1)}, f32[1]{0:T(128)}) custom-call(s32[40]{0:T(128)S(1)} %copy-done.5, f32[40]{0:T(128)S(1)} %copy-done.6, s32[4,40,16]{2,1,0:T(8,128)S(1)} %copy.29.rows_ref, s32[168]{0:T(256)S(1)} %copy-done.4), custom_call_target="tpu_custom_call" | custom-call | bytes 10800000 | tf_op jit(solution)/shard_map/plan/pallas_call | solution.py:540
  24.0 2.5 %collective-permute-done.3.edges = f32[8,128]{1,0:T(8,128)S(1)} collective-permute-done((f32[8,128]{1,0:T(8,128)S(1)}, f32[8,128]{1,0:T(8,128)S(1)}, u32[]{:S(2)}, u32[]{:S(2)}) %collective-permute-start.3) | collective-permute-done | bytes 4128 | tf_op jit(solution)/shard_map/ppermute | solution.py:619
  26.5 1.2 %collective-permute-done.4.second = f32[1,24,128]{2,1,0:T(8,128)S(1)} collective-permute-done((f32[1,24,128]{2,1,0:T(8,128)S(1)}, f32[1,24,128]{2,1,0:T(8,128)S(1)}, u32[]{:S(2)}, u32[]{:S(2)}) %collective-permute-start.4) | collective-permute-done | bytes 12320 | tf_op jit(solution)/shard_map/ppermute | solution.py:556
  27.7 3.8 %collective-permute-done.5.second = f32[2,24,128]{2,1,0:T(8,128)S(1)} collective-permute-done((f32[2,24,128]{2,1,0:T(8,128)S(1)}, f32[2,24,128]{2,1,0:T(8,128)S(1)}, u32[]{:S(2)}, u32[]{:S(2)}) %collective-permute-start.5) | collective-permute-done | bytes 24608 | tf_op jit(solution)/shard_map/ppermute | solution.py:558
  32.2 4.6 %collective-permute-done.6.second = f32[4,24,128]{2,1,0:T(8,128)S(1)} collective-permute-done((f32[4,24,128]{2,1,0:T(8,128)S(1)}, f32[4,24,128]{2,1,0:T(8,128)S(1)}, u32[]{:S(2)}, u32[]{:S(2)}) %collective-permute-start.6) | collective-permute-done | bytes 49184 | tf_op jit(solution)/shard_map/ppermute | solution.py:560
  37.0 2.7 %bulk_load.1 = (f32[3,2,536,128]{3,2,1,0:T(8,128)S(1)}, f32[3,2,528,128]{3,2,1,0:T(8,128)S(1)}, f32[4,2,528,128]{3,2,1,0:T(8,128)S(1)}) custom-call(f32[8,512,128]{2,1,0:T(8,128)S(1)} %copy-done.1, f32[8,48,128]{2,1,0:T(8,128)S(1)} %collective-permute-done.inner, f32[8,48,128]{2,1,0:T(8,128)S(1)} %collective-permute-done.1.outer, ...), custom_call_target="tpu_custom_call" | custom-call | bytes 7200000 | tf_op jit(solution)/shard_map/bulk_load/pallas_call | solution.py:540
  39.6 0.9 %window_load.1 = (f32[3,2,72,128]{3,2,1,0:T(8,128)S(1)}, f32[3,2,64,128]{3,2,1,0:T(8,128)S(1)}, f32[4,2,64,128]{3,2,1,0:T(8,128)S(1)}) custom-call(s32[2]{0:T(128)S(1)} %get-tuple-element.59.where_ref, f32[8,512,128]{2,1,0:T(8,128)S(1)} %copy-done.1, f32[8,48,128]{2,1,0:T(8,128)S(1)} %collective-permute-done.inner, ...), custom_call_target="tpu_custom_call" | custom-call | bytes 2880000 | tf_op jit(solution)/shard_map/window_load/pallas_call | solution.py:540
  42.0 0.8 %bulk_step.13 = (f32[3,2,536,128]{3,2,1,0:T(8,128)S(1)}, f32[3,2,528,128]{3,2,1,0:T(8,128)S(1)}) custom-call(f32[16,128]{1,0:T(8,128)S(1)} %dynamic-slice_bitcast_fusion.table, f32[3,2,536,128]{3,2,1,0:T(8,128)S(1)} %get-tuple-element.63.rest_1_.state, f32[3,2,528,128]{3,2,1,0:T(8,128)S(1)} %get-tuple-element.64.vels, ...), custom_call_target="tpu_custom_call", output_to_operand_aliasing={{0}: (4, {}), {1}: (5, {})} | custom-call | bytes 2879999 | tf_op jit(solution)/shard_map/bulk_step/pallas_call | solution.py:540
  42.8 3.4 %collective-permute-done.8.got = f32[2,24,128]{2,1,0:T(8,128)S(1)} collective-permute-done((f32[2,24,128]{2,1,0:T(8,128)S(1)}, f32[2,24,128]{2,1,0:T(8,128)S(1)}, u32[]{:S(2)}, u32[]{:S(2)}) %collective-permute-start.8) | collective-permute-done | bytes 24608 | tf_op jit(solution)/shard_map/ppermute | solution.py:569
  46.2 0.8 %bulk_step.14 = (f32[3,2,536,128]{3,2,1,0:T(8,128)S(1)}, f32[3,2,528,128]{3,2,1,0:T(8,128)S(1)}) custom-call(f32[16,128]{1,0:T(8,128)S(1)} %dynamic-slice_bitcast_fusion.table, f32[3,2,536,128]{3,2,1,0:T(8,128)S(1)} %get-tuple-element.63.rest_1_.state, f32[3,2,528,128]{3,2,1,0:T(8,128)S(1)} %get-tuple-element.64.vels, ...), custom_call_target="tpu_custom_call", output_to_operand_aliasing={{0}: (4, {}), {1}: (5, {})} | custom-call | bytes 2879999 | tf_op jit(solution)/shard_map/bulk_step/pallas_call | solution.py:540
  47.7 2.2 %collective-permute-done.9.handed = f32[1,24,128]{2,1,0:T(8,128)S(1)} collective-permute-done((f32[1,24,128]{2,1,0:T(8,128)S(1)}, f32[1,24,128]{2,1,0:T(8,128)S(1)}, u32[]{:S(2)}, u32[]{:S(2)}) %collective-permute-start.9) | collective-permute-done | bytes 12320 | tf_op jit(solution)/shard_map/ppermute | solution.py:574
  49.9 2.3 %window.1 = (f32[3,2,72,128]{3,2,1,0:T(8,128)S(1)}, f32[3,2,64,128]{3,2,1,0:T(8,128)S(1)}, f32[2,2,64,128]{3,2,1,0:T(8,128)S(1)}, f32[1,16,128]{2,1,0:T(8,128)S(1)}) custom-call(s32[4,16]{1,0:T(4,128)S(1)} %get-tuple-element.81.list_ref, f32[1]{0:T(128)} %get-tuple-element.82.lift_ref, s32[32,128]{1,0:T(8,128)S(1)} %get-tuple-element.66.rest_0_.plan, ...), custom_call_target="tpu_custom_call" | custom-call | bytes 7200000 | tf_op jit(solution)/shard_map/window/pallas_call | solution.py:540
  52.5 0.9 %collective-permute-done.10.second = f32[1,16,128]{2,1,0:T(8,128)S(1)} collective-permute-done((f32[1,16,128]{2,1,0:T(8,128)S(1)}, f32[1,16,128]{2,1,0:T(8,128)S(1)}, u32[]{:S(2)}, u32[]{:S(2)}) %collective-permute-start.10) | collective-permute-done | bytes 8224 | tf_op jit(solution)/shard_map/ppermute | solution.py:556
  53.4 0.8 %bulk_step.16 = (f32[3,2,536,128]{3,2,1,0:T(8,128)S(1)}, f32[3,2,528,128]{3,2,1,0:T(8,128)S(1)}) custom-call(f32[16,128]{1,0:T(8,128)S(1)} %dynamic-slice_bitcast_fusion.table, f32[3,2,536,128]{3,2,1,0:T(8,128)S(1)} %get-tuple-element.77.state, f32[3,2,528,128]{3,2,1,0:T(8,128)S(1)} %get-tuple-element.78.vels, ...), custom_call_target="tpu_custom_call", output_to_operand_aliasing={{0}: (4, {}), {1}: (5, {})} | custom-call | bytes 2879999 | tf_op jit(solution)/shard_map/bulk_step/pallas_call | solution.py:540
  54.2 0.8 %bulk_step.17 = (f32[3,2,536,128]{3,2,1,0:T(8,128)S(1)}, f32[3,2,528,128]{3,2,1,0:T(8,128)S(1)}) custom-call(f32[16,128]{1,0:T(8,128)S(1)} %dynamic-slice_bitcast_fusion.table, f32[3,2,536,128]{3,2,1,0:T(8,128)S(1)} %get-tuple-element.77.state, f32[3,2,528,128]{3,2,1,0:T(8,128)S(1)} %get-tuple-element.78.vels, ...), custom_call_target="tpu_custom_call", output_to_operand_aliasing={{0}: (4, {}), {1}: (5, {})} | custom-call | bytes 2879999 | tf_op jit(solution)/shard_map/bulk_step/pallas_call | solution.py:540
  55.0 2.1 %collective-permute-done.11.second = f32[2,16,128]{2,1,0:T(8,128)S(1)} collective-permute-done((f32[2,16,128]{2,1,0:T(8,128)S(1)}, f32[2,16,128]{2,1,0:T(8,128)S(1)}, u32[]{:S(2)}, u32[]{:S(2)}) %collective-permute-start.11) | collective-permute-done | bytes 16416 | tf_op jit(solution)/shard_map/ppermute | solution.py:558
  57.2 0.8 %collective-permute-start.12 = (f32[4,16,128]{2,1,0:T(8,128)S(1)}, f32[4,16,128]{2,1,0:T(8,128)S(1)}, u32[]{:S(2)}, u32[]{:S(2)}) collective-permute-start(f32[4,16,128]{2,1,0:T(8,128)S(1)} %stack.7.rest_0_.rest_2_.first), channel_id=1, source_target_pairs={{0,96},{2,98},{4,100},{6,102},{8,104},{10,106},{12,108},{14,110},{... | collective-permute-start | bytes 98312 | tf_op jit(solution)/shard_map/ppermute | solution.py:560
  58.6 0.8 %bulk_step.19 = (f32[3,2,536,128]{3,2,1,0:T(8,128)S(1)}, f32[3,2,528,128]{3,2,1,0:T(8,128)S(1)}) custom-call(f32[16,128]{1,0:T(8,128)S(1)} %dynamic-slice_bitcast_fusion.table, f32[3,2,536,128]{3,2,1,0:T(8,128)S(1)} %get-tuple-element.92.rest_0_.state, f32[3,2,528,128]{3,2,1,0:T(8,128)S(1)} %get-tuple-element.93.vels, ...), custom_call_target="tpu_custom_call", output_to_operand_aliasing={{0}: (4, {}), {1}: (5, {})} | custom-call | bytes 2879999 | tf_op jit(solution)/shard_map/bulk_step/pallas_call | solution.py:540
  59.4 2.9 %collective-permute-done.12.second = f32[4,16,128]{2,1,0:T(8,128)S(1)} collective-permute-done((f32[4,16,128]{2,1,0:T(8,128)S(1)}, f32[4,16,128]{2,1,0:T(8,128)S(1)}, u32[]{:S(2)}, u32[]{:S(2)}) %collective-permute-start.12) | collective-permute-done | bytes 32800 | tf_op jit(solution)/shard_map/ppermute | solution.py:560
  62.6 0.8 %bulk_step.20 = (f32[3,2,536,128]{3,2,1,0:T(8,128)S(1)}, f32[3,2,528,128]{3,2,1,0:T(8,128)S(1)}) custom-call(f32[16,128]{1,0:T(8,128)S(1)} %dynamic-slice_bitcast_fusion.table, f32[3,2,536,128]{3,2,1,0:T(8,128)S(1)} %get-tuple-element.92.rest_0_.state, f32[3,2,528,128]{3,2,1,0:T(8,128)S(1)} %get-tuple-element.93.vels, ...), custom_call_target="tpu_custom_call", output_to_operand_aliasing={{0}: (4, {}), {1}: (5, {})} | custom-call | bytes 2879999 | tf_op jit(solution)/shard_map/bulk_step/pallas_call | solution.py:540
  64.1 2.2 %collective-permute-done.13.got = f32[4,16,128]{2,1,0:T(8,128)S(1)} collective-permute-done((f32[4,16,128]{2,1,0:T(8,128)S(1)}, f32[4,16,128]{2,1,0:T(8,128)S(1)}, u32[]{:S(2)}, u32[]{:S(2)}) %collective-permute-start.13) | collective-permute-done | bytes 32800 | tf_op jit(solution)/shard_map/ppermute | solution.py:564
  66.7 0.8 %bulk_step.22 = (f32[3,2,536,128]{3,2,1,0:T(8,128)S(1)}, f32[3,2,528,128]{3,2,1,0:T(8,128)S(1)}) custom-call(f32[16,128]{1,0:T(8,128)S(1)} %dynamic-slice_bitcast_fusion.table, f32[3,2,536,128]{3,2,1,0:T(8,128)S(1)} %get-tuple-element.99.state, f32[3,2,528,128]{3,2,1,0:T(8,128)S(1)} %get-tuple-element.100.vels, ...), custom_call_target="tpu_custom_call", output_to_operand_aliasing={{0}: (4, {}), {1}: (5, {})} | custom-call | bytes 2879999 | tf_op jit(solution)/shard_map/bulk_step/pallas_call | solution.py:540
  67.5 0.8 %bulk_step.23 = (f32[3,2,536,128]{3,2,1,0:T(8,128)S(1)}, f32[3,2,528,128]{3,2,1,0:T(8,128)S(1)}) custom-call(f32[16,128]{1,0:T(8,128)S(1)} %dynamic-slice_bitcast_fusion.table, f32[3,2,536,128]{3,2,1,0:T(8,128)S(1)} %get-tuple-element.99.state, f32[3,2,528,128]{3,2,1,0:T(8,128)S(1)} %get-tuple-element.100.vels, ...), custom_call_target="tpu_custom_call", output_to_operand_aliasing={{0}: (4, {}), {1}: (5, {})} | custom-call | bytes 2879999 | tf_op jit(solution)/shard_map/bulk_step/pallas_call | solution.py:540
  68.3 3.1 %collective-permute-done.14.got = f32[2,16,128]{2,1,0:T(8,128)S(1)} collective-permute-done((f32[2,16,128]{2,1,0:T(8,128)S(1)}, f32[2,16,128]{2,1,0:T(8,128)S(1)}, u32[]{:S(2)}, u32[]{:S(2)}) %collective-permute-start.14) | collective-permute-done | bytes 16416 | tf_op jit(solution)/shard_map/ppermute | solution.py:569
  71.4 1.9 %bulk_store.1 = (f32[3,512,128]{2,1,0:T(8,128)}, f32[3,512,128]{2,1,0:T(8,128)}, f32[8,128]{1,0:T(8,128)S(1)}) custom-call(s32[2]{0:T(128)S(1)} %get-tuple-element.59.where_ref, f32[3,2,536,128]{3,2,1,0:T(8,128)S(1)} %get-tuple-element.107.rest_0_.state, f32[3,2,528,128]{3,2,1,0:T(8,128)S(1)} %get-tuple-element.108.vels, ...), custom_call_target="tpu_custom_call" | custom-call | bytes 7200000 | tf_op jit(solution)/shard_map/bulk_store/pallas_call | solution.py:540
  73.4 1.7 %collective-permute-done.15.handed = f32[1,16,128]{2,1,0:T(8,128)S(1)} collective-permute-done((f32[1,16,128]{2,1,0:T(8,128)S(1)}, f32[1,16,128]{2,1,0:T(8,128)S(1)}, u32[]{:S(2)}, u32[]{:S(2)}) %collective-permute-start.15) | collective-permute-done | bytes 8224 | tf_op jit(solution)/shard_map/ppermute | solution.py:574
  (53 shorter events, 7.1 us)
Async XLA Ops:
  0.6 20.6 %copy-start.3 = (f32[1,16,128]{2,1,0:T(8,128)S(1)}, f32[1,16,128]{2,1,0:T(8,128)}, u32[]{:S(2)}) copy-start(f32[1,16,128]{2,1,0:T(8,128)} %before.1) | copy-start | bytes 24580
  0.6 21.9 %copy-start.7 = (s32[4,40,16]{1,2,0:T(8,128)S(1)}, s32[4,40,16]{1,2,0:T(8,128)}, u32[]{:S(2)}) copy-start(s32[4,40,16]{1,2,0:T(8,128)} %param.16) | copy-start | bytes 30724
  3.8 18.8 %copy-start.4 = (s32[168]{0:T(256)S(1)}, s32[168]{0:T(256)}, u32[]{:S(2)}) copy-start(s32[168]{0:T(256)} %constant.13.clone.static_ref) | copy-start | bytes 2020
  3.8 18.8 %copy-start.5 = (s32[40]{0:T(128)S(1)}, s32[40]{0:T(128)}, u32[]{:S(2)}) copy-start(s32[40]{0:T(128)} %slot_ref.1) | copy-start | bytes 484
  3.8 18.8 %copy-start.6 = (f32[40]{0:T(128)S(1)}, f32[40]{0:T(128)}, u32[]{:S(2)}) copy-start(f32[40]{0:T(128)} %lift_ref.1) | copy-start | bytes 484
  3.9 7.7 %collective-permute-start = (f32[8,48,128]{2,1,0:T(8,128)}, f32[8,48,128]{2,1,0:T(8,128)S(1)}, u32[]{:S(2)}, u32[]{:S(2)}) collective-permute-start(f32[8,48,128]{2,1,0:T(8,128)} %get-tuple-element.61.rest_1_), channel_id=1, source_target_pairs={{0,2},{2,0},{4,6},{6,4},{8,10},{10,8},{12,14},{14,12},{16,18},{18,... | collective-permute-start | bytes 589832 | tf_op jit(solution)/shard_map/ppermute | solution.py:635
  4.0 12.5 %collective-permute-start.1 = (f32[8,48,128]{2,1,0:T(8,128)}, f32[8,48,128]{2,1,0:T(8,128)S(1)}, u32[]{:S(2)}, u32[]{:S(2)}) collective-permute-start(f32[8,48,128]{2,1,0:T(8,128)} %get-tuple-element.62), channel_id=1, source_target_pairs={{2,4},{4,2},{6,8},{8,6},{10,12},{12,10},{14,16},{16,14},{18,20},{2... | collective-permute-start | bytes 589832 | tf_op jit(solution)/shard_map/ppermute | solution.py:636
  16.4 1.6 %copy-start = (f32[8,512,128]{2,1,0:T(8,128)S(1)}, f32[8,512,128]{2,1,0:T(8,128)}, u32[]{:S(2)}) copy-start(f32[8,512,128]{2,1,0:T(8,128)} %get-tuple-element.60.field) | copy-start | bytes 6291460
  18.0 8.5 %copy-start.2 = (f32[8,48,128]{2,1,0:T(8,128)S(1)}, f32[8,48,128]{2,1,0:T(8,128)}, u32[]{:S(2)}) copy-start(f32[8,48,128]{2,1,0:T(8,128)} %get-tuple-element.61.rest_1_) | copy-start | bytes 589828
  18.0 19.0 %copy-start.1 = (f32[8,512,128]{2,1,0:T(8,128)S(1)}, f32[8,512,128]{2,1,0:T(8,128)}, u32[]{:S(2)}) copy-start(f32[8,512,128]{2,1,0:T(8,128)} %get-tuple-element.60.field) | copy-start | bytes 6291460
  18.7 18.2 %collective-permute-start.2 = (f32[304,128]{1,0:T(8,128)S(1)}, f32[304,128]{1,0:T(8,128)S(1)}, u32[]{:S(2)}, u32[]{:S(2)}) collective-permute-start(f32[304,128]{1,0:T(8,128)S(1)} %pack.1.rest_0_), channel_id=1, source_target_pairs={{0,1},{1,0},{2,3},{3,2},{4,5},{5,4},{6,7},{7,6},{8,9},{9,8},{10,11... | collective-permute-start | bytes 466952 | tf_op jit(solution)/shard_map/ppermute | solution.py:638
  21.3 5.2 %collective-permute-start.3 = (f32[8,128]{1,0:T(8,128)S(1)}, f32[8,128]{1,0:T(8,128)S(1)}, u32[]{:S(2)}, u32[]{:S(2)}) collective-permute-start(f32[8,128]{1,0:T(8,128)S(1)} %pad_edge.1), channel_id=1, source_target_pairs={{0,1},{1,0},{2,3},{3,2},{4,5},{5,4},{6,7},{7,6},{8,9},{9,8},{10,11... | collective-permute-start | bytes 12296 | tf_op jit(solution)/shard_map/ppermute | solution.py:619
  26.5 1.2 %collective-permute-start.4 = (f32[1,24,128]{2,1,0:T(8,128)S(1)}, f32[1,24,128]{2,1,0:T(8,128)S(1)}, u32[]{:S(2)}, u32[]{:S(2)}) collective-permute-start(f32[1,24,128]{2,1,0:T(8,128)S(1)} %pad_extend.1.first), channel_id=1, source_target_pairs={{0,2},{2,0},{4,6},{6,4},{8,10},{10,8},{12,14},{14,12},{16,18},{18,... | collective-permute-start | bytes 36872 | tf_op jit(solution)/shard_map/ppermute | solution.py:556
  27.7 3.8 %collective-permute-start.5 = (f32[2,24,128]{2,1,0:T(8,128)S(1)}, f32[2,24,128]{2,1,0:T(8,128)S(1)}, u32[]{:S(2)}, u32[]{:S(2)}) collective-permute-start(f32[2,24,128]{2,1,0:T(8,128)S(1)} %stack.4.first), channel_id=1, source_target_pairs={{0,32},{2,34},{4,36},{6,38},{8,40},{10,42},{12,44},{14,46},{16,48}... | collective-permute-start | bytes 73736 | tf_op jit(solution)/shard_map/ppermute | solution.py:558
  31.5 5.3 %collective-permute-start.6 = (f32[4,24,128]{2,1,0:T(8,128)S(1)}, f32[4,24,128]{2,1,0:T(8,128)S(1)}, u32[]{:S(2)}, u32[]{:S(2)}) collective-permute-start(f32[4,24,128]{2,1,0:T(8,128)S(1)} %stack.5.first), channel_id=1, source_target_pairs={{0,96},{2,98},{4,100},{6,102},{8,104},{10,106},{12,108},{14,110},{... | collective-permute-start | bytes 147464 | tf_op jit(solution)/shard_map/ppermute | solution.py:560
  36.9 4.2 %collective-permute-start.7 = (f32[4,24,128]{2,1,0:T(8,128)S(1)}, f32[4,24,128]{2,1,0:T(8,128)S(1)}, u32[]{:S(2)}, u32[]{:S(2)}) collective-permute-start(f32[4,24,128]{2,1,0:T(8,128)S(1)} %get-tuple-element.68), channel_id=1, source_target_pairs={{0,8},{2,10},{4,12},{6,14},{8,0},{10,2},{12,4},{14,6},{16,24},{18,... | collective-permute-start | bytes 147464 | tf_op jit(solution)/shard_map/ppermute | solution.py:564
  40.5 0.8 %copy-start.8 = (f32[2,16,128]{2,1,0:T(8,128)S(1)}, f32[2,16,128]{2,1,0:T(8,128)}, u32[]{:S(2)}) copy-start(f32[2,16,128]{2,1,0:T(8,128)} %constant.12.clone) | copy-start | bytes 49156
  41.0 5.1 %collective-permute-start.8 = (f32[2,24,128]{2,1,0:T(8,128)S(1)}, f32[2,24,128]{2,1,0:T(8,128)S(1)}, u32[]{:S(2)}, u32[]{:S(2)}) collective-permute-start(f32[2,24,128]{2,1,0:T(8,128)S(1)} %get-tuple-element.70.rest_0_.rest_2_), channel_id=1, source_target_pairs={{0,24},{2,26},{4,28},{6,30},{8,16},{10,18},{12,20},{14,22},{16,8},... | collective-permute-start | bytes 73736 | tf_op jit(solution)/shard_map/ppermute | solution.py:569
  46.2 3.7 %collective-permute-start.9 = (f32[1,24,128]{2,1,0:T(8,128)S(1)}, f32[1,24,128]{2,1,0:T(8,128)S(1)}, u32[]{:S(2)}, u32[]{:S(2)}) collective-permute-start(f32[1,24,128]{2,1,0:T(8,128)S(1)} %get-tuple-element.76.rest_2_.rest_0_), channel_id=1, source_target_pairs={{0,4},{2,6},{4,0},{6,2},{8,12},{10,14},{12,8},{14,10},{16,20},{18,... | collective-permute-start | bytes 36872 | tf_op jit(solution)/shard_map/ppermute | solution.py:574
  52.2 1.3 %collective-permute-start.10 = (f32[1,16,128]{2,1,0:T(8,128)S(1)}, f32[1,16,128]{2,1,0:T(8,128)S(1)}, u32[]{:S(2)}, u32[]{:S(2)}) collective-permute-start(f32[1,16,128]{2,1,0:T(8,128)S(1)} %get-tuple-element.86.first), channel_id=1, source_target_pairs={{0,2},{2,0},{4,6},{6,4},{8,10},{10,8},{12,14},{14,12},{16,18},{18,... | collective-permute-start | bytes 24584 | tf_op jit(solution)/shard_map/ppermute | solution.py:556
  53.4 3.7 %collective-permute-start.11 = (f32[2,16,128]{2,1,0:T(8,128)S(1)}, f32[2,16,128]{2,1,0:T(8,128)S(1)}, u32[]{:S(2)}, u32[]{:S(2)}) collective-permute-start(f32[2,16,128]{2,1,0:T(8,128)S(1)} %stack.6.rest_2_.first), channel_id=1, source_target_pairs={{0,32},{2,34},{4,36},{6,38},{8,40},{10,42},{12,44},{14,46},{16,48}... | collective-permute-start | bytes 49160 | tf_op jit(solution)/shard_map/ppermute | solution.py:558
  57.2 5.1 %collective-permute-start.12 = (f32[4,16,128]{2,1,0:T(8,128)S(1)}, f32[4,16,128]{2,1,0:T(8,128)S(1)}, u32[]{:S(2)}, u32[]{:S(2)}) collective-permute-start(f32[4,16,128]{2,1,0:T(8,128)S(1)} %stack.7.rest_0_.rest_2_.first), channel_id=1, source_target_pairs={{0,96},{2,98},{4,100},{6,102},{8,104},{10,106},{12,108},{14,110},{... | collective-permute-start | bytes 98312 | tf_op jit(solution)/shard_map/ppermute | solution.py:560
  62.3 4.0 %collective-permute-start.13 = (f32[4,16,128]{2,1,0:T(8,128)S(1)}, f32[4,16,128]{2,1,0:T(8,128)S(1)}, u32[]{:S(2)}, u32[]{:S(2)}) collective-permute-start(f32[4,16,128]{2,1,0:T(8,128)S(1)} %get-tuple-element.98.rest_2_.rest_0_), channel_id=1, source_target_pairs={{0,8},{2,10},{4,12},{6,14},{8,0},{10,2},{12,4},{14,6},{16,24},{18,... | collective-permute-start | bytes 98312 | tf_op jit(solution)/shard_map/ppermute | solution.py:564
  66.3 5.0 %collective-permute-start.14 = (f32[2,16,128]{2,1,0:T(8,128)S(1)}, f32[2,16,128]{2,1,0:T(8,128)S(1)}, u32[]{:S(2)}, u32[]{:S(2)}) collective-permute-start(f32[2,16,128]{2,1,0:T(8,128)S(1)} %get-tuple-element.104.rest_2_), channel_id=1, source_target_pairs={{0,24},{2,26},{4,28},{6,30},{8,16},{10,18},{12,20},{14,22},{16,8},... | collective-permute-start | bytes 49160 | tf_op jit(solution)/shard_map/ppermute | solution.py:569
  71.4 3.7 %collective-permute-start.15 = (f32[1,16,128]{2,1,0:T(8,128)S(1)}, f32[1,16,128]{2,1,0:T(8,128)S(1)}, u32[]{:S(2)}, u32[]{:S(2)}) collective-permute-start(f32[1,16,128]{2,1,0:T(8,128)S(1)} %get-tuple-element.110.rest_0_), channel_id=1, source_target_pairs={{0,4},{2,6},{4,0},{6,2},{8,12},{10,14},{12,8},{14,10},{16,20},{18,... | collective-permute-start | bytes 24584 | tf_op jit(solution)/shard_map/ppermute | solution.py:574

commit v4 on v3

--- a/solution.py
+++ b/solution.py
@@ -26,7 +26,7 @@
 GROUP = 11
 PARTS = 3
 LOAD_GROUP = 4
-LIMIT = 40 * 1024 * 1024
+LIMIT = 16 * 1024 * 1024
 MOST = 60 * 1024 * 1024
 
 
@@ -72,15 +72,11 @@
     return np.stack(rows).astype(np.float32), axial, hoop_gain
 
 
-def edge_kernel(halo, disp, vel, mass, stiff, field, inner, outer, sems):
+def edge_kernel(halo, disp, vel, mass, stiff, *rest):
+    inner, outer, sems = rest[-3:]
     own = disp.shape[1]
     odd = lax.axis_index("arc") & 1
-    copies = [
-        pltpu.make_async_copy(disp, field.at[0:3], sems.at[8]),
-        pltpu.make_async_copy(vel, field.at[3:6], sems.at[9]),
-        pltpu.make_async_copy(mass, field.at[6], sems.at[10]),
-        pltpu.make_async_copy(stiff, field.at[7], sems.at[11]),
-    ]
+    copies = []
     for n, (edge, at) in enumerate(((inner, (1 - odd) * (own - halo)), (outer, odd * (own - halo)))):
         span = pl.ds(pl.multiple_of(at, 8), halo)
         copies += [
@@ -149,27 +145,37 @@
         line(at + USED, (source[me] >= 0).astype(jnp.int32))
 
 
-def row_block(field, inner, outer, odd, a, row):
+def take(fields, a, span):
+    disp, vel, mass, stiff = fields
+    if a < 3:
+        return disp[a, span, :]
+    if a < 6:
+        return vel[a - 3, span, :]
+    return mass[span, :] if a == 6 else stiff[span, :]
+
+
+def row_block(fields, inner, outer, odd, a, row):
     halo = inner.shape[1]
-    own = field.shape[1]
+    own = fields[0].shape[1]
     if row < halo:
         span = slice(row, row + 8)
         return jnp.where(odd, inner[a, span, :], outer[a, span, :])
     if row < halo + own:
-        return field[a, row - halo : row - halo + 8, :]
+        return take(fields, a, slice(row - halo, row - halo + 8))
     span = slice(row - halo - own, row - halo - own + 8)
     return jnp.where(odd, outer[a, span, :], inner[a, span, :])
 
 
-def pack_kernel(field, inner, outer, pack):
-    half = field.shape[1] // 2 + inner.shape[1]
+def pack_kernel(*refs):
+    fields, inner, outer, pack = refs[:4], refs[4], refs[5], refs[-1]
+    half = fields[0].shape[1] // 2 + inner.shape[1]
     odd = (lax.axis_index("arc") & 1) > 0
     lane = lax.broadcasted_iota(jnp.int32, (8, LANES), 1) // (2 * EDGE)
     for r in range(0, half, 8):
         packed = jnp.zeros((8, LANES), jnp.float32)
         for part in range(2):
             for a in range(8):
-                value = row_block(field, inner, outer, odd, a, r + part * half)
+                value = row_block(fields, inner, outer, odd, a, r + part * half)
                 moved = pltpu.roll(value, (8 * a + EDGE + 64 * part) % LANES, 1)
                 packed = jnp.where(lane == a + 8 * part, moved, packed)
         pack[r : r + 8, :] = packed
@@ -347,15 +353,16 @@
     out[0, slots:, :] = edges[...]
 
 
-def window_load_kernel(half, base, cycle_total, where_ref, field, inner, outer, columns, state, vels, coef):
+def window_load_kernel(half, base, cycle_total, where_ref, *refs):
+    fields, (inner, outer, columns, state, vels, coef) = refs[:4], refs[4:]
     start = pl.multiple_of(where_ref[0], 8)
     halo = inner.shape[1]
-    own = field.shape[1]
+    own = fields[0].shape[1]
     odd = (lax.axis_index("arc") & 1) > 0
 
     def source(a, r):
         row = start + r
-        mid = field[a, pl.ds(pl.multiple_of(jnp.clip(row - halo, 0, own - 8), 8), 8), :]
+        mid = take(fields, a, pl.ds(pl.multiple_of(jnp.clip(row - halo, 0, own - 8), 8), 8))
         before = row < halo
         at = jnp.where(before, row, jnp.maximum(row - halo - own, 0))
         span = pl.ds(pl.multiple_of(at, 8), 8)
@@ -424,14 +431,15 @@
         result[3 + a] = vels_later[a, 0] * (1.0 / TIME_STEP)
 
 
-def bulk_load_kernel(half, base, cycle_total, rows, field, inner, outer, columns, state, vels, coef):
+def bulk_load_kernel(half, base, cycle_total, rows, *refs):
+    fields, (inner, outer, columns, state, vels, coef) = refs[:4], refs[4:]
     first_row = HALO - 8
     odd = (lax.axis_index("arc") & 1) > 0
 
     def source(a, r):
         if isinstance(r, int):
-            return row_block(field, inner, outer, odd, a, first_row + r)
-        return field[a, pl.ds(pl.multiple_of(r - 8, 8), 8), :]
+            return row_block(fields, inner, outer, odd, a, first_row + r)
+        return take(fields, a, pl.ds(pl.multiple_of(r - 8, 8), 8))
 
     first_id = base(lax.axis_index("arc"))
     load_state(
@@ -617,10 +625,10 @@
 
     pad_edges = call(pad_edge_kernel, "pad_edge", real(8, LANES), (pad_state,))
     pad_edges = lax.ppermute(pad_edges, "circ", swap)
-    field, inner, outer = call(
+    inner, outer = call(
         functools.partial(edge_kernel, HALO), "edge",
-        (real(8, cycle_dev, LANES), real(8, HALO, LANES), real(8, HALO, LANES)), fields,
-        in_specs=[HBM] * 4, scratch=[pltpu.SemaphoreType.DMA((12,))], micros=2.0, limit=MOST,
+        (real(8, HALO, LANES), real(8, HALO, LANES)), fields,
+        in_specs=[HBM] * 4, scratch=[pltpu.SemaphoreType.DMA((8,))], micros=2.0, limit=MOST,
     )
     plan, where, rows_in, lift = call(
         functools.partial(plan_kernel, arc_count, cycle_dev), "plan",
@@ -631,23 +639,20 @@
     )
 
     outward = [pair for i in range(1, arc_count, 2) for pair in ((i, (i + 1) % arc_count), ((i + 1) % arc_count, i))]
-    token = inner
     inner = lax.ppermute(inner, "arc", flips(c=1))
     outer = lax.ppermute(outer, "arc", outward)
-    pack = call(pack_kernel, "pack", real(half, LANES), (field, inner, outer), micros=2.0)
-    columns = lax.ppermute(pack, "circ", swap)
     kept = {"done": 0}
 
     def load_window():
         return call(
             functools.partial(window_load_kernel, half, base, cycle_total), "window_load", buffers(WIN),
-            (where, field, inner, outer, columns), in_specs=[SMEM] + [VMEM] * 4, micros=0.8,
+            (where, *fields, inner, outer, kept["columns"]), in_specs=[SMEM] + [VMEM] * 7, micros=0.8,
         )
 
     def load_bulk():
         return call(
             functools.partial(bulk_load_kernel, half, base, cycle_total, rows), "bulk_load", buffers(rows),
-            (field, inner, outer, columns), micros=2.0,
+            (*fields, inner, outer, kept["columns"]), micros=2.0,
         )
 
     def step_bulk(value, count):
@@ -680,15 +685,17 @@
 
     def going(stage, value):
         if stage == 1:
+            pack = call(pack_kernel, "pack", real(half, LANES), (*fields, inner, outer), micros=2.0, after=(value,))
+            kept["columns"] = lax.ppermute(pack, "circ", swap)
             return (pack,)
         if stage == 3:
             kept["window"] = load_window()
             kept["bulk"] = load_bulk()
             return (kept["window"][0], kept["bulk"][0])
-        return step_bulk(value, 2) if stage > 3 else ()
+        return step_bulk(value, 3) if stage > 3 else ()
 
     value = call(
-        pad_extend_kernel, "pad_extend", real(1, slots + 8, LANES), (pad_state, pad_edges), after=(plan, token)
+        pad_extend_kernel, "pad_extend", real(1, slots + 8, LANES), (pad_state, pad_edges), after=(plan,)
     )
     pads, handed, done = route(value, plan, 0, going)
 
@@ -714,7 +721,9 @@
                 scratch=room(WIN), micros=0.6,
             )
             return (kept["last"],)
-        return store_bulk(value) if stage == 5 else step_bulk(value, 2)
+        if stage == 4:
+            return store_bulk(value)
+        return step_bulk(value, 2) if stage < 4 else ()
 
     pads, handed, done = route(pad_new, plan, 1, coming)
     pad_result = call(last_kernel, "last", real(1, slots, LANES), (plan, pads, handed, pad_state), after=done)

time: 75.8 us -> 70.2 us (0.926)
  waiting for transfers between devices: 35.8 us -> 28.5 us
  starting transfers between devices: 14.1 us -> 16.2 us
  Pallas kernels: 23 us -> 21.9 us
    ppermute x1, waiting for transfers between devices: 4.86 us -> 0.01 us  [local(): outer = lax.ppermute(outer, 'arc', outward)]
    ppermute x1, waiting for transfers between devices: 2.51 us -> 0.81 us  [local(): pad_edges = lax.ppermute(pad_edges, 'circ', swap)]
    ppermute x1, starting transfers between devices: 1.22 us -> 2.81 us  [local(): pad_edges = lax.ppermute(pad_edges, 'circ', swap)]
    ppermute x2, waiting for transfers between devices: 6.41 us -> 5.03 us  [route(): got = lax.ppermute(send, 'arc', flips(z=3))]
    pallas_call x33, Pallas kernels: 23 us -> 21.9 us  [call(): pl.pallas_call(kernel, out_shape=shapes, in_specs=list(in_specs or [VMEM]...]
    unnamed x19 -> x23, local copies, waits for them, and re-layouts: 1.71 us -> 2.34 us
  transfers between devices with their start and end apart: 16 -> 16, of which waited for: 14 -> 13; matrix products, arithmetic and copies ran while one was open for 0% -> 1% of each run, Pallas kernels for 21% -> 23%
where the time goes in v4:
time: 70.2 us; the launch traced here: 69.8 us
  waiting for transfers between devices  28.5 us (41%)
  Pallas kernels  21.9 us (31%)
  starting transfers between devices  16.2 us (23%)
  local copies, waits for them, and re-layouts  2.34 us (3%)
  between operations  0.99 us (1%)
    pallas_call x33, Pallas kernels, call(): pl.pallas_call(kernel, out_shape=shapes, in_specs=list(in_specs or [VMEM]...  21.9 us
    ppermute x1, starting transfers between devices, local(): outer = lax.ppermute(outer, 'arc', outward)  7.6 us
    ppermute x2, waiting for transfers between devices, route(): got = lax.ppermute(held, 'arc', flips(y=3))  7.41 us
    ppermute x2, waiting for transfers between devices, route(): got = lax.ppermute(held, 'arc', flips(y=1))  6.08 us
    ppermute x2, waiting for transfers between devices, route(): got = lax.ppermute(send, 'arc', flips(z=3))  5.03 us
    ppermute x2, waiting for transfers between devices, route(): return (keep, lax.ppermute(send, 'arc', flips(x=1)), between(5, send))  4.39 us
    ppermute x1, starting transfers between devices, local(): pad_edges = lax.ppermute(pad_edges, 'circ', swap)  2.81 us
    ppermute x2, waiting for transfers between devices, route(): got = lax.ppermute(send, 'arc', flips(z=1))  2.62 us
  transfers between devices with their start and end apart: 16, of which 13 were waited for; matrix products, arithmetic and copies ran while one was open for 1% of the time, Pallas kernels for 23%

profile of v4, /device:TPU:0, one launch (start us, length us, event | category | flops | bytes accessed | tf_op | source)
XLA Modules:
  0.0 69.8 jit_solution(5429060600487722821)
XLA Ops:
  0.7 2.0 %edge.1 = (f32[8,48,128]{2,1,0:T(8,128)}, f32[8,48,128]{2,1,0:T(8,128)}) custom-call(f32[3,512,128]{2,1,0:T(8,128)} %refs_0_.5, f32[3,512,128]{2,1,0:T(8,128)} %refs_1_.5, f32[512,128]{1,0:T(8,128)} %refs_2_.5, f32[512,128]{1,0:T(8,128)} %refs_3_.5), custom_call_target="tpu_custom_call" | custom-call | bytes 7200000 | tf_op jit(solution)/shard_map/edge/pallas_call | solution.py:548
  2.8 7.6 %collective-permute-start.1 = (f32[8,48,128]{2,1,0:T(8,128)}, f32[8,48,128]{2,1,0:T(8,128)S(1)}, u32[]{:S(2)}, u32[]{:S(2)}) collective-permute-start(f32[8,48,128]{2,1,0:T(8,128)} %get-tuple-element.60), channel_id=1, source_target_pairs={{2,4},{4,2},{6,8},{8,6},{10,12},{12,10},{14,16},{16,14},{18,20},{2... | collective-permute-start | bytes 589832 | tf_op jit(solution)/shard_map/ppermute | solution.py:643
  11.2 2.8 %collective-permute-start.2 = (f32[8,128]{1,0:T(8,128)S(1)}, f32[8,128]{1,0:T(8,128)S(1)}, u32[]{:S(2)}, u32[]{:S(2)}) collective-permute-start(f32[8,128]{1,0:T(8,128)S(1)} %pad_edge.1), channel_id=1, source_target_pairs={{0,1},{1,0},{2,3},{3,2},{4,5},{5,4},{6,7},{7,6},{8,9},{9,8},{10,11... | collective-permute-start | bytes 12296 | tf_op jit(solution)/shard_map/ppermute | solution.py:627
  14.0 0.8 %copy.29.rows_ref = s32[4,40,16]{2,1,0:T(8,128)S(1)} copy(s32[4,40,16]{1,2,0:T(8,128)} %param.16) | data formatting | bytes 20480 | tf_op args[6]
  14.8 1.3 %plan.1 = (s32[32,128]{1,0:T(8,128)S(1)}, s32[2]{0:T(128)S(1)}, s32[4,16]{1,0:T(4,128)S(1)}, f32[1]{0:T(128)}) custom-call(s32[40]{0:T(128)S(1)} %copy-done.8, f32[40]{0:T(128)S(1)} %copy-done.9, s32[4,40,16]{2,1,0:T(8,128)S(1)} %copy.29.rows_ref, s32[168]{0:T(256)S(1)} %copy-done.7), custom_call_target="tpu_custom_call" | custom-call | bytes 10800000 | tf_op jit(solution)/shard_map/plan/pallas_call | solution.py:548
  16.2 0.8 %collective-permute-done.2.edges = f32[8,128]{1,0:T(8,128)S(1)} collective-permute-done((f32[8,128]{1,0:T(8,128)S(1)}, f32[8,128]{1,0:T(8,128)S(1)}, u32[]{:S(2)}, u32[]{:S(2)}) %collective-permute-start.2) | collective-permute-done | bytes 4128 | tf_op jit(solution)/shard_map/ppermute | solution.py:627
  17.7 1.2 %collective-permute-done.3.second = f32[1,24,128]{2,1,0:T(8,128)S(1)} collective-permute-done((f32[1,24,128]{2,1,0:T(8,128)S(1)}, f32[1,24,128]{2,1,0:T(8,128)S(1)}, u32[]{:S(2)}, u32[]{:S(2)}) %collective-permute-start.3) | collective-permute-done | bytes 12320 | tf_op jit(solution)/shard_map/ppermute | solution.py:564
  19.6 2.2 %collective-permute-start.4 = (f32[304,128]{1,0:T(8,128)S(1)}, f32[304,128]{1,0:T(8,128)S(1)}, u32[]{:S(2)}, u32[]{:S(2)}) collective-permute-start(f32[304,128]{1,0:T(8,128)S(1)} %pack.1.rest_0_), channel_id=1, source_target_pairs={{0,1},{1,0},{2,3},{3,2},{4,5},{5,4},{6,7},{7,6},{8,9},{9,8},{10,11... | collective-permute-start | bytes 466952 | tf_op jit(solution)/shard_map/ppermute | solution.py:689
  21.8 3.8 %collective-permute-done.5.second = f32[2,24,128]{2,1,0:T(8,128)S(1)} collective-permute-done((f32[2,24,128]{2,1,0:T(8,128)S(1)}, f32[2,24,128]{2,1,0:T(8,128)S(1)}, u32[]{:S(2)}, u32[]{:S(2)}) %collective-permute-start.5) | collective-permute-done | bytes 24608 | tf_op jit(solution)/shard_map/ppermute | solution.py:566
  25.6 0.7 %collective-permute-start.6 = (f32[4,24,128]{2,1,0:T(8,128)S(1)}, f32[4,24,128]{2,1,0:T(8,128)S(1)}, u32[]{:S(2)}, u32[]{:S(2)}) collective-permute-start(f32[4,24,128]{2,1,0:T(8,128)S(1)} %stack.5.first), channel_id=1, source_target_pairs={{0,96},{2,98},{4,100},{6,102},{8,104},{10,106},{12,108},{14,110},{... | collective-permute-start | bytes 147464 | tf_op jit(solution)/shard_map/ppermute | solution.py:568
  26.4 4.6 %collective-permute-done.6.second = f32[4,24,128]{2,1,0:T(8,128)S(1)} collective-permute-done((f32[4,24,128]{2,1,0:T(8,128)S(1)}, f32[4,24,128]{2,1,0:T(8,128)S(1)}, u32[]{:S(2)}, u32[]{:S(2)}) %collective-permute-start.6) | collective-permute-done | bytes 49184 | tf_op jit(solution)/shard_map/ppermute | solution.py:568
  31.1 2.6 %bulk_load.1 = (f32[3,2,536,128]{3,2,1,0:T(8,128)S(1)}, f32[3,2,528,128]{3,2,1,0:T(8,128)S(1)}, f32[4,2,528,128]{3,2,1,0:T(8,128)S(1)}) custom-call(f32[3,512,128]{2,1,0:T(8,128)S(1)} %copy-done, f32[3,512,128]{2,1,0:T(8,128)S(1)} %copy-done.1, f32[512,128]{1,0:T(8,128)S(1)} %copy-done.2, f32[512,128]{1,0:T(8,128)S(1)} %copy-done.3, ...), custom_call_target="tpu_custom_call" | custom-call | bytes 7200000 | tf_op jit(solution)/shard_map/bulk_load/pallas_call | solution.py:548
  33.8 0.9 %window_load.1 = (f32[3,2,72,128]{3,2,1,0:T(8,128)S(1)}, f32[3,2,64,128]{3,2,1,0:T(8,128)S(1)}, f32[4,2,64,128]{3,2,1,0:T(8,128)S(1)}) custom-call(s32[2]{0:T(128)S(1)} %get-tuple-element.58.where_ref, f32[3,512,128]{2,1,0:T(8,128)S(1)} %copy-done, f32[3,512,128]{2,1,0:T(8,128)S(1)} %copy-done.1, f32[512,128]{1,0:T(8,128)S(1)} %copy-done.2, ...), custom_call_target="tpu_custom_call" | custom-call | bytes 2880000 | tf_op jit(solution)/shard_map/window_load/pallas_call | solution.py:548
  36.0 0.8 %bulk_step.13 = (f32[3,2,536,128]{3,2,1,0:T(8,128)S(1)}, f32[3,2,528,128]{3,2,1,0:T(8,128)S(1)}) custom-call(f32[16,128]{1,0:T(8,128)S(1)} %dynamic-slice_bitcast_fusion.table, f32[3,2,536,128]{3,2,1,0:T(8,128)S(1)} %get-tuple-element.62.rest_1_.state, f32[3,2,528,128]{3,2,1,0:T(8,128)S(1)} %get-tuple-element.63.vels, ...), custom_call_target="tpu_custom_call", output_to_operand_aliasing={{0}: (4, {}), {1}: (5, {})} | custom-call | bytes 2879999 | tf_op jit(solution)/shard_map/bulk_step/pallas_call | solution.py:548
  36.8 0.8 %bulk_step.14 = (f32[3,2,536,128]{3,2,1,0:T(8,128)S(1)}, f32[3,2,528,128]{3,2,1,0:T(8,128)S(1)}) custom-call(f32[16,128]{1,0:T(8,128)S(1)} %dynamic-slice_bitcast_fusion.table, f32[3,2,536,128]{3,2,1,0:T(8,128)S(1)} %get-tuple-element.62.rest_1_.state, f32[3,2,528,128]{3,2,1,0:T(8,128)S(1)} %get-tuple-element.63.vels, ...), custom_call_target="tpu_custom_call", output_to_operand_aliasing={{0}: (4, {}), {1}: (5, {})} | custom-call | bytes 2879999 | tf_op jit(solution)/shard_map/bulk_step/pallas_call | solution.py:548
  37.6 2.7 %collective-permute-done.8.got = f32[2,24,128]{2,1,0:T(8,128)S(1)} collective-permute-done((f32[2,24,128]{2,1,0:T(8,128)S(1)}, f32[2,24,128]{2,1,0:T(8,128)S(1)}, u32[]{:S(2)}, u32[]{:S(2)}) %collective-permute-start.8) | collective-permute-done | bytes 24608 | tf_op jit(solution)/shard_map/ppermute | solution.py:577
  41.0 0.8 %bulk_step.16 = (f32[3,2,536,128]{3,2,1,0:T(8,128)S(1)}, f32[3,2,528,128]{3,2,1,0:T(8,128)S(1)}) custom-call(f32[16,128]{1,0:T(8,128)S(1)} %dynamic-slice_bitcast_fusion.table, f32[3,2,536,128]{3,2,1,0:T(8,128)S(1)} %get-tuple-element.73.rest_0_.state, f32[3,2,528,128]{3,2,1,0:T(8,128)S(1)} %get-tuple-element.74.vels, ...), custom_call_target="tpu_custom_call", output_to_operand_aliasing={{0}: (4, {}), {1}: (5, {})} | custom-call | bytes 2879999 | tf_op jit(solution)/shard_map/bulk_step/pallas_call | solution.py:548
  41.8 0.8 %bulk_step.17 = (f32[3,2,536,128]{3,2,1,0:T(8,128)S(1)}, f32[3,2,528,128]{3,2,1,0:T(8,128)S(1)}) custom-call(f32[16,128]{1,0:T(8,128)S(1)} %dynamic-slice_bitcast_fusion.table, f32[3,2,536,128]{3,2,1,0:T(8,128)S(1)} %get-tuple-element.73.rest_0_.state, f32[3,2,528,128]{3,2,1,0:T(8,128)S(1)} %get-tuple-element.74.vels, ...), custom_call_target="tpu_custom_call", output_to_operand_aliasing={{0}: (4, {}), {1}: (5, {})} | custom-call | bytes 2879999 | tf_op jit(solution)/shard_map/bulk_step/pallas_call | solution.py:548
  42.6 1.4 %collective-permute-done.9.handed = f32[1,24,128]{2,1,0:T(8,128)S(1)} collective-permute-done((f32[1,24,128]{2,1,0:T(8,128)S(1)}, f32[1,24,128]{2,1,0:T(8,128)S(1)}, u32[]{:S(2)}, u32[]{:S(2)}) %collective-permute-start.9) | collective-permute-done | bytes 12320 | tf_op jit(solution)/shard_map/ppermute | solution.py:582
  44.0 2.3 %window.1 = (f32[3,2,72,128]{3,2,1,0:T(8,128)S(1)}, f32[3,2,64,128]{3,2,1,0:T(8,128)S(1)}, f32[2,2,64,128]{3,2,1,0:T(8,128)S(1)}, f32[1,16,128]{2,1,0:T(8,128)S(1)}) custom-call(s32[4,16]{1,0:T(4,128)S(1)} %get-tuple-element.83.list_ref, f32[1]{0:T(128)} %get-tuple-element.84.lift_ref, s32[32,128]{1,0:T(8,128)S(1)} %get-tuple-element.61.rest_0_.plan, ...), custom_call_target="tpu_custom_call" | custom-call | bytes 7200000 | tf_op jit(solution)/shard_map/window/pallas_call | solution.py:548
  46.6 0.9 %collective-permute-done.10.second = f32[1,16,128]{2,1,0:T(8,128)S(1)} collective-permute-done((f32[1,16,128]{2,1,0:T(8,128)S(1)}, f32[1,16,128]{2,1,0:T(8,128)S(1)}, u32[]{:S(2)}, u32[]{:S(2)}) %collective-permute-start.10) | collective-permute-done | bytes 8224 | tf_op jit(solution)/shard_map/ppermute | solution.py:564
  48.3 0.8 %bulk_step.19 = (f32[3,2,536,128]{3,2,1,0:T(8,128)S(1)}, f32[3,2,528,128]{3,2,1,0:T(8,128)S(1)}) custom-call(f32[16,128]{1,0:T(8,128)S(1)} %dynamic-slice_bitcast_fusion.table, f32[3,2,536,128]{3,2,1,0:T(8,128)S(1)} %get-tuple-element.81.rest_0_.state, f32[3,2,528,128]{3,2,1,0:T(8,128)S(1)} %get-tuple-element.82.vels, ...), custom_call_target="tpu_custom_call", output_to_operand_aliasing={{0}: (4, {}), {1}: (5, {})} | custom-call | bytes 2879999 | tf_op jit(solution)/shard_map/bulk_step/pallas_call | solution.py:548
  49.1 2.3 %collective-permute-done.11.second = f32[2,16,128]{2,1,0:T(8,128)S(1)} collective-permute-done((f32[2,16,128]{2,1,0:T(8,128)S(1)}, f32[2,16,128]{2,1,0:T(8,128)S(1)}, u32[]{:S(2)}, u32[]{:S(2)}) %collective-permute-start.11) | collective-permute-done | bytes 16416 | tf_op jit(solution)/shard_map/ppermute | solution.py:566
  51.3 0.8 %collective-permute-start.12 = (f32[4,16,128]{2,1,0:T(8,128)S(1)}, f32[4,16,128]{2,1,0:T(8,128)S(1)}, u32[]{:S(2)}, u32[]{:S(2)}) collective-permute-start(f32[4,16,128]{2,1,0:T(8,128)S(1)} %stack.7.rest_2_.rest_0_.first), channel_id=1, source_target_pairs={{0,96},{2,98},{4,100},{6,102},{8,104},{10,106},{12,108},{14,110},{... | collective-permute-start | bytes 98312 | tf_op jit(solution)/shard_map/ppermute | solution.py:568
  52.1 0.8 %bulk_step.20 = (f32[3,2,536,128]{3,2,1,0:T(8,128)S(1)}, f32[3,2,528,128]{3,2,1,0:T(8,128)S(1)}) custom-call(f32[16,128]{1,0:T(8,128)S(1)} %dynamic-slice_bitcast_fusion.table, f32[3,2,536,128]{3,2,1,0:T(8,128)S(1)} %get-tuple-element.81.rest_0_.state, f32[3,2,528,128]{3,2,1,0:T(8,128)S(1)} %get-tuple-element.82.vels, ...), custom_call_target="tpu_custom_call", output_to_operand_aliasing={{0}: (4, {}), {1}: (5, {})} | custom-call | bytes 2879999 | tf_op jit(solution)/shard_map/bulk_step/pallas_call | solution.py:548
  53.6 2.9 %collective-permute-done.12.second = f32[4,16,128]{2,1,0:T(8,128)S(1)} collective-permute-done((f32[4,16,128]{2,1,0:T(8,128)S(1)}, f32[4,16,128]{2,1,0:T(8,128)S(1)}, u32[]{:S(2)}, u32[]{:S(2)}) %collective-permute-start.12) | collective-permute-done | bytes 32800 | tf_op jit(solution)/shard_map/ppermute | solution.py:568
  56.8 0.8 %bulk_step.22 = (f32[3,2,536,128]{3,2,1,0:T(8,128)S(1)}, f32[3,2,528,128]{3,2,1,0:T(8,128)S(1)}) custom-call(f32[16,128]{1,0:T(8,128)S(1)} %dynamic-slice_bitcast_fusion.table, f32[3,2,536,128]{3,2,1,0:T(8,128)S(1)} %get-tuple-element.96.state, f32[3,2,528,128]{3,2,1,0:T(8,128)S(1)} %get-tuple-element.97.vels, ...), custom_call_target="tpu_custom_call", output_to_operand_aliasing={{0}: (4, {}), {1}: (5, {})} | custom-call | bytes 2879999 | tf_op jit(solution)/shard_map/bulk_step/pallas_call | solution.py:548
  57.6 0.8 %bulk_step.23 = (f32[3,2,536,128]{3,2,1,0:T(8,128)S(1)}, f32[3,2,528,128]{3,2,1,0:T(8,128)S(1)}) custom-call(f32[16,128]{1,0:T(8,128)S(1)} %dynamic-slice_bitcast_fusion.table, f32[3,2,536,128]{3,2,1,0:T(8,128)S(1)} %get-tuple-element.96.state, f32[3,2,528,128]{3,2,1,0:T(8,128)S(1)} %get-tuple-element.97.vels, ...), custom_call_target="tpu_custom_call", output_to_operand_aliasing={{0}: (4, {}), {1}: (5, {})} | custom-call | bytes 2879999 | tf_op jit(solution)/shard_map/bulk_step/pallas_call | solution.py:548
  58.4 2.1 %collective-permute-done.13.got = f32[4,16,128]{2,1,0:T(8,128)S(1)} collective-permute-done((f32[4,16,128]{2,1,0:T(8,128)S(1)}, f32[4,16,128]{2,1,0:T(8,128)S(1)}, u32[]{:S(2)}, u32[]{:S(2)}) %collective-permute-start.13) | collective-permute-done | bytes 32800 | tf_op jit(solution)/shard_map/ppermute | solution.py:572
  61.2 1.9 %bulk_store.1 = (f32[3,512,128]{2,1,0:T(8,128)}, f32[3,512,128]{2,1,0:T(8,128)}, f32[8,128]{1,0:T(8,128)S(1)}) custom-call(s32[2]{0:T(128)S(1)} %get-tuple-element.58.where_ref, f32[3,2,536,128]{3,2,1,0:T(8,128)S(1)} %get-tuple-element.103.rest_0_.state, f32[3,2,528,128]{3,2,1,0:T(8,128)S(1)} %get-tuple-element.104.vels, ...), custom_call_target="tpu_custom_call" | custom-call | bytes 7200000 | tf_op jit(solution)/shard_map/bulk_store/pallas_call | solution.py:548
  63.2 2.4 %collective-permute-done.14.got = f32[2,16,128]{2,1,0:T(8,128)S(1)} collective-permute-done((f32[2,16,128]{2,1,0:T(8,128)S(1)}, f32[2,16,128]{2,1,0:T(8,128)S(1)}, u32[]{:S(2)}, u32[]{:S(2)}) %collective-permute-start.14) | collective-permute-done | bytes 16416 | tf_op jit(solution)/shard_map/ppermute | solution.py:577
  66.2 3.0 %collective-permute-done.15.handed = f32[1,16,128]{2,1,0:T(8,128)S(1)} collective-permute-done((f32[1,16,128]{2,1,0:T(8,128)S(1)}, f32[1,16,128]{2,1,0:T(8,128)S(1)}, u32[]{:S(2)}, u32[]{:S(2)}) %collective-permute-start.15) | collective-permute-done | bytes 8224 | tf_op jit(solution)/shard_map/ppermute | solution.py:582
  (57 shorter events, 8.5 us)
Async XLA Ops:
  0.6 14.2 %copy-start.7 = (s32[168]{0:T(256)S(1)}, s32[168]{0:T(256)}, u32[]{:S(2)}) copy-start(s32[168]{0:T(256)} %constant.13.clone.static_ref) | copy-start | bytes 2020
  0.6 18.3 %copy-start = (f32[3,512,128]{2,1,0:T(8,128)S(1)}, f32[3,512,128]{2,1,0:T(8,128)}, u32[]{:S(2)}) copy-start(f32[3,512,128]{2,1,0:T(8,128)} %refs_0_.5) | copy-start | bytes 2359300
  0.7 18.3 %copy-start.1 = (f32[3,512,128]{2,1,0:T(8,128)S(1)}, f32[3,512,128]{2,1,0:T(8,128)}, u32[]{:S(2)}) copy-start(f32[3,512,128]{2,1,0:T(8,128)} %refs_1_.5) | copy-start | bytes 2359300
  0.7 18.3 %copy-start.2 = (f32[512,128]{1,0:T(8,128)S(1)}, f32[512,128]{1,0:T(8,128)}, u32[]{:S(2)}) copy-start(f32[512,128]{1,0:T(8,128)} %refs_2_.5) | copy-start | bytes 786436
  0.7 18.3 %copy-start.3 = (f32[512,128]{1,0:T(8,128)S(1)}, f32[512,128]{1,0:T(8,128)}, u32[]{:S(2)}) copy-start(f32[512,128]{1,0:T(8,128)} %refs_3_.5) | copy-start | bytes 786436
  0.7 14.1 %copy-start.9 = (f32[40]{0:T(128)S(1)}, f32[40]{0:T(128)}, u32[]{:S(2)}) copy-start(f32[40]{0:T(128)} %lift_ref.1) | copy-start | bytes 484
  0.7 14.1 %copy-start.8 = (s32[40]{0:T(128)S(1)}, s32[40]{0:T(128)}, u32[]{:S(2)}) copy-start(s32[40]{0:T(128)} %slot_ref.1) | copy-start | bytes 484
  2.7 16.2 %collective-permute-start = (f32[8,48,128]{2,1,0:T(8,128)}, f32[8,48,128]{2,1,0:T(8,128)S(1)}, u32[]{:S(2)}, u32[]{:S(2)}) collective-permute-start(f32[8,48,128]{2,1,0:T(8,128)} %get-tuple-element.59), channel_id=1, source_target_pairs={{0,2},{2,0},{4,6},{6,4},{8,10},{10,8},{12,14},{14,12},{16,18},{18,... | collective-permute-start | bytes 589832 | tf_op jit(solution)/shard_map/ppermute | solution.py:642
  2.8 16.1 %collective-permute-start.1 = (f32[8,48,128]{2,1,0:T(8,128)}, f32[8,48,128]{2,1,0:T(8,128)S(1)}, u32[]{:S(2)}, u32[]{:S(2)}) collective-permute-start(f32[8,48,128]{2,1,0:T(8,128)} %get-tuple-element.60), channel_id=1, source_target_pairs={{2,4},{4,2},{6,8},{8,6},{10,12},{12,10},{14,16},{16,14},{18,20},{2... | collective-permute-start | bytes 589832 | tf_op jit(solution)/shard_map/ppermute | solution.py:643
  10.4 0.7 copy-start.4
  11.2 5.8 %collective-permute-start.2 = (f32[8,128]{1,0:T(8,128)S(1)}, f32[8,128]{1,0:T(8,128)S(1)}, u32[]{:S(2)}, u32[]{:S(2)}) collective-permute-start(f32[8,128]{1,0:T(8,128)S(1)} %pad_edge.1), channel_id=1, source_target_pairs={{0,1},{1,0},{2,3},{3,2},{4,5},{5,4},{6,7},{7,6},{8,9},{9,8},{10,11... | collective-permute-start | bytes 12296 | tf_op jit(solution)/shard_map/ppermute | solution.py:627
  17.0 0.7 copy-start.5
  17.7 1.2 %collective-permute-start.3 = (f32[1,24,128]{2,1,0:T(8,128)S(1)}, f32[1,24,128]{2,1,0:T(8,128)S(1)}, u32[]{:S(2)}, u32[]{:S(2)}) collective-permute-start(f32[1,24,128]{2,1,0:T(8,128)S(1)} %pad_extend.1.first), channel_id=1, source_target_pairs={{0,2},{2,0},{4,6},{6,4},{8,10},{10,8},{12,14},{14,12},{16,18},{18,... | collective-permute-start | bytes 36872 | tf_op jit(solution)/shard_map/ppermute | solution.py:564
  19.6 11.4 %collective-permute-start.4 = (f32[304,128]{1,0:T(8,128)S(1)}, f32[304,128]{1,0:T(8,128)S(1)}, u32[]{:S(2)}, u32[]{:S(2)}) collective-permute-start(f32[304,128]{1,0:T(8,128)S(1)} %pack.1.rest_0_), channel_id=1, source_target_pairs={{0,1},{1,0},{2,3},{3,2},{4,5},{5,4},{6,7},{7,6},{8,9},{9,8},{10,11... | collective-permute-start | bytes 466952 | tf_op jit(solution)/shard_map/ppermute | solution.py:689
  21.8 3.8 %collective-permute-start.5 = (f32[2,24,128]{2,1,0:T(8,128)S(1)}, f32[2,24,128]{2,1,0:T(8,128)S(1)}, u32[]{:S(2)}, u32[]{:S(2)}) collective-permute-start(f32[2,24,128]{2,1,0:T(8,128)S(1)} %stack.4.refs_6_.first), channel_id=1, source_target_pairs={{0,32},{2,34},{4,36},{6,38},{8,40},{10,42},{12,44},{14,46},{16,48}... | collective-permute-start | bytes 73736 | tf_op jit(solution)/shard_map/ppermute | solution.py:566
  25.6 5.3 %collective-permute-start.6 = (f32[4,24,128]{2,1,0:T(8,128)S(1)}, f32[4,24,128]{2,1,0:T(8,128)S(1)}, u32[]{:S(2)}, u32[]{:S(2)}) collective-permute-start(f32[4,24,128]{2,1,0:T(8,128)S(1)} %stack.5.first), channel_id=1, source_target_pairs={{0,96},{2,98},{4,100},{6,102},{8,104},{10,106},{12,108},{14,110},{... | collective-permute-start | bytes 147464 | tf_op jit(solution)/shard_map/ppermute | solution.py:568
  31.0 4.2 %collective-permute-start.7 = (f32[4,24,128]{2,1,0:T(8,128)S(1)}, f32[4,24,128]{2,1,0:T(8,128)S(1)}, u32[]{:S(2)}, u32[]{:S(2)}) collective-permute-start(f32[4,24,128]{2,1,0:T(8,128)S(1)} %get-tuple-element.66), channel_id=1, source_target_pairs={{0,8},{2,10},{4,12},{6,14},{8,0},{10,2},{12,4},{14,6},{16,24},{18,... | collective-permute-start | bytes 147464 | tf_op jit(solution)/shard_map/ppermute | solution.py:572
  34.6 0.7 %copy-start.10 = (f32[2,16,128]{2,1,0:T(8,128)S(1)}, f32[2,16,128]{2,1,0:T(8,128)}, u32[]{:S(2)}) copy-start(f32[2,16,128]{2,1,0:T(8,128)} %constant.12.clone) | copy-start | bytes 49156
  35.2 5.1 %collective-permute-start.8 = (f32[2,24,128]{2,1,0:T(8,128)S(1)}, f32[2,24,128]{2,1,0:T(8,128)S(1)}, u32[]{:S(2)}, u32[]{:S(2)}) collective-permute-start(f32[2,24,128]{2,1,0:T(8,128)S(1)} %get-tuple-element.68.rest_0_.rest_2_), channel_id=1, source_target_pairs={{0,24},{2,26},{4,28},{6,30},{8,16},{10,18},{12,20},{14,22},{16,8},... | collective-permute-start | bytes 73736 | tf_op jit(solution)/shard_map/ppermute | solution.py:577
  40.3 3.7 %collective-permute-start.9 = (f32[1,24,128]{2,1,0:T(8,128)S(1)}, f32[1,24,128]{2,1,0:T(8,128)S(1)}, u32[]{:S(2)}, u32[]{:S(2)}) collective-permute-start(f32[1,24,128]{2,1,0:T(8,128)S(1)} %get-tuple-element.76.rest_0_.rest_2_), channel_id=1, source_target_pairs={{0,4},{2,6},{4,0},{6,2},{8,12},{10,14},{12,8},{14,10},{16,20},{18,... | collective-permute-start | bytes 36872 | tf_op jit(solution)/shard_map/ppermute | solution.py:582
  46.3 1.3 %collective-permute-start.10 = (f32[1,16,128]{2,1,0:T(8,128)S(1)}, f32[1,16,128]{2,1,0:T(8,128)S(1)}, u32[]{:S(2)}, u32[]{:S(2)}) collective-permute-start(f32[1,16,128]{2,1,0:T(8,128)S(1)} %get-tuple-element.88.first), channel_id=1, source_target_pairs={{0,2},{2,0},{4,6},{6,4},{8,10},{10,8},{12,14},{14,12},{16,18},{18,... | collective-permute-start | bytes 24584 | tf_op jit(solution)/shard_map/ppermute | solution.py:564
  47.6 3.7 %collective-permute-start.11 = (f32[2,16,128]{2,1,0:T(8,128)S(1)}, f32[2,16,128]{2,1,0:T(8,128)S(1)}, u32[]{:S(2)}, u32[]{:S(2)}) collective-permute-start(f32[2,16,128]{2,1,0:T(8,128)S(1)} %stack.6.rest_0_.rest_2_.first), channel_id=1, source_target_pairs={{0,32},{2,34},{4,36},{6,38},{8,40},{10,42},{12,44},{14,46},{16,48}... | collective-permute-start | bytes 49160 | tf_op jit(solution)/shard_map/ppermute | solution.py:566
  51.3 5.1 %collective-permute-start.12 = (f32[4,16,128]{2,1,0:T(8,128)S(1)}, f32[4,16,128]{2,1,0:T(8,128)S(1)}, u32[]{:S(2)}, u32[]{:S(2)}) collective-permute-start(f32[4,16,128]{2,1,0:T(8,128)S(1)} %stack.7.rest_2_.rest_0_.first), channel_id=1, source_target_pairs={{0,96},{2,98},{4,100},{6,102},{8,104},{10,106},{12,108},{14,110},{... | collective-permute-start | bytes 98312 | tf_op jit(solution)/shard_map/ppermute | solution.py:568
  56.5 4.0 %collective-permute-start.13 = (f32[4,16,128]{2,1,0:T(8,128)S(1)}, f32[4,16,128]{2,1,0:T(8,128)S(1)}, u32[]{:S(2)}, u32[]{:S(2)}) collective-permute-start(f32[4,16,128]{2,1,0:T(8,128)S(1)} %get-tuple-element.100.rest_2_), channel_id=1, source_target_pairs={{0,8},{2,10},{4,12},{6,14},{8,0},{10,2},{12,4},{14,6},{16,24},{18,... | collective-permute-start | bytes 98312 | tf_op jit(solution)/shard_map/ppermute | solution.py:572
  60.5 5.0 %collective-permute-start.14 = (f32[2,16,128]{2,1,0:T(8,128)S(1)}, f32[2,16,128]{2,1,0:T(8,128)S(1)}, u32[]{:S(2)}, u32[]{:S(2)}) collective-permute-start(f32[2,16,128]{2,1,0:T(8,128)S(1)} %get-tuple-element.106.rest_0_), channel_id=1, source_target_pairs={{0,24},{2,26},{4,28},{6,30},{8,16},{10,18},{12,20},{14,22},{16,8},... | collective-permute-start | bytes 49160 | tf_op jit(solution)/shard_map/ppermute | solution.py:577
  61.2 8.0 %copy-start.6 = (f32[1,16,128]{2,1,0:T(8,128)S(1)}, f32[1,16,128]{2,1,0:T(8,128)}, u32[]{:S(2)}) copy-start(f32[1,16,128]{2,1,0:T(8,128)} %before.1) | copy-start | bytes 24580
  65.6 3.7 %collective-permute-start.15 = (f32[1,16,128]{2,1,0:T(8,128)S(1)}, f32[1,16,128]{2,1,0:T(8,128)S(1)}, u32[]{:S(2)}, u32[]{:S(2)}) collective-permute-start(f32[1,16,128]{2,1,0:T(8,128)S(1)} %get-tuple-element.112), channel_id=1, source_target_pairs={{0,4},{2,6},{4,0},{6,2},{8,12},{10,14},{12,8},{14,10},{16,20},{18,... | collective-permute-start | bytes 24584 | tf_op jit(solution)/shard_map/ppermute | solution.py:582

commit v5 on v4

--- a/solution.py
+++ b/solution.py
@@ -95,8 +95,9 @@
 
 
 def plan_kernel(
-    arc_count, own, slot_ref, lift_ref, rows_ref, static_ref, plan, where_ref, list_ref, lift_out, source
+    arc_count, own, slot_ref, lift_ref, rows_ref, static_ref, *rest
 ):
+    plan, where_ref, list_ref, lift_out, source = rest[-5:]
     me = lax.axis_index("arc")
     y, z, x, c = arc_digits(me)
     rollers = slot_ref.shape[0]
@@ -336,21 +337,17 @@
         lax.fori_loop(begin // (8 * group), end // (8 * group), body, carry)
 
 
-def pad_edge_kernel(pad, out):
+def pad_edge_kernel(plan, kept, got, *rest):
+    out, edges = rest[-2:]
+    pad = jnp.where(plan[SAME_X : SAME_X + 1, :] > 0, kept[0], got[0])
+    out[...] = pad
     lane = lax.broadcasted_iota(jnp.int32, (1, LANES), 1) // (2 * EDGE)
     total = jnp.zeros((1, LANES), jnp.float32)
-    slots = pad.shape[1]
+    slots = pad.shape[0]
     for m in range(slots):
-        moved = pltpu.roll(pad[0, m : m + 1, :], LANES - EDGE - 2 * EDGE * m, 1)
+        moved = pltpu.roll(pad[m : m + 1, :], LANES - EDGE - 2 * EDGE * m, 1)
         total = jnp.where(lane == slots - 1 - m, moved, total)
-    out[...] = jnp.broadcast_to(total, out.shape)
-
-
-def pad_extend_kernel(pad, edges, *rest):
-    out = rest[-1]
-    slots = pad.shape[1]
-    out[0, :slots, :] = pad[0]
-    out[0, slots:, :] = edges[...]
+    edges[...] = jnp.broadcast_to(total, edges.shape)
 
 
 def window_load_kernel(half, base, cycle_total, where_ref, *refs):
@@ -399,17 +396,14 @@
 
 
 def window_kernel(
-    list_ref, lift_ref, plan, table, state, vels, coef, pads, handed, *rest
+    list_ref, lift_ref, table, state, vels, coef, pads, edges, *rest
 ):
     state_out, vels_out, push, pad_out, spare, vels_spare, taken, given, held = rest[-9:]
-    same = plan[SAME_X : SAME_X + 1, :] > 0
-    slots = held.shape[1]
     lane = lax.broadcasted_iota(jnp.int32, (8, LANES), 1)
     keep = (lane < EDGE) | (lane >= LANES - EDGE)
-    both = jnp.where(same, pads[0], handed[0])
-    held[0] = both[:slots]
+    held[0] = pads[...]
     for part in range(2):
-        moved = pltpu.roll(both[slots:], EDGE + 64 * part, 1, stride=2 * EDGE, stride_axis=0)
+        moved = pltpu.roll(edges[...], EDGE + 64 * part, 1, stride=2 * EDGE, stride_axis=0)
         held[1, 8 * part : 8 * part + 8, :] = jnp.where(keep, moved, 0.0)
     lift = lift_ref[0]
     clear_tail(spare, WIN)
@@ -559,15 +553,17 @@
     return result[0] if single else result
 
 
-def route(value, plan, way, between):
+def route(value, kept, way, between):
     shape = value.shape[1:]
     got = lax.ppermute(value, "arc", flips(c=1))
     held = call(stack_kernel, "stack", real(2, *shape), (value, got), after=between(0, value))
     got = lax.ppermute(held, "arc", flips(y=1))
     held = call(stack_kernel, "stack", real(4, *shape), (held, got), after=between(1, held))
     got = lax.ppermute(held, "arc", flips(y=3))
+    ready = between(2, held)
+    plan = kept["plan"][0]
     keep, send = call(
-        functools.partial(pick_kernel, way), "pick", (real(4, *shape),) * 2, (plan, held, got), after=between(2, held)
+        functools.partial(pick_kernel, way), "pick", (real(4, *shape),) * 2, (plan, held, got), after=ready
     )
     got = lax.ppermute(send, "arc", flips(z=1))
     keep, send = call(
@@ -623,36 +619,36 @@
     def room(count):
         return [pltpu.VMEM(shape.shape, jnp.float32) for shape in buffers(count)[:2]]
 
-    pad_edges = call(pad_edge_kernel, "pad_edge", real(8, LANES), (pad_state,))
-    pad_edges = lax.ppermute(pad_edges, "circ", swap)
+    outward = [pair for i in range(1, arc_count, 2) for pair in ((i, (i + 1) % arc_count), ((i + 1) % arc_count, i))]
+
     inner, outer = call(
-        functools.partial(edge_kernel, HALO), "edge",
-        (real(8, HALO, LANES), real(8, HALO, LANES)), fields,
+        functools.partial(edge_kernel, HALO), "edge", (real(8, HALO, LANES), real(8, HALO, LANES)), fields,
         in_specs=[HBM] * 4, scratch=[pltpu.SemaphoreType.DMA((8,))], micros=2.0, limit=MOST,
     )
-    plan, where, rows_in, lift = call(
-        functools.partial(plan_kernel, arc_count, cycle_dev), "plan",
-        (whole(2 * PLAN, LANES), whole(2), whole(STEPS, slots), real(1)),
-        (roller_slot, roller_lift, contact_rows, jnp.asarray(static)),
-        in_specs=[SMEM, SMEM, VMEM, SMEM], out_specs=[VMEM, SMEM, VMEM, SMEM],
-        scratch=[pltpu.SMEM((arc_count,), jnp.int32)], micros=3.0,
-    )
-
-    outward = [pair for i in range(1, arc_count, 2) for pair in ((i, (i + 1) % arc_count), ((i + 1) % arc_count, i))]
-    inner = lax.ppermute(inner, "arc", flips(c=1))
-    outer = lax.ppermute(outer, "arc", outward)
+    ends = lax.ppermute(inner, "arc", flips(c=1)), lax.ppermute(outer, "arc", outward)
+
+    def make_plan(value):
+        kept["plan"] = call(
+            functools.partial(plan_kernel, arc_count, cycle_dev), "plan",
+            (whole(2 * PLAN, LANES), whole(2), whole(STEPS, slots), real(1)),
+            (roller_slot, roller_lift, contact_rows, jnp.asarray(static)),
+            in_specs=[SMEM, SMEM, VMEM, SMEM], out_specs=[VMEM, SMEM, VMEM, SMEM],
+            scratch=[pltpu.SMEM((arc_count,), jnp.int32)], micros=1.5, after=(value,),
+        )
+        return kept["plan"][:1]
+
     kept = {"done": 0}
 
     def load_window():
         return call(
             functools.partial(window_load_kernel, half, base, cycle_total), "window_load", buffers(WIN),
-            (where, *fields, inner, outer, kept["columns"]), in_specs=[SMEM] + [VMEM] * 7, micros=0.8,
+            (kept["plan"][1], *fields, *ends, kept["columns"]), in_specs=[SMEM] + [VMEM] * 7, micros=0.8,
         )
 
     def load_bulk():
         return call(
             functools.partial(bulk_load_kernel, half, base, cycle_total, rows), "bulk_load", buffers(rows),
-            (*fields, inner, outer, kept["columns"]), micros=2.0,
+            (*fields, *ends, kept["columns"]), micros=2.0,
         )
 
     def step_bulk(value, count):
@@ -675,7 +671,7 @@
         outs = call(
             functools.partial(bulk_store_kernel, rows), "bulk_store",
             (real(3, cycle_dev, LANES), real(3, cycle_dev, LANES), real(8, LANES)),
-            (where, state, vels, kept["last"], value),
+            (kept["plan"][1], state, vels, kept["last"], value),
             in_specs=[SMEM] + [VMEM] * 3 + [ANY], out_specs=[HBM] * 2 + [VMEM],
             scratch=[pltpu.VMEM((6, cycle_dev, LANES), jnp.float32), pltpu.SemaphoreType.DMA((2 * CHUNKS,))],
             micros=2.0,
@@ -685,26 +681,31 @@
 
     def going(stage, value):
         if stage == 1:
-            pack = call(pack_kernel, "pack", real(half, LANES), (*fields, inner, outer), micros=2.0, after=(value,))
+            return make_plan(value)
+        if stage == 2:
+            pack = call(pack_kernel, "pack", real(half, LANES), (*fields, *ends), micros=2.0, after=(value,))
             kept["columns"] = lax.ppermute(pack, "circ", swap)
             return (pack,)
-        if stage == 3:
+        if stage == 6:
             kept["window"] = load_window()
             kept["bulk"] = load_bulk()
             return (kept["window"][0], kept["bulk"][0])
-        return step_bulk(value, 3) if stage > 3 else ()
-
-    value = call(
-        pad_extend_kernel, "pad_extend", real(1, slots + 8, LANES), (pad_state, pad_edges), after=(plan,)
-    )
-    pads, handed, done = route(value, plan, 0, going)
-
+        return ()
+
+    pads, handed, _ = route(pad_state, kept, 0, going)
+    pads, edges = call(
+        pad_edge_kernel, "pad_edge", (real(slots, LANES), real(8, LANES)), (kept["plan"][0], pads, handed)
+    )
+    done = going(6, edges)
+    edges = lax.ppermute(edges, "circ", swap)
+
+    plan, _, rows_in, lift = kept["plan"]
     win_state, win_vels, win_coef = kept["window"]
     win_state, win_vels, push, pad_new = call(
         window_kernel, "window", (*buffers(WIN)[:2], real(2, 2, WIN, LANES), real(1, slots, LANES)),
-        (rows_in, lift, plan, table, win_state, win_vels, win_coef, pads, handed),
+        (rows_in, lift, table, win_state, win_vels, win_coef, pads, edges),
         after=done,
-        in_specs=[SMEM] * 2 + [VMEM] * 7,
+        in_specs=[SMEM] * 2 + [VMEM] * 6,
         scratch=room(WIN)
         + [
             pltpu.VMEM((2, 2, slots, LANES), jnp.float32),
@@ -723,9 +724,9 @@
             return (kept["last"],)
         if stage == 4:
             return store_bulk(value)
-        return step_bulk(value, 2) if stage < 4 else ()
-
-    pads, handed, done = route(pad_new, plan, 1, coming)
+        return step_bulk(value, 4) if stage < 4 else ()
+
+    pads, handed, done = route(pad_new, kept, 1, coming)
     pad_result = call(last_kernel, "last", real(1, slots, LANES), (plan, pads, handed, pad_state), after=done)
     return *kept["outs"], pad_result
 

time: 70.2 us -> 66.5 us (0.947)
  waiting for transfers between devices: 28.5 us -> 26.5 us
  starting transfers between devices: 16.2 us -> 15.3 us
  local copies, waits for them, and re-layouts: 2.34 us -> 1.58 us
    ppermute x2, waiting for transfers between devices: 6.08 us -> 2.28 us  [route(): got = lax.ppermute(held, 'arc', flips(y=1))]
    ppermute x2, waiting for transfers between devices: 4.39 us -> 7.28 us  [route(): return (keep, lax.ppermute(send, 'arc', flips(x=1)), between(5, send))]
    ppermute x2, waiting for transfers between devices: 5.03 us -> 7.89 us  [route(): got = lax.ppermute(send, 'arc', flips(z=3))]
    ppermute x2, waiting for transfers between devices: 7.41 us -> 4.88 us  [route(): got = lax.ppermute(held, 'arc', flips(y=3))]
    ppermute x3, waiting for transfers between devices: 0.82 us -> 0.01 us  [the longest x1 0.01 us: local(): edges = lax.ppermute(edges, 'circ', swap)]
    unnamed x23 -> x21, local copies, waits for them, and re-layouts: 2.34 us -> 1.57 us
    ppermute x2, waiting for transfers between devices: 2.62 us -> 1.89 us  [route(): got = lax.ppermute(send, 'arc', flips(z=1))]
    pallas_call x33 -> x32, Pallas kernels: 21.9 us -> 21.9 us  [call(): pl.pallas_call(kernel, out_shape=shapes, in_specs=list(in_specs or [VMEM]...]
  transfers between devices with their start and end apart: 16 -> 16, of which waited for: 13 -> 12; matrix products, arithmetic and copies ran while one was open for 1% -> 1% of each run, Pallas kernels for 23% -> 25%
where the time goes in v5:
time: 66.5 us; the launch traced here: 66.3 us
  waiting for transfers between devices  26.5 us (40%)
  Pallas kernels  21.9 us (33%)
  starting transfers between devices  15.3 us (23%)
  local copies, waits for them, and re-layouts  1.58 us (2%)
  between operations  0.99 us (1%)
    pallas_call x32, Pallas kernels, call(): pl.pallas_call(kernel, out_shape=shapes, in_specs=list(in_specs or [VMEM]...  21.9 us
    ppermute x2, waiting for transfers between devices, route(): got = lax.ppermute(send, 'arc', flips(z=3))  7.89 us
    ppermute x1, starting transfers between devices, local(): lax.ppermute(outer, 'arc', outward)  7.6 us
    ppermute x2, waiting for transfers between devices, route(): return (keep, lax.ppermute(send, 'arc', flips(x=1)), between(5, send))  7.28 us
    ppermute x2, waiting for transfers between devices, route(): got = lax.ppermute(held, 'arc', flips(y=3))  4.88 us
    ppermute x1, starting transfers between devices, local(): edges = lax.ppermute(edges, 'circ', swap)  2.81 us
    ppermute x1, starting transfers between devices, going(): kept['columns'] = lax.ppermute(pack, 'circ', swap)  2.81 us
    ppermute x2, waiting for transfers between devices, route(): got = lax.ppermute(value, 'arc', flips(c=1))  2.31 us
  transfers between devices with their start and end apart: 16, of which 12 were waited for; matrix products, arithmetic and copies ran while one was open for 1% of the time, Pallas kernels for 25%

profile of v5, /device:TPU:0, one launch (start us, length us, event | category | flops | bytes accessed | tf_op | source)
XLA Modules:
  0.0 66.3 jit_solution(16825125993718740488)
XLA Ops:
  0.7 2.0 %edge.1 = (f32[8,48,128]{2,1,0:T(8,128)}, f32[8,48,128]{2,1,0:T(8,128)}) custom-call(f32[3,512,128]{2,1,0:T(8,128)} %refs_0_.5, f32[3,512,128]{2,1,0:T(8,128)} %refs_1_.5, f32[512,128]{1,0:T(8,128)} %refs_2_.5, f32[512,128]{1,0:T(8,128)} %refs_3_.5), custom_call_target="tpu_custom_call" | custom-call | bytes 7200000 | tf_op jit(solution)/shard_map/edge/pallas_call | solution.py:542
  2.8 7.6 %collective-permute-start.2 = (f32[8,48,128]{2,1,0:T(8,128)}, f32[8,48,128]{2,1,0:T(8,128)S(1)}, u32[]{:S(2)}, u32[]{:S(2)}) collective-permute-start(f32[8,48,128]{2,1,0:T(8,128)} %get-tuple-element.62), channel_id=1, source_target_pairs={{2,4},{4,2},{6,8},{8,6},{10,12},{12,10},{14,16},{16,14},{18,20},{2... | collective-permute-start | bytes 589832 | tf_op jit(solution)/shard_map/ppermute | solution.py:628
  10.4 1.4 %collective-permute-done.second = f32[1,16,128]{2,1,0:T(8,128)S(1)} collective-permute-done((f32[1,16,128]{2,1,0:T(8,128)}, f32[1,16,128]{2,1,0:T(8,128)S(1)}, u32[]{:S(2)}, u32[]{:S(2)}) %collective-permute-start) | collective-permute-done | bytes 8224 | tf_op jit(solution)/shard_map/ppermute | solution.py:558
  12.5 0.8 %copy.29.rows_ref = s32[4,40,16]{2,1,0:T(8,128)S(1)} copy(s32[4,40,16]{1,2,0:T(8,128)} %param.16) | data formatting | bytes 20480 | tf_op args[6]
  13.3 1.3 %plan.1 = (s32[32,128]{1,0:T(8,128)S(1)}, s32[2]{0:T(128)S(1)}, s32[4,16]{1,0:T(4,128)S(1)}, f32[1]{0:T(128)}) custom-call(s32[40]{0:T(128)S(1)} %copy-done.7, f32[40]{0:T(128)S(1)} %copy-done.8, s32[4,40,16]{2,1,0:T(8,128)S(1)} %copy.29.rows_ref, s32[168]{0:T(256)S(1)} %copy-done.6, f32[2,16,128]{2,1,0:T(8,128)S(1)} %stack.4.rest_0_.first), custom_call_target="tpu_custom_call" | custom-call | bytes 5400000 | tf_op jit(solution)/shard_map/plan/pallas_call | solution.py:542
  14.7 1.5 %collective-permute-done.3.second = f32[2,16,128]{2,1,0:T(8,128)S(1)} collective-permute-done((f32[2,16,128]{2,1,0:T(8,128)S(1)}, f32[2,16,128]{2,1,0:T(8,128)S(1)}, u32[]{:S(2)}, u32[]{:S(2)}) %collective-permute-start.3) | collective-permute-done | bytes 16416 | tf_op jit(solution)/shard_map/ppermute | solution.py:560
  16.2 0.7 %collective-permute-start.5 = (f32[4,16,128]{2,1,0:T(8,128)S(1)}, f32[4,16,128]{2,1,0:T(8,128)S(1)}, u32[]{:S(2)}, u32[]{:S(2)}) collective-permute-start(f32[4,16,128]{2,1,0:T(8,128)S(1)} %stack.5.refs_6_.first), channel_id=1, source_target_pairs={{0,96},{2,98},{4,100},{6,102},{8,104},{10,106},{12,108},{14,110},{... | collective-permute-start | bytes 98312 | tf_op jit(solution)/shard_map/ppermute | solution.py:562
  17.7 3.6 %collective-permute-done.5.second = f32[4,16,128]{2,1,0:T(8,128)S(1)} collective-permute-done((f32[4,16,128]{2,1,0:T(8,128)S(1)}, f32[4,16,128]{2,1,0:T(8,128)S(1)}, u32[]{:S(2)}, u32[]{:S(2)}) %collective-permute-start.5) | collective-permute-done | bytes 32800 | tf_op jit(solution)/shard_map/ppermute | solution.py:562
  21.5 2.8 %collective-permute-start.4 = (f32[304,128]{1,0:T(8,128)S(1)}, f32[304,128]{1,0:T(8,128)S(1)}, u32[]{:S(2)}, u32[]{:S(2)}) collective-permute-start(f32[304,128]{1,0:T(8,128)S(1)} %pack.1.rest_0_), channel_id=1, source_target_pairs={{0,1},{1,0},{2,3},{3,2},{4,5},{5,4},{6,7},{7,6},{8,9},{9,8},{10,11... | collective-permute-start | bytes 466952 | tf_op jit(solution)/shard_map/ppermute | solution.py:687
  24.3 1.1 %collective-permute-done.6.got = f32[4,16,128]{2,1,0:T(8,128)S(1)} collective-permute-done((f32[4,16,128]{2,1,0:T(8,128)S(1)}, f32[4,16,128]{2,1,0:T(8,128)S(1)}, u32[]{:S(2)}, u32[]{:S(2)}) %collective-permute-start.6) | collective-permute-done | bytes 32800 | tf_op jit(solution)/shard_map/ppermute | solution.py:568
  25.5 4.9 %collective-permute-done.7.got = f32[2,16,128]{2,1,0:T(8,128)S(1)} collective-permute-done((f32[2,16,128]{2,1,0:T(8,128)S(1)}, f32[2,16,128]{2,1,0:T(8,128)S(1)}, u32[]{:S(2)}, u32[]{:S(2)}) %collective-permute-start.7) | collective-permute-done | bytes 16416 | tf_op jit(solution)/shard_map/ppermute | solution.py:573
  30.4 3.6 %collective-permute-done.8.got = f32[1,16,128]{2,1,0:T(8,128)S(1)} collective-permute-done((f32[1,16,128]{2,1,0:T(8,128)S(1)}, f32[1,16,128]{2,1,0:T(8,128)S(1)}, u32[]{:S(2)}, u32[]{:S(2)}) %collective-permute-start.8) | collective-permute-done | bytes 8224 | tf_op jit(solution)/shard_map/ppermute | solution.py:578
  34.2 2.8 %collective-permute-start.9 = (f32[8,128]{1,0:T(8,128)S(1)}, f32[8,128]{1,0:T(8,128)S(1)}, u32[]{:S(2)}, u32[]{:S(2)}) collective-permute-start(f32[8,128]{1,0:T(8,128)S(1)} %get-tuple-element.79), channel_id=1, source_target_pairs={{0,1},{1,0},{2,3},{3,2},{4,5},{5,4},{6,7},{7,6},{8,9},{9,8},{10,11... | collective-permute-start | bytes 12296 | tf_op jit(solution)/shard_map/ppermute | solution.py:700
  37.0 2.6 %bulk_load.1 = (f32[3,2,536,128]{3,2,1,0:T(8,128)S(1)}, f32[3,2,528,128]{3,2,1,0:T(8,128)S(1)}, f32[4,2,528,128]{3,2,1,0:T(8,128)S(1)}) custom-call(f32[3,512,128]{2,1,0:T(8,128)S(1)} %copy-done, f32[3,512,128]{2,1,0:T(8,128)S(1)} %copy-done.1, f32[512,128]{1,0:T(8,128)S(1)} %copy-done.2, f32[512,128]{1,0:T(8,128)S(1)} %copy-done.3, ...), custom_call_target="tpu_custom_call" | custom-call | bytes 7200000 | tf_op jit(solution)/shard_map/bulk_load/pallas_call | solution.py:542
  39.6 0.9 %window_load.1 = (f32[3,2,72,128]{3,2,1,0:T(8,128)S(1)}, f32[3,2,64,128]{3,2,1,0:T(8,128)S(1)}, f32[4,2,64,128]{3,2,1,0:T(8,128)S(1)}) custom-call(s32[2]{0:T(128)S(1)} %get-tuple-element.60.where_ref, f32[3,512,128]{2,1,0:T(8,128)S(1)} %copy-done, f32[3,512,128]{2,1,0:T(8,128)S(1)} %copy-done.1, f32[512,128]{1,0:T(8,128)S(1)} %copy-done.2, ...), custom_call_target="tpu_custom_call" | custom-call | bytes 2880000 | tf_op jit(solution)/shard_map/window_load/pallas_call | solution.py:542
  40.5 2.3 %window.1 = (f32[3,2,72,128]{3,2,1,0:T(8,128)S(1)}, f32[3,2,64,128]{3,2,1,0:T(8,128)S(1)}, f32[2,2,64,128]{3,2,1,0:T(8,128)S(1)}, f32[1,16,128]{2,1,0:T(8,128)S(1)}) custom-call(s32[4,16]{1,0:T(4,128)S(1)} %get-tuple-element.67.list_ref, f32[1]{0:T(128)} %get-tuple-element.68.lift_ref, f32[16,128]{1,0:T(8,128)S(1)} %dynamic-slice_bitcast_fusion.table, ...), custom_call_target="tpu_custom_call" | custom-call | bytes 7200000 | tf_op jit(solution)/shard_map/window/pallas_call | solution.py:542
  43.1 0.9 %collective-permute-done.10.second = f32[1,16,128]{2,1,0:T(8,128)S(1)} collective-permute-done((f32[1,16,128]{2,1,0:T(8,128)S(1)}, f32[1,16,128]{2,1,0:T(8,128)S(1)}, u32[]{:S(2)}, u32[]{:S(2)}) %collective-permute-start.10) | collective-permute-done | bytes 8224 | tf_op jit(solution)/shard_map/ppermute | solution.py:558
  44.8 0.8 %bulk_step.13 = (f32[3,2,536,128]{3,2,1,0:T(8,128)S(1)}, f32[3,2,528,128]{3,2,1,0:T(8,128)S(1)}) custom-call(f32[16,128]{1,0:T(8,128)S(1)} %dynamic-slice_bitcast_fusion.table, f32[3,2,536,128]{3,2,1,0:T(8,128)S(1)} %get-tuple-element.64.rest_1_.state, f32[3,2,528,128]{3,2,1,0:T(8,128)S(1)} %get-tuple-element.65.vels, ...), custom_call_target="tpu_custom_call", output_to_operand_aliasing={{0}: (4, {}), {1}: (5, {})} | custom-call | bytes 2879999 | tf_op jit(solution)/shard_map/bulk_step/pallas_call | solution.py:542
  45.6 0.8 %bulk_step.14 = (f32[3,2,536,128]{3,2,1,0:T(8,128)S(1)}, f32[3,2,528,128]{3,2,1,0:T(8,128)S(1)}) custom-call(f32[16,128]{1,0:T(8,128)S(1)} %dynamic-slice_bitcast_fusion.table, f32[3,2,536,128]{3,2,1,0:T(8,128)S(1)} %get-tuple-element.64.rest_1_.state, f32[3,2,528,128]{3,2,1,0:T(8,128)S(1)} %get-tuple-element.65.vels, ...), custom_call_target="tpu_custom_call", output_to_operand_aliasing={{0}: (4, {}), {1}: (5, {})} | custom-call | bytes 2879999 | tf_op jit(solution)/shard_map/bulk_step/pallas_call | solution.py:542
  47.0 0.8 %collective-permute-done.11.second = f32[2,16,128]{2,1,0:T(8,128)S(1)} collective-permute-done((f32[2,16,128]{2,1,0:T(8,128)S(1)}, f32[2,16,128]{2,1,0:T(8,128)S(1)}, u32[]{:S(2)}, u32[]{:S(2)}) %collective-permute-start.11) | collective-permute-done | bytes 16416 | tf_op jit(solution)/shard_map/ppermute | solution.py:560
  47.8 0.8 %collective-permute-start.12 = (f32[4,16,128]{2,1,0:T(8,128)S(1)}, f32[4,16,128]{2,1,0:T(8,128)S(1)}, u32[]{:S(2)}, u32[]{:S(2)}) collective-permute-start(f32[4,16,128]{2,1,0:T(8,128)S(1)} %stack.7.rest_2_.rest_0_.first), channel_id=1, source_target_pairs={{0,96},{2,98},{4,100},{6,102},{8,104},{10,106},{12,108},{14,110},{... | collective-permute-start | bytes 98312 | tf_op jit(solution)/shard_map/ppermute | solution.py:562
  48.6 0.8 %bulk_step.16 = (f32[3,2,536,128]{3,2,1,0:T(8,128)S(1)}, f32[3,2,528,128]{3,2,1,0:T(8,128)S(1)}) custom-call(f32[16,128]{1,0:T(8,128)S(1)} %dynamic-slice_bitcast_fusion.table, f32[3,2,536,128]{3,2,1,0:T(8,128)S(1)} %get-tuple-element.88.state, f32[3,2,528,128]{3,2,1,0:T(8,128)S(1)} %get-tuple-element.89.vels, ...), custom_call_target="tpu_custom_call", output_to_operand_aliasing={{0}: (4, {}), {1}: (5, {})} | custom-call | bytes 2879999 | tf_op jit(solution)/shard_map/bulk_step/pallas_call | solution.py:542
  49.4 0.8 %bulk_step.17 = (f32[3,2,536,128]{3,2,1,0:T(8,128)S(1)}, f32[3,2,528,128]{3,2,1,0:T(8,128)S(1)}) custom-call(f32[16,128]{1,0:T(8,128)S(1)} %dynamic-slice_bitcast_fusion.table, f32[3,2,536,128]{3,2,1,0:T(8,128)S(1)} %get-tuple-element.88.state, f32[3,2,528,128]{3,2,1,0:T(8,128)S(1)} %get-tuple-element.89.vels, ...), custom_call_target="tpu_custom_call", output_to_operand_aliasing={{0}: (4, {}), {1}: (5, {})} | custom-call | bytes 2879999 | tf_op jit(solution)/shard_map/bulk_step/pallas_call | solution.py:542
  50.9 0.8 %bulk_step.19 = (f32[3,2,536,128]{3,2,1,0:T(8,128)S(1)}, f32[3,2,528,128]{3,2,1,0:T(8,128)S(1)}) custom-call(f32[16,128]{1,0:T(8,128)S(1)} %dynamic-slice_bitcast_fusion.table, f32[3,2,536,128]{3,2,1,0:T(8,128)S(1)} %get-tuple-element.94.state, f32[3,2,528,128]{3,2,1,0:T(8,128)S(1)} %get-tuple-element.95.vels, ...), custom_call_target="tpu_custom_call", output_to_operand_aliasing={{0}: (4, {}), {1}: (5, {})} | custom-call | bytes 2879999 | tf_op jit(solution)/shard_map/bulk_step/pallas_call | solution.py:542
  51.7 1.3 %collective-permute-done.12.second = f32[4,16,128]{2,1,0:T(8,128)S(1)} collective-permute-done((f32[4,16,128]{2,1,0:T(8,128)S(1)}, f32[4,16,128]{2,1,0:T(8,128)S(1)}, u32[]{:S(2)}, u32[]{:S(2)}) %collective-permute-start.12) | collective-permute-done | bytes 32800 | tf_op jit(solution)/shard_map/ppermute | solution.py:562
  53.1 0.8 %bulk_step.20 = (f32[3,2,536,128]{3,2,1,0:T(8,128)S(1)}, f32[3,2,528,128]{3,2,1,0:T(8,128)S(1)}) custom-call(f32[16,128]{1,0:T(8,128)S(1)} %dynamic-slice_bitcast_fusion.table, f32[3,2,536,128]{3,2,1,0:T(8,128)S(1)} %get-tuple-element.94.state, f32[3,2,528,128]{3,2,1,0:T(8,128)S(1)} %get-tuple-element.95.vels, ...), custom_call_target="tpu_custom_call", output_to_operand_aliasing={{0}: (4, {}), {1}: (5, {})} | custom-call | bytes 2879999 | tf_op jit(solution)/shard_map/bulk_step/pallas_call | solution.py:542
  54.6 0.8 %bulk_step.22 = (f32[3,2,536,128]{3,2,1,0:T(8,128)S(1)}, f32[3,2,528,128]{3,2,1,0:T(8,128)S(1)}) custom-call(f32[16,128]{1,0:T(8,128)S(1)} %dynamic-slice_bitcast_fusion.table, f32[3,2,536,128]{3,2,1,0:T(8,128)S(1)} %get-tuple-element.101.state, f32[3,2,528,128]{3,2,1,0:T(8,128)S(1)} %get-tuple-element.102.vels, ...), custom_call_target="tpu_custom_call", output_to_operand_aliasing={{0}: (4, {}), {1}: (5, {})} | custom-call | bytes 2879999 | tf_op jit(solution)/shard_map/bulk_step/pallas_call | solution.py:542
  55.4 0.8 %bulk_step.23 = (f32[3,2,536,128]{3,2,1,0:T(8,128)S(1)}, f32[3,2,528,128]{3,2,1,0:T(8,128)S(1)}) custom-call(f32[16,128]{1,0:T(8,128)S(1)} %dynamic-slice_bitcast_fusion.table, f32[3,2,536,128]{3,2,1,0:T(8,128)S(1)} %get-tuple-element.101.state, f32[3,2,528,128]{3,2,1,0:T(8,128)S(1)} %get-tuple-element.102.vels, ...), custom_call_target="tpu_custom_call", output_to_operand_aliasing={{0}: (4, {}), {1}: (5, {})} | custom-call | bytes 2879999 | tf_op jit(solution)/shard_map/bulk_step/pallas_call | solution.py:542
  56.2 0.8 %collective-permute-done.13.got = f32[4,16,128]{2,1,0:T(8,128)S(1)} collective-permute-done((f32[4,16,128]{2,1,0:T(8,128)S(1)}, f32[4,16,128]{2,1,0:T(8,128)S(1)}, u32[]{:S(2)}, u32[]{:S(2)}) %collective-permute-start.13) | collective-permute-done | bytes 32800 | tf_op jit(solution)/shard_map/ppermute | solution.py:568
  57.1 1.9 %bulk_store.1 = (f32[3,512,128]{2,1,0:T(8,128)}, f32[3,512,128]{2,1,0:T(8,128)}, f32[8,128]{1,0:T(8,128)S(1)}) custom-call(s32[2]{0:T(128)S(1)} %get-tuple-element.60.where_ref, f32[3,2,536,128]{3,2,1,0:T(8,128)S(1)} %get-tuple-element.107.rest_0_.state, f32[3,2,528,128]{3,2,1,0:T(8,128)S(1)} %get-tuple-element.108.vels, ...), custom_call_target="tpu_custom_call" | custom-call | bytes 7200000 | tf_op jit(solution)/shard_map/bulk_store/pallas_call | solution.py:542
  59.1 3.0 %collective-permute-done.14.got = f32[2,16,128]{2,1,0:T(8,128)S(1)} collective-permute-done((f32[2,16,128]{2,1,0:T(8,128)S(1)}, f32[2,16,128]{2,1,0:T(8,128)S(1)}, u32[]{:S(2)}, u32[]{:S(2)}) %collective-permute-start.14) | collective-permute-done | bytes 16416 | tf_op jit(solution)/shard_map/ppermute | solution.py:573
  62.0 3.6 %collective-permute-done.15.handed = f32[1,16,128]{2,1,0:T(8,128)S(1)} collective-permute-done((f32[1,16,128]{2,1,0:T(8,128)S(1)}, f32[1,16,128]{2,1,0:T(8,128)S(1)}, u32[]{:S(2)}, u32[]{:S(2)}) %collective-permute-start.15) | collective-permute-done | bytes 8224 | tf_op jit(solution)/shard_map/ppermute | solution.py:578
  (54 shorter events, 5.7 us)
Async XLA Ops:
  0.6 12.7 %copy-start.6 = (s32[168]{0:T(256)S(1)}, s32[168]{0:T(256)}, u32[]{:S(2)}) copy-start(s32[168]{0:T(256)} %constant.13.clone.static_ref) | copy-start | bytes 2020
  0.6 16.3 %copy-start = (f32[3,512,128]{2,1,0:T(8,128)S(1)}, f32[3,512,128]{2,1,0:T(8,128)}, u32[]{:S(2)}) copy-start(f32[3,512,128]{2,1,0:T(8,128)} %refs_0_.5) | copy-start | bytes 2359300
  0.7 16.3 %copy-start.1 = (f32[3,512,128]{2,1,0:T(8,128)S(1)}, f32[3,512,128]{2,1,0:T(8,128)}, u32[]{:S(2)}) copy-start(f32[3,512,128]{2,1,0:T(8,128)} %refs_1_.5) | copy-start | bytes 2359300
  0.7 16.3 %copy-start.2 = (f32[512,128]{1,0:T(8,128)S(1)}, f32[512,128]{1,0:T(8,128)}, u32[]{:S(2)}) copy-start(f32[512,128]{1,0:T(8,128)} %refs_2_.5) | copy-start | bytes 786436
  0.7 16.3 %copy-start.3 = (f32[512,128]{1,0:T(8,128)S(1)}, f32[512,128]{1,0:T(8,128)}, u32[]{:S(2)}) copy-start(f32[512,128]{1,0:T(8,128)} %refs_3_.5) | copy-start | bytes 786436
  0.7 12.6 %copy-start.8 = (f32[40]{0:T(128)S(1)}, f32[40]{0:T(128)}, u32[]{:S(2)}) copy-start(f32[40]{0:T(128)} %lift_ref.1) | copy-start | bytes 484
  0.7 12.6 %copy-start.7 = (s32[40]{0:T(128)S(1)}, s32[40]{0:T(128)}, u32[]{:S(2)}) copy-start(s32[40]{0:T(128)} %slot_ref.1) | copy-start | bytes 484
  2.7 14.3 %collective-permute-start.1 = (f32[8,48,128]{2,1,0:T(8,128)}, f32[8,48,128]{2,1,0:T(8,128)S(1)}, u32[]{:S(2)}, u32[]{:S(2)}) collective-permute-start(f32[8,48,128]{2,1,0:T(8,128)} %get-tuple-element.61), channel_id=1, source_target_pairs={{0,2},{2,0},{4,6},{6,4},{8,10},{10,8},{12,14},{14,12},{16,18},{18,... | collective-permute-start | bytes 589832 | tf_op jit(solution)/shard_map/ppermute | solution.py:628
  2.8 14.2 %collective-permute-start.2 = (f32[8,48,128]{2,1,0:T(8,128)}, f32[8,48,128]{2,1,0:T(8,128)S(1)}, u32[]{:S(2)}, u32[]{:S(2)}) collective-permute-start(f32[8,48,128]{2,1,0:T(8,128)} %get-tuple-element.62), channel_id=1, source_target_pairs={{2,4},{4,2},{6,8},{8,6},{10,12},{12,10},{14,16},{16,14},{18,20},{2... | collective-permute-start | bytes 589832 | tf_op jit(solution)/shard_map/ppermute | solution.py:628
  10.4 1.4 %collective-permute-start = (f32[1,16,128]{2,1,0:T(8,128)}, f32[1,16,128]{2,1,0:T(8,128)S(1)}, u32[]{:S(2)}, u32[]{:S(2)}) collective-permute-start(f32[1,16,128]{2,1,0:T(8,128)} %before.1), channel_id=1, source_target_pairs={{0,2},{2,0},{4,6},{6,4},{8,10},{10,8},{12,14},{14,12},{16,18},{18,... | collective-permute-start | bytes 24584 | tf_op jit(solution)/shard_map/ppermute | solution.py:558
  11.8 0.7 %copy-start.4 = (f32[1,16,128]{2,1,0:T(8,128)S(1)}, f32[1,16,128]{2,1,0:T(8,128)}, u32[]{:S(2)}) copy-start(f32[1,16,128]{2,1,0:T(8,128)} %before.1) | copy-start | bytes 24580
  12.5 3.7 %collective-permute-start.3 = (f32[2,16,128]{2,1,0:T(8,128)S(1)}, f32[2,16,128]{2,1,0:T(8,128)S(1)}, u32[]{:S(2)}, u32[]{:S(2)}) collective-permute-start(f32[2,16,128]{2,1,0:T(8,128)S(1)} %stack.4.rest_0_.first), channel_id=1, source_target_pairs={{0,32},{2,34},{4,36},{6,38},{8,40},{10,42},{12,44},{14,46},{16,48}... | collective-permute-start | bytes 49160 | tf_op jit(solution)/shard_map/ppermute | solution.py:560
  13.3 23.6 %copy-start.9 = (f32[2,16,128]{2,1,0:T(8,128)S(1)}, f32[2,16,128]{2,1,0:T(8,128)}, u32[]{:S(2)}) copy-start(f32[2,16,128]{2,1,0:T(8,128)} %constant.12.clone) | copy-start | bytes 49156
  16.2 5.1 %collective-permute-start.5 = (f32[4,16,128]{2,1,0:T(8,128)S(1)}, f32[4,16,128]{2,1,0:T(8,128)S(1)}, u32[]{:S(2)}, u32[]{:S(2)}) collective-permute-start(f32[4,16,128]{2,1,0:T(8,128)S(1)} %stack.5.refs_6_.first), channel_id=1, source_target_pairs={{0,96},{2,98},{4,100},{6,102},{8,104},{10,106},{12,108},{14,110},{... | collective-permute-start | bytes 98312 | tf_op jit(solution)/shard_map/ppermute | solution.py:562
  21.4 4.0 %collective-permute-start.6 = (f32[4,16,128]{2,1,0:T(8,128)S(1)}, f32[4,16,128]{2,1,0:T(8,128)S(1)}, u32[]{:S(2)}, u32[]{:S(2)}) collective-permute-start(f32[4,16,128]{2,1,0:T(8,128)S(1)} %get-tuple-element.73), channel_id=1, source_target_pairs={{0,8},{2,10},{4,12},{6,14},{8,0},{10,2},{12,4},{14,6},{16,24},{18,... | collective-permute-start | bytes 98312 | tf_op jit(solution)/shard_map/ppermute | solution.py:568
  21.5 15.5 %collective-permute-start.4 = (f32[304,128]{1,0:T(8,128)S(1)}, f32[304,128]{1,0:T(8,128)S(1)}, u32[]{:S(2)}, u32[]{:S(2)}) collective-permute-start(f32[304,128]{1,0:T(8,128)S(1)} %pack.1.rest_0_), channel_id=1, source_target_pairs={{0,1},{1,0},{2,3},{3,2},{4,5},{5,4},{6,7},{7,6},{8,9},{9,8},{10,11... | collective-permute-start | bytes 466952 | tf_op jit(solution)/shard_map/ppermute | solution.py:687
  25.4 5.0 %collective-permute-start.7 = (f32[2,16,128]{2,1,0:T(8,128)S(1)}, f32[2,16,128]{2,1,0:T(8,128)S(1)}, u32[]{:S(2)}, u32[]{:S(2)}) collective-permute-start(f32[2,16,128]{2,1,0:T(8,128)S(1)} %get-tuple-element.75), channel_id=1, source_target_pairs={{0,24},{2,26},{4,28},{6,30},{8,16},{10,18},{12,20},{14,22},{16,8},... | collective-permute-start | bytes 49160 | tf_op jit(solution)/shard_map/ppermute | solution.py:573
  30.4 3.7 %collective-permute-start.8 = (f32[1,16,128]{2,1,0:T(8,128)S(1)}, f32[1,16,128]{2,1,0:T(8,128)S(1)}, u32[]{:S(2)}, u32[]{:S(2)}) collective-permute-start(f32[1,16,128]{2,1,0:T(8,128)S(1)} %get-tuple-element.77), channel_id=1, source_target_pairs={{0,4},{2,6},{4,0},{6,2},{8,12},{10,14},{12,8},{14,10},{16,20},{18,... | collective-permute-start | bytes 24584 | tf_op jit(solution)/shard_map/ppermute | solution.py:578
  34.2 6.3 %collective-permute-start.9 = (f32[8,128]{1,0:T(8,128)S(1)}, f32[8,128]{1,0:T(8,128)S(1)}, u32[]{:S(2)}, u32[]{:S(2)}) collective-permute-start(f32[8,128]{1,0:T(8,128)S(1)} %get-tuple-element.79), channel_id=1, source_target_pairs={{0,1},{1,0},{2,3},{3,2},{4,5},{5,4},{6,7},{7,6},{8,9},{9,8},{10,11... | collective-permute-start | bytes 12296 | tf_op jit(solution)/shard_map/ppermute | solution.py:700
  42.8 1.3 %collective-permute-start.10 = (f32[1,16,128]{2,1,0:T(8,128)S(1)}, f32[1,16,128]{2,1,0:T(8,128)S(1)}, u32[]{:S(2)}, u32[]{:S(2)}) collective-permute-start(f32[1,16,128]{2,1,0:T(8,128)S(1)} %get-tuple-element.80.first), channel_id=1, source_target_pairs={{0,2},{2,0},{4,6},{6,4},{8,10},{10,8},{12,14},{14,12},{16,18},{18,... | collective-permute-start | bytes 24584 | tf_op jit(solution)/shard_map/ppermute | solution.py:558
  44.1 3.7 %collective-permute-start.11 = (f32[2,16,128]{2,1,0:T(8,128)S(1)}, f32[2,16,128]{2,1,0:T(8,128)S(1)}, u32[]{:S(2)}, u32[]{:S(2)}) collective-permute-start(f32[2,16,128]{2,1,0:T(8,128)S(1)} %stack.6.rest_0_.rest_2_.first), channel_id=1, source_target_pairs={{0,32},{2,34},{4,36},{6,38},{8,40},{10,42},{12,44},{14,46},{16,48}... | collective-permute-start | bytes 49160 | tf_op jit(solution)/shard_map/ppermute | solution.py:560
  47.8 5.1 %collective-permute-start.12 = (f32[4,16,128]{2,1,0:T(8,128)S(1)}, f32[4,16,128]{2,1,0:T(8,128)S(1)}, u32[]{:S(2)}, u32[]{:S(2)}) collective-permute-start(f32[4,16,128]{2,1,0:T(8,128)S(1)} %stack.7.rest_2_.rest_0_.first), channel_id=1, source_target_pairs={{0,96},{2,98},{4,100},{6,102},{8,104},{10,106},{12,108},{14,110},{... | collective-permute-start | bytes 98312 | tf_op jit(solution)/shard_map/ppermute | solution.py:562
  53.0 4.0 %collective-permute-start.13 = (f32[4,16,128]{2,1,0:T(8,128)S(1)}, f32[4,16,128]{2,1,0:T(8,128)S(1)}, u32[]{:S(2)}, u32[]{:S(2)}) collective-permute-start(f32[4,16,128]{2,1,0:T(8,128)S(1)} %get-tuple-element.100.rest_2_.rest_0_), channel_id=1, source_target_pairs={{0,8},{2,10},{4,12},{6,14},{8,0},{10,2},{12,4},{14,6},{16,24},{18,... | collective-permute-start | bytes 98312 | tf_op jit(solution)/shard_map/ppermute | solution.py:568
  57.0 5.0 %collective-permute-start.14 = (f32[2,16,128]{2,1,0:T(8,128)S(1)}, f32[2,16,128]{2,1,0:T(8,128)S(1)}, u32[]{:S(2)}, u32[]{:S(2)}) collective-permute-start(f32[2,16,128]{2,1,0:T(8,128)S(1)} %get-tuple-element.110.rest_0_), channel_id=1, source_target_pairs={{0,24},{2,26},{4,28},{6,30},{8,16},{10,18},{12,20},{14,22},{16,8},... | collective-permute-start | bytes 49160 | tf_op jit(solution)/shard_map/ppermute | solution.py:573
  57.1 8.6 %copy-start.5 = (f32[1,16,128]{2,1,0:T(8,128)S(1)}, f32[1,16,128]{2,1,0:T(8,128)}, u32[]{:S(2)}) copy-start(f32[1,16,128]{2,1,0:T(8,128)} %before.1) | copy-start | bytes 24580
  62.0 3.7 %collective-permute-start.15 = (f32[1,16,128]{2,1,0:T(8,128)S(1)}, f32[1,16,128]{2,1,0:T(8,128)S(1)}, u32[]{:S(2)}, u32[]{:S(2)}) collective-permute-start(f32[1,16,128]{2,1,0:T(8,128)S(1)} %get-tuple-element.116), channel_id=1, source_target_pairs={{0,4},{2,6},{4,0},{6,2},{8,12},{10,14},{12,8},{14,10},{16,20},{18,... | collective-permute-start | bytes 24584 | tf_op jit(solution)/shard_map/ppermute | solution.py:578

commit v6 on v5

--- a/solution.py
+++ b/solution.py
@@ -337,19 +337,6 @@
         lax.fori_loop(begin // (8 * group), end // (8 * group), body, carry)
 
 
-def pad_edge_kernel(plan, kept, got, *rest):
-    out, edges = rest[-2:]
-    pad = jnp.where(plan[SAME_X : SAME_X + 1, :] > 0, kept[0], got[0])
-    out[...] = pad
-    lane = lax.broadcasted_iota(jnp.int32, (1, LANES), 1) // (2 * EDGE)
-    total = jnp.zeros((1, LANES), jnp.float32)
-    slots = pad.shape[0]
-    for m in range(slots):
-        moved = pltpu.roll(pad[m : m + 1, :], LANES - EDGE - 2 * EDGE * m, 1)
-        total = jnp.where(lane == slots - 1 - m, moved, total)
-    edges[...] = jnp.broadcast_to(total, edges.shape)
-
-
 def window_load_kernel(half, base, cycle_total, where_ref, *refs):
     fields, (inner, outer, columns, state, vels, coef) = refs[:4], refs[4:]
     start = pl.multiple_of(where_ref[0], 8)
@@ -396,15 +383,12 @@
 
 
 def window_kernel(
-    list_ref, lift_ref, table, state, vels, coef, pads, edges, *rest
+    list_ref, lift_ref, plan, table, state, vels, coef, kept, near, far, cross, *rest
 ):
     state_out, vels_out, push, pad_out, spare, vels_spare, taken, given, held = rest[-9:]
-    lane = lax.broadcasted_iota(jnp.int32, (8, LANES), 1)
-    keep = (lane < EDGE) | (lane >= LANES - EDGE)
-    held[0] = pads[...]
-    for part in range(2):
-        moved = pltpu.roll(edges[...], EDGE + 64 * part, 1, stride=2 * EDGE, stride_axis=0)
-        held[1, 8 * part : 8 * part + 8, :] = jnp.where(keep, moved, 0.0)
+    same = plan[SAME_X : SAME_X + 1, :] > 0
+    held[0] = jnp.where(same, kept[0], near[0])
+    held[1] = jnp.where(same, far[0], cross[0])
     lift = lift_ref[0]
     clear_tail(spare, WIN)
     clear_tail(state_out, WIN)
@@ -575,7 +559,7 @@
         functools.partial(choose_kernel, way, FAR_Z), "choose", (real(1, *shape),) * 2, (plan, keep, got),
         after=between(4, send),
     )
-    return keep, lax.ppermute(send, "arc", flips(x=1)), between(5, send)
+    return keep, lax.ppermute(send, "arc", flips(x=1)), between(5, send), send
 
 
 def static_tables(arc_count, cycle_dev, roller_total):
@@ -686,26 +670,24 @@
             pack = call(pack_kernel, "pack", real(half, LANES), (*fields, *ends), micros=2.0, after=(value,))
             kept["columns"] = lax.ppermute(pack, "circ", swap)
             return (pack,)
-        if stage == 6:
+        if stage == 5:
             kept["window"] = load_window()
             kept["bulk"] = load_bulk()
             return (kept["window"][0], kept["bulk"][0])
         return ()
 
-    pads, handed, _ = route(pad_state, kept, 0, going)
-    pads, edges = call(
-        pad_edge_kernel, "pad_edge", (real(slots, LANES), real(8, LANES)), (kept["plan"][0], pads, handed)
-    )
-    done = going(6, edges)
-    edges = lax.ppermute(edges, "circ", swap)
+    mine, near, done, sent = route(pad_state, kept, 0, going)
+    double = [(2 * s + h, 2 * d + 1 - h) for s, d in flips(x=1) for h in range(2)]
+    far = lax.ppermute(mine, "circ", swap)
+    cross = lax.ppermute(sent, ("arc", "circ"), double)
 
     plan, _, rows_in, lift = kept["plan"]
     win_state, win_vels, win_coef = kept["window"]
     win_state, win_vels, push, pad_new = call(
         window_kernel, "window", (*buffers(WIN)[:2], real(2, 2, WIN, LANES), real(1, slots, LANES)),
-        (rows_in, lift, table, win_state, win_vels, win_coef, pads, edges),
+        (rows_in, lift, plan, table, win_state, win_vels, win_coef, mine, near, far, cross),
         after=done,
-        in_specs=[SMEM] * 2 + [VMEM] * 6,
+        in_specs=[SMEM] * 2 + [VMEM] * 9,
         scratch=room(WIN)
         + [
             pltpu.VMEM((2, 2, slots, LANES), jnp.float32),
@@ -726,7 +708,7 @@
             return store_bulk(value)
         return step_bulk(value, 4) if stage < 4 else ()
 
-    pads, handed, done = route(pad_new, kept, 1, coming)
+    pads, handed, done, _ = route(pad_new, kept, 1, coming)
     pad_result = call(last_kernel, "last", real(1, slots, LANES), (plan, pads, handed, pad_state), after=done)
     return *kept["outs"], pad_result
 

time: 66.5 us -> 64.7 us (0.973)
  waiting for transfers between devices: 26.5 us -> 22.9 us
  starting transfers between devices: 15.3 us -> 17.2 us
    ppermute x3 -> x4, waiting for transfers between devices: 7.28 us -> 3.65 us  [the longest x2 3.64 us: route(): return (keep, lax.ppermute(send, 'arc', flips(x=1)), between(5, send), send)]
    ppermute x3 -> x4, starting transfers between devices: 2.81 us -> 4.7 us  [the longest x2 2.68 us: route(): return (keep, lax.ppermute(send, 'arc', flips(x=1)), between(5, send), send)]
    pallas_call x32 -> x31, Pallas kernels: 21.9 us -> 21.8 us  [call(): pl.pallas_call(kernel, out_shape=shapes, in_specs=list(in_specs or [VMEM]...]
  transfers between devices with their start and end apart: 16 -> 17, of which waited for: 12 -> 11; matrix products, arithmetic and copies ran while one was open for 1% -> 1% of each run, Pallas kernels for 25% -> 26%
where the time goes in v6:
time: 64.7 us; the launch traced here: 64.5 us
  waiting for transfers between devices  22.9 us (35%)
  Pallas kernels  21.8 us (34%)
  starting transfers between devices  17.2 us (27%)
  local copies, waits for them, and re-layouts  1.58 us (2%)
  between operations  1 us (2%)
    pallas_call x31, Pallas kernels, call(): pl.pallas_call(kernel, out_shape=shapes, in_specs=list(in_specs or [VMEM]...  21.8 us
    ppermute x2, waiting for transfers between devices, route(): got = lax.ppermute(send, 'arc', flips(z=3))  7.88 us
    ppermute x1, starting transfers between devices, local(): lax.ppermute(outer, 'arc', outward)  7.6 us
    ppermute x2, waiting for transfers between devices, route(): got = lax.ppermute(held, 'arc', flips(y=3))  4.88 us
    ppermute x2, waiting for transfers between devices, route(): return (keep, lax.ppermute(send, 'arc', flips(x=1)), between(5, send), send)  3.64 us
    ppermute x1, starting transfers between devices, going(): kept['columns'] = lax.ppermute(pack, 'circ', swap)  2.81 us
    ppermute x2, starting transfers between devices, route(): return (keep, lax.ppermute(send, 'arc', flips(x=1)), between(5, send), send)  2.68 us
    ppermute x2, waiting for transfers between devices, route(): got = lax.ppermute(value, 'arc', flips(c=1))  2.32 us
  transfers between devices with their start and end apart: 17, of which 11 were waited for; matrix products, arithmetic and copies ran while one was open for 1% of the time, Pallas kernels for 26%

profile of v6, /device:TPU:0, one launch (start us, length us, event | category | flops | bytes accessed | tf_op | source)
XLA Modules:
  0.0 64.5 jit_solution(9164590415967691495)
XLA Ops:
  0.7 2.0 %edge.1 = (f32[8,48,128]{2,1,0:T(8,128)}, f32[8,48,128]{2,1,0:T(8,128)}) custom-call(f32[3,512,128]{2,1,0:T(8,128)} %refs_0_.5, f32[3,512,128]{2,1,0:T(8,128)} %refs_1_.5, f32[512,128]{1,0:T(8,128)} %refs_2_.5, f32[512,128]{1,0:T(8,128)} %refs_3_.5), custom_call_target="tpu_custom_call" | custom-call | bytes 7200000 | tf_op jit(solution)/shard_map/edge/pallas_call | solution.py:526
  2.8 7.6 %collective-permute-start.2 = (f32[8,48,128]{2,1,0:T(8,128)}, f32[8,48,128]{2,1,0:T(8,128)S(1)}, u32[]{:S(2)}, u32[]{:S(2)}) collective-permute-start(f32[8,48,128]{2,1,0:T(8,128)} %get-tuple-element.60), channel_id=1, source_target_pairs={{2,4},{4,2},{6,8},{8,6},{10,12},{12,10},{14,16},{16,14},{18,20},{2... | collective-permute-start | bytes 589832 | tf_op jit(solution)/shard_map/ppermute | solution.py:612
  10.4 1.4 %collective-permute-done.second = f32[1,16,128]{2,1,0:T(8,128)S(1)} collective-permute-done((f32[1,16,128]{2,1,0:T(8,128)}, f32[1,16,128]{2,1,0:T(8,128)S(1)}, u32[]{:S(2)}, u32[]{:S(2)}) %collective-permute-start) | collective-permute-done | bytes 8224 | tf_op jit(solution)/shard_map/ppermute | solution.py:542
  12.5 0.8 %copy.29.rows_ref = s32[4,40,16]{2,1,0:T(8,128)S(1)} copy(s32[4,40,16]{1,2,0:T(8,128)} %param.16) | data formatting | bytes 20480 | tf_op args[6]
  13.3 1.3 %plan.1 = (s32[32,128]{1,0:T(8,128)S(1)}, s32[2]{0:T(128)S(1)}, s32[4,16]{1,0:T(4,128)S(1)}, f32[1]{0:T(128)}) custom-call(s32[40]{0:T(128)S(1)} %copy-done.7, f32[40]{0:T(128)S(1)} %copy-done.8, s32[4,40,16]{2,1,0:T(8,128)S(1)} %copy.29.rows_ref, s32[168]{0:T(256)S(1)} %copy-done.6, f32[2,16,128]{2,1,0:T(8,128)S(1)} %stack.4.rest_0_.first), custom_call_target="tpu_custom_call" | custom-call | bytes 5400000 | tf_op jit(solution)/shard_map/plan/pallas_call | solution.py:526
  14.7 1.5 %collective-permute-done.3.second = f32[2,16,128]{2,1,0:T(8,128)S(1)} collective-permute-done((f32[2,16,128]{2,1,0:T(8,128)S(1)}, f32[2,16,128]{2,1,0:T(8,128)S(1)}, u32[]{:S(2)}, u32[]{:S(2)}) %collective-permute-start.3) | collective-permute-done | bytes 16416 | tf_op jit(solution)/shard_map/ppermute | solution.py:544
  16.2 0.7 %collective-permute-start.5 = (f32[4,16,128]{2,1,0:T(8,128)S(1)}, f32[4,16,128]{2,1,0:T(8,128)S(1)}, u32[]{:S(2)}, u32[]{:S(2)}) collective-permute-start(f32[4,16,128]{2,1,0:T(8,128)S(1)} %stack.5.refs_6_.first), channel_id=1, source_target_pairs={{0,96},{2,98},{4,100},{6,102},{8,104},{10,106},{12,108},{14,110},{... | collective-permute-start | bytes 98312 | tf_op jit(solution)/shard_map/ppermute | solution.py:546
  17.7 3.6 %collective-permute-done.5.second = f32[4,16,128]{2,1,0:T(8,128)S(1)} collective-permute-done((f32[4,16,128]{2,1,0:T(8,128)S(1)}, f32[4,16,128]{2,1,0:T(8,128)S(1)}, u32[]{:S(2)}, u32[]{:S(2)}) %collective-permute-start.5) | collective-permute-done | bytes 32800 | tf_op jit(solution)/shard_map/ppermute | solution.py:546
  21.5 2.8 %collective-permute-start.4 = (f32[304,128]{1,0:T(8,128)S(1)}, f32[304,128]{1,0:T(8,128)S(1)}, u32[]{:S(2)}, u32[]{:S(2)}) collective-permute-start(f32[304,128]{1,0:T(8,128)S(1)} %pack.1.rest_0_), channel_id=1, source_target_pairs={{0,1},{1,0},{2,3},{3,2},{4,5},{5,4},{6,7},{7,6},{8,9},{9,8},{10,11... | collective-permute-start | bytes 466952 | tf_op jit(solution)/shard_map/ppermute | solution.py:671
  24.3 1.1 %collective-permute-done.6.got = f32[4,16,128]{2,1,0:T(8,128)S(1)} collective-permute-done((f32[4,16,128]{2,1,0:T(8,128)S(1)}, f32[4,16,128]{2,1,0:T(8,128)S(1)}, u32[]{:S(2)}, u32[]{:S(2)}) %collective-permute-start.6) | collective-permute-done | bytes 32800 | tf_op jit(solution)/shard_map/ppermute | solution.py:552
  25.5 4.9 %collective-permute-done.7.got = f32[2,16,128]{2,1,0:T(8,128)S(1)} collective-permute-done((f32[2,16,128]{2,1,0:T(8,128)S(1)}, f32[2,16,128]{2,1,0:T(8,128)S(1)}, u32[]{:S(2)}, u32[]{:S(2)}) %collective-permute-start.7) | collective-permute-done | bytes 16416 | tf_op jit(solution)/shard_map/ppermute | solution.py:557
  30.4 2.7 %collective-permute-start.8 = (f32[1,16,128]{2,1,0:T(8,128)S(1)}, f32[1,16,128]{2,1,0:T(8,128)S(1)}, u32[]{:S(2)}, u32[]{:S(2)}) collective-permute-start(f32[1,16,128]{2,1,0:T(8,128)S(1)} %get-tuple-element.75), channel_id=1, source_target_pairs={{0,4},{2,6},{4,0},{6,2},{8,12},{10,14},{12,8},{14,10},{16,20},{18,... | collective-permute-start | bytes 24584 | tf_op jit(solution)/shard_map/ppermute | solution.py:562
  33.1 2.0 %collective-permute-start.9 = (f32[1,16,128]{2,1,0:T(8,128)S(1)}, f32[1,16,128]{2,1,0:T(8,128)S(1)}, u32[]{:S(2)}, u32[]{:S(2)}) collective-permute-start(f32[1,16,128]{2,1,0:T(8,128)S(1)} %get-tuple-element.74.kept), channel_id=1, source_target_pairs={{0,1},{1,0},{2,3},{3,2},{4,5},{5,4},{6,7},{7,6},{8,9},{9,8},{10,11... | collective-permute-start | bytes 24584 | tf_op jit(solution)/shard_map/ppermute | solution.py:681
  35.1 2.6 %bulk_load.1 = (f32[3,2,536,128]{3,2,1,0:T(8,128)S(1)}, f32[3,2,528,128]{3,2,1,0:T(8,128)S(1)}, f32[4,2,528,128]{3,2,1,0:T(8,128)S(1)}) custom-call(f32[3,512,128]{2,1,0:T(8,128)S(1)} %copy-done, f32[3,512,128]{2,1,0:T(8,128)S(1)} %copy-done.1, f32[512,128]{1,0:T(8,128)S(1)} %copy-done.2, f32[512,128]{1,0:T(8,128)S(1)} %copy-done.3, ...), custom_call_target="tpu_custom_call" | custom-call | bytes 7200000 | tf_op jit(solution)/shard_map/bulk_load/pallas_call | solution.py:526
  37.8 0.9 %window_load.1 = (f32[3,2,72,128]{3,2,1,0:T(8,128)S(1)}, f32[3,2,64,128]{3,2,1,0:T(8,128)S(1)}, f32[4,2,64,128]{3,2,1,0:T(8,128)S(1)}) custom-call(s32[2]{0:T(128)S(1)} %get-tuple-element.58.where_ref, f32[3,512,128]{2,1,0:T(8,128)S(1)} %copy-done, f32[3,512,128]{2,1,0:T(8,128)S(1)} %copy-done.1, f32[512,128]{1,0:T(8,128)S(1)} %copy-done.2, ...), custom_call_target="tpu_custom_call" | custom-call | bytes 2880000 | tf_op jit(solution)/shard_map/window_load/pallas_call | solution.py:526
  38.7 2.3 %window.1 = (f32[3,2,72,128]{3,2,1,0:T(8,128)S(1)}, f32[3,2,64,128]{3,2,1,0:T(8,128)S(1)}, f32[2,2,64,128]{3,2,1,0:T(8,128)S(1)}, f32[1,16,128]{2,1,0:T(8,128)S(1)}) custom-call(s32[4,16]{1,0:T(4,128)S(1)} %get-tuple-element.65.list_ref, f32[1]{0:T(128)} %get-tuple-element.66.lift_ref, s32[32,128]{1,0:T(8,128)S(1)} %get-tuple-element.61.rest_0_.plan, ...), custom_call_target="tpu_custom_call" | custom-call | bytes 7200000 | tf_op jit(solution)/shard_map/window/pallas_call | solution.py:526
  41.3 0.9 %collective-permute-done.11.second = f32[1,16,128]{2,1,0:T(8,128)S(1)} collective-permute-done((f32[1,16,128]{2,1,0:T(8,128)S(1)}, f32[1,16,128]{2,1,0:T(8,128)S(1)}, u32[]{:S(2)}, u32[]{:S(2)}) %collective-permute-start.11) | collective-permute-done | bytes 8224 | tf_op jit(solution)/shard_map/ppermute | solution.py:542
  42.9 0.8 %bulk_step.13 = (f32[3,2,536,128]{3,2,1,0:T(8,128)S(1)}, f32[3,2,528,128]{3,2,1,0:T(8,128)S(1)}) custom-call(f32[16,128]{1,0:T(8,128)S(1)} %dynamic-slice_bitcast_fusion.table, f32[3,2,536,128]{3,2,1,0:T(8,128)S(1)} %get-tuple-element.62.rest_1_.state, f32[3,2,528,128]{3,2,1,0:T(8,128)S(1)} %get-tuple-element.63.vels, ...), custom_call_target="tpu_custom_call", output_to_operand_aliasing={{0}: (4, {}), {1}: (5, {})} | custom-call | bytes 2879999 | tf_op jit(solution)/shard_map/bulk_step/pallas_call | solution.py:526
  43.7 0.8 %bulk_step.14 = (f32[3,2,536,128]{3,2,1,0:T(8,128)S(1)}, f32[3,2,528,128]{3,2,1,0:T(8,128)S(1)}) custom-call(f32[16,128]{1,0:T(8,128)S(1)} %dynamic-slice_bitcast_fusion.table, f32[3,2,536,128]{3,2,1,0:T(8,128)S(1)} %get-tuple-element.62.rest_1_.state, f32[3,2,528,128]{3,2,1,0:T(8,128)S(1)} %get-tuple-element.63.vels, ...), custom_call_target="tpu_custom_call", output_to_operand_aliasing={{0}: (4, {}), {1}: (5, {})} | custom-call | bytes 2879999 | tf_op jit(solution)/shard_map/bulk_step/pallas_call | solution.py:526
  45.2 0.8 %collective-permute-done.12.second = f32[2,16,128]{2,1,0:T(8,128)S(1)} collective-permute-done((f32[2,16,128]{2,1,0:T(8,128)S(1)}, f32[2,16,128]{2,1,0:T(8,128)S(1)}, u32[]{:S(2)}, u32[]{:S(2)}) %collective-permute-start.12) | collective-permute-done | bytes 16416 | tf_op jit(solution)/shard_map/ppermute | solution.py:544
  46.0 0.8 %collective-permute-start.13 = (f32[4,16,128]{2,1,0:T(8,128)S(1)}, f32[4,16,128]{2,1,0:T(8,128)S(1)}, u32[]{:S(2)}, u32[]{:S(2)}) collective-permute-start(f32[4,16,128]{2,1,0:T(8,128)S(1)} %stack.7.rest_2_.rest_0_.first), channel_id=1, source_target_pairs={{0,96},{2,98},{4,100},{6,102},{8,104},{10,106},{12,108},{14,110},{... | collective-permute-start | bytes 98312 | tf_op jit(solution)/shard_map/ppermute | solution.py:546
  46.8 0.8 %bulk_step.16 = (f32[3,2,536,128]{3,2,1,0:T(8,128)S(1)}, f32[3,2,528,128]{3,2,1,0:T(8,128)S(1)}) custom-call(f32[16,128]{1,0:T(8,128)S(1)} %dynamic-slice_bitcast_fusion.table, f32[3,2,536,128]{3,2,1,0:T(8,128)S(1)} %get-tuple-element.84.state, f32[3,2,528,128]{3,2,1,0:T(8,128)S(1)} %get-tuple-element.85.vels, ...), custom_call_target="tpu_custom_call", output_to_operand_aliasing={{0}: (4, {}), {1}: (5, {})} | custom-call | bytes 2879999 | tf_op jit(solution)/shard_map/bulk_step/pallas_call | solution.py:526
  47.6 0.8 %bulk_step.17 = (f32[3,2,536,128]{3,2,1,0:T(8,128)S(1)}, f32[3,2,528,128]{3,2,1,0:T(8,128)S(1)}) custom-call(f32[16,128]{1,0:T(8,128)S(1)} %dynamic-slice_bitcast_fusion.table, f32[3,2,536,128]{3,2,1,0:T(8,128)S(1)} %get-tuple-element.84.state, f32[3,2,528,128]{3,2,1,0:T(8,128)S(1)} %get-tuple-element.85.vels, ...), custom_call_target="tpu_custom_call", output_to_operand_aliasing={{0}: (4, {}), {1}: (5, {})} | custom-call | bytes 2879999 | tf_op jit(solution)/shard_map/bulk_step/pallas_call | solution.py:526
  49.1 0.8 %bulk_step.19 = (f32[3,2,536,128]{3,2,1,0:T(8,128)S(1)}, f32[3,2,528,128]{3,2,1,0:T(8,128)S(1)}) custom-call(f32[16,128]{1,0:T(8,128)S(1)} %dynamic-slice_bitcast_fusion.table, f32[3,2,536,128]{3,2,1,0:T(8,128)S(1)} %get-tuple-element.90.state, f32[3,2,528,128]{3,2,1,0:T(8,128)S(1)} %get-tuple-element.91.vels, ...), custom_call_target="tpu_custom_call", output_to_operand_aliasing={{0}: (4, {}), {1}: (5, {})} | custom-call | bytes 2879999 | tf_op jit(solution)/shard_map/bulk_step/pallas_call | solution.py:526
  49.9 1.2 %collective-permute-done.13.second = f32[4,16,128]{2,1,0:T(8,128)S(1)} collective-permute-done((f32[4,16,128]{2,1,0:T(8,128)S(1)}, f32[4,16,128]{2,1,0:T(8,128)S(1)}, u32[]{:S(2)}, u32[]{:S(2)}) %collective-permute-start.13) | collective-permute-done | bytes 32800 | tf_op jit(solution)/shard_map/ppermute | solution.py:546
  51.2 0.8 %bulk_step.20 = (f32[3,2,536,128]{3,2,1,0:T(8,128)S(1)}, f32[3,2,528,128]{3,2,1,0:T(8,128)S(1)}) custom-call(f32[16,128]{1,0:T(8,128)S(1)} %dynamic-slice_bitcast_fusion.table, f32[3,2,536,128]{3,2,1,0:T(8,128)S(1)} %get-tuple-element.90.state, f32[3,2,528,128]{3,2,1,0:T(8,128)S(1)} %get-tuple-element.91.vels, ...), custom_call_target="tpu_custom_call", output_to_operand_aliasing={{0}: (4, {}), {1}: (5, {})} | custom-call | bytes 2879999 | tf_op jit(solution)/shard_map/bulk_step/pallas_call | solution.py:526
  52.7 0.8 %bulk_step.22 = (f32[3,2,536,128]{3,2,1,0:T(8,128)S(1)}, f32[3,2,528,128]{3,2,1,0:T(8,128)S(1)}) custom-call(f32[16,128]{1,0:T(8,128)S(1)} %dynamic-slice_bitcast_fusion.table, f32[3,2,536,128]{3,2,1,0:T(8,128)S(1)} %get-tuple-element.97.state, f32[3,2,528,128]{3,2,1,0:T(8,128)S(1)} %get-tuple-element.98.vels, ...), custom_call_target="tpu_custom_call", output_to_operand_aliasing={{0}: (4, {}), {1}: (5, {})} | custom-call | bytes 2879999 | tf_op jit(solution)/shard_map/bulk_step/pallas_call | solution.py:526
  53.5 0.8 %bulk_step.23 = (f32[3,2,536,128]{3,2,1,0:T(8,128)S(1)}, f32[3,2,528,128]{3,2,1,0:T(8,128)S(1)}) custom-call(f32[16,128]{1,0:T(8,128)S(1)} %dynamic-slice_bitcast_fusion.table, f32[3,2,536,128]{3,2,1,0:T(8,128)S(1)} %get-tuple-element.97.state, f32[3,2,528,128]{3,2,1,0:T(8,128)S(1)} %get-tuple-element.98.vels, ...), custom_call_target="tpu_custom_call", output_to_operand_aliasing={{0}: (4, {}), {1}: (5, {})} | custom-call | bytes 2879999 | tf_op jit(solution)/shard_map/bulk_step/pallas_call | solution.py:526
  54.3 0.8 %collective-permute-done.14.got = f32[4,16,128]{2,1,0:T(8,128)S(1)} collective-permute-done((f32[4,16,128]{2,1,0:T(8,128)S(1)}, f32[4,16,128]{2,1,0:T(8,128)S(1)}, u32[]{:S(2)}, u32[]{:S(2)}) %collective-permute-start.14) | collective-permute-done | bytes 32800 | tf_op jit(solution)/shard_map/ppermute | solution.py:552
  55.3 1.9 %bulk_store.1 = (f32[3,512,128]{2,1,0:T(8,128)}, f32[3,512,128]{2,1,0:T(8,128)}, f32[8,128]{1,0:T(8,128)S(1)}) custom-call(s32[2]{0:T(128)S(1)} %get-tuple-element.58.where_ref, f32[3,2,536,128]{3,2,1,0:T(8,128)S(1)} %get-tuple-element.103.rest_0_.state, f32[3,2,528,128]{3,2,1,0:T(8,128)S(1)} %get-tuple-element.104.vels, ...), custom_call_target="tpu_custom_call" | custom-call | bytes 7200000 | tf_op jit(solution)/shard_map/bulk_store/pallas_call | solution.py:526
  57.2 3.0 %collective-permute-done.15.got = f32[2,16,128]{2,1,0:T(8,128)S(1)} collective-permute-done((f32[2,16,128]{2,1,0:T(8,128)S(1)}, f32[2,16,128]{2,1,0:T(8,128)S(1)}, u32[]{:S(2)}, u32[]{:S(2)}) %collective-permute-start.15) | collective-permute-done | bytes 16416 | tf_op jit(solution)/shard_map/ppermute | solution.py:557
  60.2 3.6 %collective-permute-done.16.handed = f32[1,16,128]{2,1,0:T(8,128)S(1)} collective-permute-done((f32[1,16,128]{2,1,0:T(8,128)S(1)}, f32[1,16,128]{2,1,0:T(8,128)S(1)}, u32[]{:S(2)}, u32[]{:S(2)}) %collective-permute-start.16) | collective-permute-done | bytes 8224 | tf_op jit(solution)/shard_map/ppermute | solution.py:562
  (55 shorter events, 5.7 us)
Async XLA Ops:
  0.6 12.7 %copy-start.6 = (s32[168]{0:T(256)S(1)}, s32[168]{0:T(256)}, u32[]{:S(2)}) copy-start(s32[168]{0:T(256)} %constant.13.clone.static_ref) | copy-start | bytes 2020
  0.6 16.3 %copy-start = (f32[3,512,128]{2,1,0:T(8,128)S(1)}, f32[3,512,128]{2,1,0:T(8,128)}, u32[]{:S(2)}) copy-start(f32[3,512,128]{2,1,0:T(8,128)} %refs_0_.5) | copy-start | bytes 2359300
  0.7 16.3 %copy-start.1 = (f32[3,512,128]{2,1,0:T(8,128)S(1)}, f32[3,512,128]{2,1,0:T(8,128)}, u32[]{:S(2)}) copy-start(f32[3,512,128]{2,1,0:T(8,128)} %refs_1_.5) | copy-start | bytes 2359300
  0.7 16.3 %copy-start.2 = (f32[512,128]{1,0:T(8,128)S(1)}, f32[512,128]{1,0:T(8,128)}, u32[]{:S(2)}) copy-start(f32[512,128]{1,0:T(8,128)} %refs_2_.5) | copy-start | bytes 786436
  0.7 16.3 %copy-start.3 = (f32[512,128]{1,0:T(8,128)S(1)}, f32[512,128]{1,0:T(8,128)}, u32[]{:S(2)}) copy-start(f32[512,128]{1,0:T(8,128)} %refs_3_.5) | copy-start | bytes 786436
  0.7 12.6 %copy-start.8 = (f32[40]{0:T(128)S(1)}, f32[40]{0:T(128)}, u32[]{:S(2)}) copy-start(f32[40]{0:T(128)} %lift_ref.1) | copy-start | bytes 484
  0.7 12.6 %copy-start.7 = (s32[40]{0:T(128)S(1)}, s32[40]{0:T(128)}, u32[]{:S(2)}) copy-start(s32[40]{0:T(128)} %slot_ref.1) | copy-start | bytes 484
  2.7 14.3 %collective-permute-start.1 = (f32[8,48,128]{2,1,0:T(8,128)}, f32[8,48,128]{2,1,0:T(8,128)S(1)}, u32[]{:S(2)}, u32[]{:S(2)}) collective-permute-start(f32[8,48,128]{2,1,0:T(8,128)} %get-tuple-element.59), channel_id=1, source_target_pairs={{0,2},{2,0},{4,6},{6,4},{8,10},{10,8},{12,14},{14,12},{16,18},{18,... | collective-permute-start | bytes 589832 | tf_op jit(solution)/shard_map/ppermute | solution.py:612
  2.8 14.2 %collective-permute-start.2 = (f32[8,48,128]{2,1,0:T(8,128)}, f32[8,48,128]{2,1,0:T(8,128)S(1)}, u32[]{:S(2)}, u32[]{:S(2)}) collective-permute-start(f32[8,48,128]{2,1,0:T(8,128)} %get-tuple-element.60), channel_id=1, source_target_pairs={{2,4},{4,2},{6,8},{8,6},{10,12},{12,10},{14,16},{16,14},{18,20},{2... | collective-permute-start | bytes 589832 | tf_op jit(solution)/shard_map/ppermute | solution.py:612
  10.4 1.4 %collective-permute-start = (f32[1,16,128]{2,1,0:T(8,128)}, f32[1,16,128]{2,1,0:T(8,128)S(1)}, u32[]{:S(2)}, u32[]{:S(2)}) collective-permute-start(f32[1,16,128]{2,1,0:T(8,128)} %before.1), channel_id=1, source_target_pairs={{0,2},{2,0},{4,6},{6,4},{8,10},{10,8},{12,14},{14,12},{16,18},{18,... | collective-permute-start | bytes 24584 | tf_op jit(solution)/shard_map/ppermute | solution.py:542
  11.8 0.7 %copy-start.4 = (f32[1,16,128]{2,1,0:T(8,128)S(1)}, f32[1,16,128]{2,1,0:T(8,128)}, u32[]{:S(2)}) copy-start(f32[1,16,128]{2,1,0:T(8,128)} %before.1) | copy-start | bytes 24580
  12.5 3.7 %collective-permute-start.3 = (f32[2,16,128]{2,1,0:T(8,128)S(1)}, f32[2,16,128]{2,1,0:T(8,128)S(1)}, u32[]{:S(2)}, u32[]{:S(2)}) collective-permute-start(f32[2,16,128]{2,1,0:T(8,128)S(1)} %stack.4.rest_0_.first), channel_id=1, source_target_pairs={{0,32},{2,34},{4,36},{6,38},{8,40},{10,42},{12,44},{14,46},{16,48}... | collective-permute-start | bytes 49160 | tf_op jit(solution)/shard_map/ppermute | solution.py:544
  13.3 21.8 %copy-start.9 = (f32[2,16,128]{2,1,0:T(8,128)S(1)}, f32[2,16,128]{2,1,0:T(8,128)}, u32[]{:S(2)}) copy-start(f32[2,16,128]{2,1,0:T(8,128)} %constant.12.clone) | copy-start | bytes 49156
  16.2 5.1 %collective-permute-start.5 = (f32[4,16,128]{2,1,0:T(8,128)S(1)}, f32[4,16,128]{2,1,0:T(8,128)S(1)}, u32[]{:S(2)}, u32[]{:S(2)}) collective-permute-start(f32[4,16,128]{2,1,0:T(8,128)S(1)} %stack.5.refs_6_.first), channel_id=1, source_target_pairs={{0,96},{2,98},{4,100},{6,102},{8,104},{10,106},{12,108},{14,110},{... | collective-permute-start | bytes 98312 | tf_op jit(solution)/shard_map/ppermute | solution.py:546
  21.4 4.0 %collective-permute-start.6 = (f32[4,16,128]{2,1,0:T(8,128)S(1)}, f32[4,16,128]{2,1,0:T(8,128)S(1)}, u32[]{:S(2)}, u32[]{:S(2)}) collective-permute-start(f32[4,16,128]{2,1,0:T(8,128)S(1)} %get-tuple-element.71), channel_id=1, source_target_pairs={{0,8},{2,10},{4,12},{6,14},{8,0},{10,2},{12,4},{14,6},{16,24},{18,... | collective-permute-start | bytes 98312 | tf_op jit(solution)/shard_map/ppermute | solution.py:552
  21.5 13.7 %collective-permute-start.4 = (f32[304,128]{1,0:T(8,128)S(1)}, f32[304,128]{1,0:T(8,128)S(1)}, u32[]{:S(2)}, u32[]{:S(2)}) collective-permute-start(f32[304,128]{1,0:T(8,128)S(1)} %pack.1.rest_0_), channel_id=1, source_target_pairs={{0,1},{1,0},{2,3},{3,2},{4,5},{5,4},{6,7},{7,6},{8,9},{9,8},{10,11... | collective-permute-start | bytes 466952 | tf_op jit(solution)/shard_map/ppermute | solution.py:671
  25.4 5.0 %collective-permute-start.7 = (f32[2,16,128]{2,1,0:T(8,128)S(1)}, f32[2,16,128]{2,1,0:T(8,128)S(1)}, u32[]{:S(2)}, u32[]{:S(2)}) collective-permute-start(f32[2,16,128]{2,1,0:T(8,128)S(1)} %get-tuple-element.73), channel_id=1, source_target_pairs={{0,24},{2,26},{4,28},{6,30},{8,16},{10,18},{12,20},{14,22},{16,8},... | collective-permute-start | bytes 49160 | tf_op jit(solution)/shard_map/ppermute | solution.py:557
  30.4 8.2 %collective-permute-start.10 = (f32[1,16,128]{2,1,0:T(8,128)S(1)}, f32[1,16,128]{2,1,0:T(8,128)S(1)}, u32[]{:S(2)}, u32[]{:S(2)}) collective-permute-start(f32[1,16,128]{2,1,0:T(8,128)S(1)} %get-tuple-element.75), channel_id=1, source_target_pairs={{0,5},{1,4},{2,7},{3,6},{4,1},{5,0},{6,3},{7,2},{8,13},{9,12},{10,... | collective-permute-start | bytes 24584 | tf_op jit(solution)/shard_map/ppermute | solution.py:682
  30.4 8.2 %collective-permute-start.8 = (f32[1,16,128]{2,1,0:T(8,128)S(1)}, f32[1,16,128]{2,1,0:T(8,128)S(1)}, u32[]{:S(2)}, u32[]{:S(2)}) collective-permute-start(f32[1,16,128]{2,1,0:T(8,128)S(1)} %get-tuple-element.75), channel_id=1, source_target_pairs={{0,4},{2,6},{4,0},{6,2},{8,12},{10,14},{12,8},{14,10},{16,20},{18,... | collective-permute-start | bytes 24584 | tf_op jit(solution)/shard_map/ppermute | solution.py:562
  33.1 5.6 %collective-permute-start.9 = (f32[1,16,128]{2,1,0:T(8,128)S(1)}, f32[1,16,128]{2,1,0:T(8,128)S(1)}, u32[]{:S(2)}, u32[]{:S(2)}) collective-permute-start(f32[1,16,128]{2,1,0:T(8,128)S(1)} %get-tuple-element.74.kept), channel_id=1, source_target_pairs={{0,1},{1,0},{2,3},{3,2},{4,5},{5,4},{6,7},{7,6},{8,9},{9,8},{10,11... | collective-permute-start | bytes 24584 | tf_op jit(solution)/shard_map/ppermute | solution.py:681
  41.0 1.3 %collective-permute-start.11 = (f32[1,16,128]{2,1,0:T(8,128)S(1)}, f32[1,16,128]{2,1,0:T(8,128)S(1)}, u32[]{:S(2)}, u32[]{:S(2)}) collective-permute-start(f32[1,16,128]{2,1,0:T(8,128)S(1)} %get-tuple-element.76.first), channel_id=1, source_target_pairs={{0,2},{2,0},{4,6},{6,4},{8,10},{10,8},{12,14},{14,12},{16,18},{18,... | collective-permute-start | bytes 24584 | tf_op jit(solution)/shard_map/ppermute | solution.py:542
  42.2 3.7 %collective-permute-start.12 = (f32[2,16,128]{2,1,0:T(8,128)S(1)}, f32[2,16,128]{2,1,0:T(8,128)S(1)}, u32[]{:S(2)}, u32[]{:S(2)}) collective-permute-start(f32[2,16,128]{2,1,0:T(8,128)S(1)} %stack.6.rest_0_.rest_2_.first), channel_id=1, source_target_pairs={{0,32},{2,34},{4,36},{6,38},{8,40},{10,42},{12,44},{14,46},{16,48}... | collective-permute-start | bytes 49160 | tf_op jit(solution)/shard_map/ppermute | solution.py:544
  46.0 5.1 %collective-permute-start.13 = (f32[4,16,128]{2,1,0:T(8,128)S(1)}, f32[4,16,128]{2,1,0:T(8,128)S(1)}, u32[]{:S(2)}, u32[]{:S(2)}) collective-permute-start(f32[4,16,128]{2,1,0:T(8,128)S(1)} %stack.7.rest_2_.rest_0_.first), channel_id=1, source_target_pairs={{0,96},{2,98},{4,100},{6,102},{8,104},{10,106},{12,108},{14,110},{... | collective-permute-start | bytes 98312 | tf_op jit(solution)/shard_map/ppermute | solution.py:546
  51.1 4.0 %collective-permute-start.14 = (f32[4,16,128]{2,1,0:T(8,128)S(1)}, f32[4,16,128]{2,1,0:T(8,128)S(1)}, u32[]{:S(2)}, u32[]{:S(2)}) collective-permute-start(f32[4,16,128]{2,1,0:T(8,128)S(1)} %get-tuple-element.96.rest_2_.rest_0_), channel_id=1, source_target_pairs={{0,8},{2,10},{4,12},{6,14},{8,0},{10,2},{12,4},{14,6},{16,24},{18,... | collective-permute-start | bytes 98312 | tf_op jit(solution)/shard_map/ppermute | solution.py:552
  55.2 5.0 %collective-permute-start.15 = (f32[2,16,128]{2,1,0:T(8,128)S(1)}, f32[2,16,128]{2,1,0:T(8,128)S(1)}, u32[]{:S(2)}, u32[]{:S(2)}) collective-permute-start(f32[2,16,128]{2,1,0:T(8,128)S(1)} %get-tuple-element.106.rest_0_), channel_id=1, source_target_pairs={{0,24},{2,26},{4,28},{6,30},{8,16},{10,18},{12,20},{14,22},{16,8},... | collective-permute-start | bytes 49160 | tf_op jit(solution)/shard_map/ppermute | solution.py:557
  55.3 8.6 %copy-start.5 = (f32[1,16,128]{2,1,0:T(8,128)S(1)}, f32[1,16,128]{2,1,0:T(8,128)}, u32[]{:S(2)}) copy-start(f32[1,16,128]{2,1,0:T(8,128)} %before.1) | copy-start | bytes 24580
  60.2 3.7 %collective-permute-start.16 = (f32[1,16,128]{2,1,0:T(8,128)S(1)}, f32[1,16,128]{2,1,0:T(8,128)S(1)}, u32[]{:S(2)}, u32[]{:S(2)}) collective-permute-start(f32[1,16,128]{2,1,0:T(8,128)S(1)} %get-tuple-element.112), channel_id=1, source_target_pairs={{0,4},{2,6},{4,0},{6,2},{8,12},{10,14},{12,8},{14,10},{16,20},{18,... | collective-permute-start | bytes 24584 | tf_op jit(solution)/shard_map/ppermute | solution.py:562

commit v7 on v6

--- a/solution.py
+++ b/solution.py
@@ -410,7 +410,7 @@
 
 
 def bulk_load_kernel(half, base, cycle_total, rows, *refs):
-    fields, (inner, outer, columns, state, vels, coef) = refs[:4], refs[4:]
+    fields, (inner, outer, columns), (state, vels, coef) = refs[:4], refs[4:7], refs[-3:]
     first_row = HALO - 8
     odd = (lax.axis_index("arc") & 1) > 0
 
@@ -629,10 +629,10 @@
             (kept["plan"][1], *fields, *ends, kept["columns"]), in_specs=[SMEM] + [VMEM] * 7, micros=0.8,
         )
 
-    def load_bulk():
+    def load_bulk(value):
         return call(
             functools.partial(bulk_load_kernel, half, base, cycle_total, rows), "bulk_load", buffers(rows),
-            (*fields, *ends, kept["columns"]), micros=2.0,
+            (*fields, *ends, kept["columns"]), micros=2.0, after=(value,),
         )
 
     def step_bulk(value, count):
@@ -672,8 +672,7 @@
             return (pack,)
         if stage == 5:
             kept["window"] = load_window()
-            kept["bulk"] = load_bulk()
-            return (kept["window"][0], kept["bulk"][0])
+            return kept["window"][:1]
         return ()
 
     mine, near, done, sent = route(pad_state, kept, 0, going)
@@ -704,9 +703,10 @@
                 scratch=room(WIN), micros=0.6,
             )
             return (kept["last"],)
-        if stage == 4:
-            return store_bulk(value)
-        return step_bulk(value, 4) if stage < 4 else ()
+        if stage == 1:
+            kept["bulk"] = load_bulk(value)
+            return kept["bulk"][:1]
+        return store_bulk(value) if stage == 5 else step_bulk(value, 4)
 
     pads, handed, done, _ = route(pad_new, kept, 1, coming)
     pad_result = call(last_kernel, "last", real(1, slots, LANES), (plan, pads, handed, pad_state), after=done)

time: 64.7 us -> 64.3 us (level)
    ppermute x1, waiting for transfers between devices: 0.01 us -> 2.24 us  [local(): far = lax.ppermute(mine, 'circ', swap)]
    ppermute x2, waiting for transfers between devices: 3.64 us -> 1.66 us  [route(): return (keep, lax.ppermute(send, 'arc', flips(x=1)), between(5, send), send)]
    ppermute x2, waiting for transfers between devices: 7.88 us -> 6.72 us  [route(): got = lax.ppermute(send, 'arc', flips(z=3))]
  transfers between devices with their start and end apart: 17 -> 17, of which waited for: 11 -> 12; matrix products, arithmetic and copies ran while one was open for 1% -> 1% of each run, Pallas kernels for 26% -> 26%
where the time goes in v7:
time: 64.3 us; the launch traced here: 64 us
  waiting for transfers between devices  22.4 us (35%)
  Pallas kernels  21.8 us (34%)
  starting transfers between devices  17.3 us (27%)
  local copies, waits for them, and re-layouts  1.58 us (2%)
  between operations  0.99 us (2%)
    pallas_call x31, Pallas kernels, call(): pl.pallas_call(kernel, out_shape=shapes, in_specs=list(in_specs or [VMEM]...  21.8 us
    ppermute x1, starting transfers between devices, local(): lax.ppermute(outer, 'arc', outward)  7.6 us
    ppermute x2, waiting for transfers between devices, route(): got = lax.ppermute(send, 'arc', flips(z=3))  6.72 us
    ppermute x2, waiting for transfers between devices, route(): got = lax.ppermute(held, 'arc', flips(y=3))  4.99 us
    ppermute x1, starting transfers between devices, going(): kept['columns'] = lax.ppermute(pack, 'circ', swap)  2.81 us
    ppermute x2, starting transfers between devices, route(): return (keep, lax.ppermute(send, 'arc', flips(x=1)), between(5, send), send)  2.74 us
    ppermute x2, waiting for transfers between devices, route(): got = lax.ppermute(held, 'arc', flips(y=1))  2.59 us
    ppermute x2, waiting for transfers between devices, route(): got = lax.ppermute(value, 'arc', flips(c=1))  2.32 us
  transfers between devices with their start and end apart: 17, of which 12 were waited for; matrix products, arithmetic and copies ran while one was open for 1% of the time, Pallas kernels for 26%

profile of v7, /device:TPU:0, one launch (start us, length us, event | category | flops | bytes accessed | tf_op | source)
XLA Modules:
  0.0 64.0 jit_solution(13687156803510456088)
XLA Ops:
  0.7 2.0 %edge.1 = (f32[8,48,128]{2,1,0:T(8,128)}, f32[8,48,128]{2,1,0:T(8,128)}) custom-call(f32[3,512,128]{2,1,0:T(8,128)} %refs_0_.5, f32[3,512,128]{2,1,0:T(8,128)} %refs_1_.5, f32[512,128]{1,0:T(8,128)} %refs_2_.5, f32[512,128]{1,0:T(8,128)} %refs_3_.5), custom_call_target="tpu_custom_call" | custom-call | bytes 7200000 | tf_op jit(solution)/shard_map/edge/pallas_call | solution.py:526
  2.8 7.6 %collective-permute-start.2 = (f32[8,48,128]{2,1,0:T(8,128)}, f32[8,48,128]{2,1,0:T(8,128)S(1)}, u32[]{:S(2)}, u32[]{:S(2)}) collective-permute-start(f32[8,48,128]{2,1,0:T(8,128)} %get-tuple-element.60), channel_id=1, source_target_pairs={{2,4},{4,2},{6,8},{8,6},{10,12},{12,10},{14,16},{16,14},{18,20},{2... | collective-permute-start | bytes 589832 | tf_op jit(solution)/shard_map/ppermute | solution.py:612
  10.4 1.4 %collective-permute-done.second = f32[1,16,128]{2,1,0:T(8,128)S(1)} collective-permute-done((f32[1,16,128]{2,1,0:T(8,128)}, f32[1,16,128]{2,1,0:T(8,128)S(1)}, u32[]{:S(2)}, u32[]{:S(2)}) %collective-permute-start) | collective-permute-done | bytes 8224 | tf_op jit(solution)/shard_map/ppermute | solution.py:542
  12.5 0.8 %copy.29.rows_ref = s32[4,40,16]{2,1,0:T(8,128)S(1)} copy(s32[4,40,16]{1,2,0:T(8,128)} %param.16) | data formatting | bytes 20480 | tf_op args[6]
  13.3 1.3 %plan.1 = (s32[32,128]{1,0:T(8,128)S(1)}, s32[2]{0:T(128)S(1)}, s32[4,16]{1,0:T(4,128)S(1)}, f32[1]{0:T(128)}) custom-call(s32[40]{0:T(128)S(1)} %copy-done.7, f32[40]{0:T(128)S(1)} %copy-done.8, s32[4,40,16]{2,1,0:T(8,128)S(1)} %copy.29.rows_ref, s32[168]{0:T(256)S(1)} %copy-done.6, f32[2,16,128]{2,1,0:T(8,128)S(1)} %stack.4.rest_0_.first), custom_call_target="tpu_custom_call" | custom-call | bytes 5400000 | tf_op jit(solution)/shard_map/plan/pallas_call | solution.py:526
  14.7 1.5 %collective-permute-done.3.second = f32[2,16,128]{2,1,0:T(8,128)S(1)} collective-permute-done((f32[2,16,128]{2,1,0:T(8,128)S(1)}, f32[2,16,128]{2,1,0:T(8,128)S(1)}, u32[]{:S(2)}, u32[]{:S(2)}) %collective-permute-start.3) | collective-permute-done | bytes 16416 | tf_op jit(solution)/shard_map/ppermute | solution.py:544
  17.7 3.6 %collective-permute-done.5.second = f32[4,16,128]{2,1,0:T(8,128)S(1)} collective-permute-done((f32[4,16,128]{2,1,0:T(8,128)S(1)}, f32[4,16,128]{2,1,0:T(8,128)S(1)}, u32[]{:S(2)}, u32[]{:S(2)}) %collective-permute-start.5) | collective-permute-done | bytes 32800 | tf_op jit(solution)/shard_map/ppermute | solution.py:546
  21.5 2.8 %collective-permute-start.4 = (f32[304,128]{1,0:T(8,128)S(1)}, f32[304,128]{1,0:T(8,128)S(1)}, u32[]{:S(2)}, u32[]{:S(2)}) collective-permute-start(f32[304,128]{1,0:T(8,128)S(1)} %pack.1.rest_0_), channel_id=1, source_target_pairs={{0,1},{1,0},{2,3},{3,2},{4,5},{5,4},{6,7},{7,6},{8,9},{9,8},{10,11... | collective-permute-start | bytes 466952 | tf_op jit(solution)/shard_map/ppermute | solution.py:671
  24.3 1.1 %collective-permute-done.6.got = f32[4,16,128]{2,1,0:T(8,128)S(1)} collective-permute-done((f32[4,16,128]{2,1,0:T(8,128)S(1)}, f32[4,16,128]{2,1,0:T(8,128)S(1)}, u32[]{:S(2)}, u32[]{:S(2)}) %collective-permute-start.6) | collective-permute-done | bytes 32800 | tf_op jit(solution)/shard_map/ppermute | solution.py:552
  25.5 4.9 %collective-permute-done.7.got = f32[2,16,128]{2,1,0:T(8,128)S(1)} collective-permute-done((f32[2,16,128]{2,1,0:T(8,128)S(1)}, f32[2,16,128]{2,1,0:T(8,128)S(1)}, u32[]{:S(2)}, u32[]{:S(2)}) %collective-permute-start.7) | collective-permute-done | bytes 16416 | tf_op jit(solution)/shard_map/ppermute | solution.py:557
  30.4 2.7 %collective-permute-start.8 = (f32[1,16,128]{2,1,0:T(8,128)S(1)}, f32[1,16,128]{2,1,0:T(8,128)S(1)}, u32[]{:S(2)}, u32[]{:S(2)}) collective-permute-start(f32[1,16,128]{2,1,0:T(8,128)S(1)} %get-tuple-element.72), channel_id=1, source_target_pairs={{0,4},{2,6},{4,0},{6,2},{8,12},{10,14},{12,8},{14,10},{16,20},{18,... | collective-permute-start | bytes 24584 | tf_op jit(solution)/shard_map/ppermute | solution.py:562
  33.1 2.0 %collective-permute-start.9 = (f32[1,16,128]{2,1,0:T(8,128)S(1)}, f32[1,16,128]{2,1,0:T(8,128)S(1)}, u32[]{:S(2)}, u32[]{:S(2)}) collective-permute-start(f32[1,16,128]{2,1,0:T(8,128)S(1)} %get-tuple-element.71.kept), channel_id=1, source_target_pairs={{0,1},{1,0},{2,3},{3,2},{4,5},{5,4},{6,7},{7,6},{8,9},{9,8},{10,11... | collective-permute-start | bytes 24584 | tf_op jit(solution)/shard_map/ppermute | solution.py:680
  35.1 0.9 %window_load.1 = (f32[3,2,72,128]{3,2,1,0:T(8,128)S(1)}, f32[3,2,64,128]{3,2,1,0:T(8,128)S(1)}, f32[4,2,64,128]{3,2,1,0:T(8,128)S(1)}) custom-call(s32[2]{0:T(128)S(1)} %get-tuple-element.58.where_ref, f32[3,512,128]{2,1,0:T(8,128)S(1)} %copy-done, f32[3,512,128]{2,1,0:T(8,128)S(1)} %copy-done.1, f32[512,128]{1,0:T(8,128)S(1)} %copy-done.2, ...), custom_call_target="tpu_custom_call" | custom-call | bytes 2880000 | tf_op jit(solution)/shard_map/window_load/pallas_call | solution.py:526
  36.0 2.2 %collective-permute-done.9.far = f32[1,16,128]{2,1,0:T(8,128)S(1)} collective-permute-done((f32[1,16,128]{2,1,0:T(8,128)S(1)}, f32[1,16,128]{2,1,0:T(8,128)S(1)}, u32[]{:S(2)}, u32[]{:S(2)}) %collective-permute-start.9) | collective-permute-done | bytes 8224 | tf_op jit(solution)/shard_map/ppermute | solution.py:680
  38.3 2.3 %window.1 = (f32[3,2,72,128]{3,2,1,0:T(8,128)S(1)}, f32[3,2,64,128]{3,2,1,0:T(8,128)S(1)}, f32[2,2,64,128]{3,2,1,0:T(8,128)S(1)}, f32[1,16,128]{2,1,0:T(8,128)S(1)}) custom-call(s32[4,16]{1,0:T(4,128)S(1)} %get-tuple-element.62.list_ref, f32[1]{0:T(128)} %get-tuple-element.63.lift_ref, s32[32,128]{1,0:T(8,128)S(1)} %get-tuple-element.61.rest_0_.plan, ...), custom_call_target="tpu_custom_call" | custom-call | bytes 7200000 | tf_op jit(solution)/shard_map/window/pallas_call | solution.py:526
  40.9 0.9 %collective-permute-done.11.second = f32[1,16,128]{2,1,0:T(8,128)S(1)} collective-permute-done((f32[1,16,128]{2,1,0:T(8,128)S(1)}, f32[1,16,128]{2,1,0:T(8,128)S(1)}, u32[]{:S(2)}, u32[]{:S(2)}) %collective-permute-start.11) | collective-permute-done | bytes 8224 | tf_op jit(solution)/shard_map/ppermute | solution.py:542
  41.8 2.6 %bulk_load.1 = (f32[3,2,536,128]{3,2,1,0:T(8,128)S(1)}, f32[3,2,528,128]{3,2,1,0:T(8,128)S(1)}, f32[4,2,528,128]{3,2,1,0:T(8,128)S(1)}) custom-call(f32[3,512,128]{2,1,0:T(8,128)S(1)} %copy-done, f32[3,512,128]{2,1,0:T(8,128)S(1)} %copy-done.1, f32[512,128]{1,0:T(8,128)S(1)} %copy-done.2, f32[512,128]{1,0:T(8,128)S(1)} %copy-done.3, ...), custom_call_target="tpu_custom_call" | custom-call | bytes 7200000 | tf_op jit(solution)/shard_map/bulk_load/pallas_call | solution.py:526
  44.5 1.1 %collective-permute-done.12.second = f32[2,16,128]{2,1,0:T(8,128)S(1)} collective-permute-done((f32[2,16,128]{2,1,0:T(8,128)S(1)}, f32[2,16,128]{2,1,0:T(8,128)S(1)}, u32[]{:S(2)}, u32[]{:S(2)}) %collective-permute-start.12) | collective-permute-done | bytes 16416 | tf_op jit(solution)/shard_map/ppermute | solution.py:544
  45.6 0.8 %collective-permute-start.13 = (f32[4,16,128]{2,1,0:T(8,128)S(1)}, f32[4,16,128]{2,1,0:T(8,128)S(1)}, u32[]{:S(2)}, u32[]{:S(2)}) collective-permute-start(f32[4,16,128]{2,1,0:T(8,128)S(1)} %stack.7.rest_0_.rest_2_.first), channel_id=1, source_target_pairs={{0,96},{2,98},{4,100},{6,102},{8,104},{10,106},{12,108},{14,110},{... | collective-permute-start | bytes 98312 | tf_op jit(solution)/shard_map/ppermute | solution.py:546
  47.0 0.8 %bulk_step.13 = (f32[3,2,536,128]{3,2,1,0:T(8,128)S(1)}, f32[3,2,528,128]{3,2,1,0:T(8,128)S(1)}) custom-call(f32[16,128]{1,0:T(8,128)S(1)} %dynamic-slice_bitcast_fusion.table, f32[3,2,536,128]{3,2,1,0:T(8,128)S(1)} %get-tuple-element.77.rest_0_.state, f32[3,2,528,128]{3,2,1,0:T(8,128)S(1)} %get-tuple-element.78.vels, ...), custom_call_target="tpu_custom_call", output_to_operand_aliasing={{0}: (4, {}), {1}: (5, {})} | custom-call | bytes 2879999 | tf_op jit(solution)/shard_map/bulk_step/pallas_call | solution.py:526
  47.8 0.8 %bulk_step.14 = (f32[3,2,536,128]{3,2,1,0:T(8,128)S(1)}, f32[3,2,528,128]{3,2,1,0:T(8,128)S(1)}) custom-call(f32[16,128]{1,0:T(8,128)S(1)} %dynamic-slice_bitcast_fusion.table, f32[3,2,536,128]{3,2,1,0:T(8,128)S(1)} %get-tuple-element.77.rest_0_.state, f32[3,2,528,128]{3,2,1,0:T(8,128)S(1)} %get-tuple-element.78.vels, ...), custom_call_target="tpu_custom_call", output_to_operand_aliasing={{0}: (4, {}), {1}: (5, {})} | custom-call | bytes 2879999 | tf_op jit(solution)/shard_map/bulk_step/pallas_call | solution.py:526
  49.3 1.4 %collective-permute-done.13.second = f32[4,16,128]{2,1,0:T(8,128)S(1)} collective-permute-done((f32[4,16,128]{2,1,0:T(8,128)S(1)}, f32[4,16,128]{2,1,0:T(8,128)S(1)}, u32[]{:S(2)}, u32[]{:S(2)}) %collective-permute-start.13) | collective-permute-done | bytes 32800 | tf_op jit(solution)/shard_map/ppermute | solution.py:546
  50.8 0.8 %bulk_step.16 = (f32[3,2,536,128]{3,2,1,0:T(8,128)S(1)}, f32[3,2,528,128]{3,2,1,0:T(8,128)S(1)}) custom-call(f32[16,128]{1,0:T(8,128)S(1)} %dynamic-slice_bitcast_fusion.table, f32[3,2,536,128]{3,2,1,0:T(8,128)S(1)} %get-tuple-element.84.state, f32[3,2,528,128]{3,2,1,0:T(8,128)S(1)} %get-tuple-element.85.vels, ...), custom_call_target="tpu_custom_call", output_to_operand_aliasing={{0}: (4, {}), {1}: (5, {})} | custom-call | bytes 2879999 | tf_op jit(solution)/shard_map/bulk_step/pallas_call | solution.py:526
  51.6 0.8 %bulk_step.17 = (f32[3,2,536,128]{3,2,1,0:T(8,128)S(1)}, f32[3,2,528,128]{3,2,1,0:T(8,128)S(1)}) custom-call(f32[16,128]{1,0:T(8,128)S(1)} %dynamic-slice_bitcast_fusion.table, f32[3,2,536,128]{3,2,1,0:T(8,128)S(1)} %get-tuple-element.84.state, f32[3,2,528,128]{3,2,1,0:T(8,128)S(1)} %get-tuple-element.85.vels, ...), custom_call_target="tpu_custom_call", output_to_operand_aliasing={{0}: (4, {}), {1}: (5, {})} | custom-call | bytes 2879999 | tf_op jit(solution)/shard_map/bulk_step/pallas_call | solution.py:526
  53.1 0.8 %bulk_step.19 = (f32[3,2,536,128]{3,2,1,0:T(8,128)S(1)}, f32[3,2,528,128]{3,2,1,0:T(8,128)S(1)}) custom-call(f32[16,128]{1,0:T(8,128)S(1)} %dynamic-slice_bitcast_fusion.table, f32[3,2,536,128]{3,2,1,0:T(8,128)S(1)} %get-tuple-element.91.state, f32[3,2,528,128]{3,2,1,0:T(8,128)S(1)} %get-tuple-element.92.vels, ...), custom_call_target="tpu_custom_call", output_to_operand_aliasing={{0}: (4, {}), {1}: (5, {})} | custom-call | bytes 2879999 | tf_op jit(solution)/shard_map/bulk_step/pallas_call | solution.py:526
  53.9 0.8 %collective-permute-done.14.got = f32[4,16,128]{2,1,0:T(8,128)S(1)} collective-permute-done((f32[4,16,128]{2,1,0:T(8,128)S(1)}, f32[4,16,128]{2,1,0:T(8,128)S(1)}, u32[]{:S(2)}, u32[]{:S(2)}) %collective-permute-start.14) | collective-permute-done | bytes 32800 | tf_op jit(solution)/shard_map/ppermute | solution.py:552
  54.9 0.8 %bulk_step.20 = (f32[3,2,536,128]{3,2,1,0:T(8,128)S(1)}, f32[3,2,528,128]{3,2,1,0:T(8,128)S(1)}) custom-call(f32[16,128]{1,0:T(8,128)S(1)} %dynamic-slice_bitcast_fusion.table, f32[3,2,536,128]{3,2,1,0:T(8,128)S(1)} %get-tuple-element.91.state, f32[3,2,528,128]{3,2,1,0:T(8,128)S(1)} %get-tuple-element.92.vels, ...), custom_call_target="tpu_custom_call", output_to_operand_aliasing={{0}: (4, {}), {1}: (5, {})} | custom-call | bytes 2879999 | tf_op jit(solution)/shard_map/bulk_step/pallas_call | solution.py:526
  56.4 0.8 %bulk_step.22 = (f32[3,2,536,128]{3,2,1,0:T(8,128)S(1)}, f32[3,2,528,128]{3,2,1,0:T(8,128)S(1)}) custom-call(f32[16,128]{1,0:T(8,128)S(1)} %dynamic-slice_bitcast_fusion.table, f32[3,2,536,128]{3,2,1,0:T(8,128)S(1)} %get-tuple-element.99.state, f32[3,2,528,128]{3,2,1,0:T(8,128)S(1)} %get-tuple-element.100.vels, ...), custom_call_target="tpu_custom_call", output_to_operand_aliasing={{0}: (4, {}), {1}: (5, {})} | custom-call | bytes 2879999 | tf_op jit(solution)/shard_map/bulk_step/pallas_call | solution.py:526
  57.2 0.8 %bulk_step.23 = (f32[3,2,536,128]{3,2,1,0:T(8,128)S(1)}, f32[3,2,528,128]{3,2,1,0:T(8,128)S(1)}) custom-call(f32[16,128]{1,0:T(8,128)S(1)} %dynamic-slice_bitcast_fusion.table, f32[3,2,536,128]{3,2,1,0:T(8,128)S(1)} %get-tuple-element.99.state, f32[3,2,528,128]{3,2,1,0:T(8,128)S(1)} %get-tuple-element.100.vels, ...), custom_call_target="tpu_custom_call", output_to_operand_aliasing={{0}: (4, {}), {1}: (5, {})} | custom-call | bytes 2879999 | tf_op jit(solution)/shard_map/bulk_step/pallas_call | solution.py:526
  58.0 1.8 %collective-permute-done.15.got = f32[2,16,128]{2,1,0:T(8,128)S(1)} collective-permute-done((f32[2,16,128]{2,1,0:T(8,128)S(1)}, f32[2,16,128]{2,1,0:T(8,128)S(1)}, u32[]{:S(2)}, u32[]{:S(2)}) %collective-permute-start.15) | collective-permute-done | bytes 16416 | tf_op jit(solution)/shard_map/ppermute | solution.py:557
  59.8 1.9 %bulk_store.1 = (f32[3,512,128]{2,1,0:T(8,128)}, f32[3,512,128]{2,1,0:T(8,128)}, f32[8,128]{1,0:T(8,128)S(1)}) custom-call(s32[2]{0:T(128)S(1)} %get-tuple-element.58.where_ref, f32[3,2,536,128]{3,2,1,0:T(8,128)S(1)} %get-tuple-element.105.rest_0_.state, f32[3,2,528,128]{3,2,1,0:T(8,128)S(1)} %get-tuple-element.106.vels, ...), custom_call_target="tpu_custom_call" | custom-call | bytes 7200000 | tf_op jit(solution)/shard_map/bulk_store/pallas_call | solution.py:526
  61.8 1.7 %collective-permute-done.16.handed = f32[1,16,128]{2,1,0:T(8,128)S(1)} collective-permute-done((f32[1,16,128]{2,1,0:T(8,128)S(1)}, f32[1,16,128]{2,1,0:T(8,128)S(1)}, u32[]{:S(2)}, u32[]{:S(2)}) %collective-permute-start.16) | collective-permute-done | bytes 8224 | tf_op jit(solution)/shard_map/ppermute | solution.py:562
  (55 shorter events, 6.5 us)
Async XLA Ops:
  0.6 12.7 %copy-start.6 = (s32[168]{0:T(256)S(1)}, s32[168]{0:T(256)}, u32[]{:S(2)}) copy-start(s32[168]{0:T(256)} %constant.13.clone.static_ref) | copy-start | bytes 2020
  0.6 16.3 %copy-start = (f32[3,512,128]{2,1,0:T(8,128)S(1)}, f32[3,512,128]{2,1,0:T(8,128)}, u32[]{:S(2)}) copy-start(f32[3,512,128]{2,1,0:T(8,128)} %refs_0_.5) | copy-start | bytes 2359300
  0.7 16.3 %copy-start.1 = (f32[3,512,128]{2,1,0:T(8,128)S(1)}, f32[3,512,128]{2,1,0:T(8,128)}, u32[]{:S(2)}) copy-start(f32[3,512,128]{2,1,0:T(8,128)} %refs_1_.5) | copy-start | bytes 2359300
  0.7 16.3 %copy-start.2 = (f32[512,128]{1,0:T(8,128)S(1)}, f32[512,128]{1,0:T(8,128)}, u32[]{:S(2)}) copy-start(f32[512,128]{1,0:T(8,128)} %refs_2_.5) | copy-start | bytes 786436
  0.7 16.3 %copy-start.3 = (f32[512,128]{1,0:T(8,128)S(1)}, f32[512,128]{1,0:T(8,128)}, u32[]{:S(2)}) copy-start(f32[512,128]{1,0:T(8,128)} %refs_3_.5) | copy-start | bytes 786436
  0.7 12.6 %copy-start.8 = (f32[40]{0:T(128)S(1)}, f32[40]{0:T(128)}, u32[]{:S(2)}) copy-start(f32[40]{0:T(128)} %lift_ref.1) | copy-start | bytes 484
  0.7 12.6 %copy-start.7 = (s32[40]{0:T(128)S(1)}, s32[40]{0:T(128)}, u32[]{:S(2)}) copy-start(s32[40]{0:T(128)} %slot_ref.1) | copy-start | bytes 484
  2.7 14.3 %collective-permute-start.1 = (f32[8,48,128]{2,1,0:T(8,128)}, f32[8,48,128]{2,1,0:T(8,128)S(1)}, u32[]{:S(2)}, u32[]{:S(2)}) collective-permute-start(f32[8,48,128]{2,1,0:T(8,128)} %get-tuple-element.59), channel_id=1, source_target_pairs={{0,2},{2,0},{4,6},{6,4},{8,10},{10,8},{12,14},{14,12},{16,18},{18,... | collective-permute-start | bytes 589832 | tf_op jit(solution)/shard_map/ppermute | solution.py:612
  2.8 14.2 %collective-permute-start.2 = (f32[8,48,128]{2,1,0:T(8,128)}, f32[8,48,128]{2,1,0:T(8,128)S(1)}, u32[]{:S(2)}, u32[]{:S(2)}) collective-permute-start(f32[8,48,128]{2,1,0:T(8,128)} %get-tuple-element.60), channel_id=1, source_target_pairs={{2,4},{4,2},{6,8},{8,6},{10,12},{12,10},{14,16},{16,14},{18,20},{2... | collective-permute-start | bytes 589832 | tf_op jit(solution)/shard_map/ppermute | solution.py:612
  10.4 1.4 %collective-permute-start = (f32[1,16,128]{2,1,0:T(8,128)}, f32[1,16,128]{2,1,0:T(8,128)S(1)}, u32[]{:S(2)}, u32[]{:S(2)}) collective-permute-start(f32[1,16,128]{2,1,0:T(8,128)} %before.1), channel_id=1, source_target_pairs={{0,2},{2,0},{4,6},{6,4},{8,10},{10,8},{12,14},{14,12},{16,18},{18,... | collective-permute-start | bytes 24584 | tf_op jit(solution)/shard_map/ppermute | solution.py:542
  11.8 0.7 %copy-start.4 = (f32[1,16,128]{2,1,0:T(8,128)S(1)}, f32[1,16,128]{2,1,0:T(8,128)}, u32[]{:S(2)}) copy-start(f32[1,16,128]{2,1,0:T(8,128)} %before.1) | copy-start | bytes 24580
  12.5 3.7 %collective-permute-start.3 = (f32[2,16,128]{2,1,0:T(8,128)S(1)}, f32[2,16,128]{2,1,0:T(8,128)S(1)}, u32[]{:S(2)}, u32[]{:S(2)}) collective-permute-start(f32[2,16,128]{2,1,0:T(8,128)S(1)} %stack.4.rest_0_.first), channel_id=1, source_target_pairs={{0,32},{2,34},{4,36},{6,38},{8,40},{10,42},{12,44},{14,46},{16,48}... | collective-permute-start | bytes 49160 | tf_op jit(solution)/shard_map/ppermute | solution.py:544
  13.3 21.8 %copy-start.9 = (f32[2,16,128]{2,1,0:T(8,128)S(1)}, f32[2,16,128]{2,1,0:T(8,128)}, u32[]{:S(2)}) copy-start(f32[2,16,128]{2,1,0:T(8,128)} %constant.12.clone) | copy-start | bytes 49156
  16.2 5.1 %collective-permute-start.5 = (f32[4,16,128]{2,1,0:T(8,128)S(1)}, f32[4,16,128]{2,1,0:T(8,128)S(1)}, u32[]{:S(2)}, u32[]{:S(2)}) collective-permute-start(f32[4,16,128]{2,1,0:T(8,128)S(1)} %stack.5.refs_6_.first), channel_id=1, source_target_pairs={{0,96},{2,98},{4,100},{6,102},{8,104},{10,106},{12,108},{14,110},{... | collective-permute-start | bytes 98312 | tf_op jit(solution)/shard_map/ppermute | solution.py:546
  21.4 4.0 %collective-permute-start.6 = (f32[4,16,128]{2,1,0:T(8,128)S(1)}, f32[4,16,128]{2,1,0:T(8,128)S(1)}, u32[]{:S(2)}, u32[]{:S(2)}) collective-permute-start(f32[4,16,128]{2,1,0:T(8,128)S(1)} %get-tuple-element.68), channel_id=1, source_target_pairs={{0,8},{2,10},{4,12},{6,14},{8,0},{10,2},{12,4},{14,6},{16,24},{18,... | collective-permute-start | bytes 98312 | tf_op jit(solution)/shard_map/ppermute | solution.py:552
  21.5 13.7 %collective-permute-start.4 = (f32[304,128]{1,0:T(8,128)S(1)}, f32[304,128]{1,0:T(8,128)S(1)}, u32[]{:S(2)}, u32[]{:S(2)}) collective-permute-start(f32[304,128]{1,0:T(8,128)S(1)} %pack.1.rest_0_), channel_id=1, source_target_pairs={{0,1},{1,0},{2,3},{3,2},{4,5},{5,4},{6,7},{7,6},{8,9},{9,8},{10,11... | collective-permute-start | bytes 466952 | tf_op jit(solution)/shard_map/ppermute | solution.py:671
  25.4 5.0 %collective-permute-start.7 = (f32[2,16,128]{2,1,0:T(8,128)S(1)}, f32[2,16,128]{2,1,0:T(8,128)S(1)}, u32[]{:S(2)}, u32[]{:S(2)}) collective-permute-start(f32[2,16,128]{2,1,0:T(8,128)S(1)} %get-tuple-element.70), channel_id=1, source_target_pairs={{0,24},{2,26},{4,28},{6,30},{8,16},{10,18},{12,20},{14,22},{16,8},... | collective-permute-start | bytes 49160 | tf_op jit(solution)/shard_map/ppermute | solution.py:557
  30.4 5.6 %collective-permute-start.10 = (f32[1,16,128]{2,1,0:T(8,128)S(1)}, f32[1,16,128]{2,1,0:T(8,128)S(1)}, u32[]{:S(2)}, u32[]{:S(2)}) collective-permute-start(f32[1,16,128]{2,1,0:T(8,128)S(1)} %get-tuple-element.72), channel_id=1, source_target_pairs={{0,5},{1,4},{2,7},{3,6},{4,1},{5,0},{6,3},{7,2},{8,13},{9,12},{10,... | collective-permute-start | bytes 24584 | tf_op jit(solution)/shard_map/ppermute | solution.py:681
  30.4 5.6 %collective-permute-start.8 = (f32[1,16,128]{2,1,0:T(8,128)S(1)}, f32[1,16,128]{2,1,0:T(8,128)S(1)}, u32[]{:S(2)}, u32[]{:S(2)}) collective-permute-start(f32[1,16,128]{2,1,0:T(8,128)S(1)} %get-tuple-element.72), channel_id=1, source_target_pairs={{0,4},{2,6},{4,0},{6,2},{8,12},{10,14},{12,8},{14,10},{16,20},{18,... | collective-permute-start | bytes 24584 | tf_op jit(solution)/shard_map/ppermute | solution.py:562
  33.1 5.2 %collective-permute-start.9 = (f32[1,16,128]{2,1,0:T(8,128)S(1)}, f32[1,16,128]{2,1,0:T(8,128)S(1)}, u32[]{:S(2)}, u32[]{:S(2)}) collective-permute-start(f32[1,16,128]{2,1,0:T(8,128)S(1)} %get-tuple-element.71.kept), channel_id=1, source_target_pairs={{0,1},{1,0},{2,3},{3,2},{4,5},{5,4},{6,7},{7,6},{8,9},{9,8},{10,11... | collective-permute-start | bytes 24584 | tf_op jit(solution)/shard_map/ppermute | solution.py:680
  40.6 1.3 %collective-permute-start.11 = (f32[1,16,128]{2,1,0:T(8,128)S(1)}, f32[1,16,128]{2,1,0:T(8,128)S(1)}, u32[]{:S(2)}, u32[]{:S(2)}) collective-permute-start(f32[1,16,128]{2,1,0:T(8,128)S(1)} %get-tuple-element.73.first), channel_id=1, source_target_pairs={{0,2},{2,0},{4,6},{6,4},{8,10},{10,8},{12,14},{14,12},{16,18},{18,... | collective-permute-start | bytes 24584 | tf_op jit(solution)/shard_map/ppermute | solution.py:542
  41.8 3.7 %collective-permute-start.12 = (f32[2,16,128]{2,1,0:T(8,128)S(1)}, f32[2,16,128]{2,1,0:T(8,128)S(1)}, u32[]{:S(2)}, u32[]{:S(2)}) collective-permute-start(f32[2,16,128]{2,1,0:T(8,128)S(1)} %stack.6.refs_7_.first), channel_id=1, source_target_pairs={{0,32},{2,34},{4,36},{6,38},{8,40},{10,42},{12,44},{14,46},{16,48}... | collective-permute-start | bytes 49160 | tf_op jit(solution)/shard_map/ppermute | solution.py:544
  45.6 5.1 %collective-permute-start.13 = (f32[4,16,128]{2,1,0:T(8,128)S(1)}, f32[4,16,128]{2,1,0:T(8,128)S(1)}, u32[]{:S(2)}, u32[]{:S(2)}) collective-permute-start(f32[4,16,128]{2,1,0:T(8,128)S(1)} %stack.7.rest_0_.rest_2_.first), channel_id=1, source_target_pairs={{0,96},{2,98},{4,100},{6,102},{8,104},{10,106},{12,108},{14,110},{... | collective-permute-start | bytes 98312 | tf_op jit(solution)/shard_map/ppermute | solution.py:546
  50.7 4.0 %collective-permute-start.14 = (f32[4,16,128]{2,1,0:T(8,128)S(1)}, f32[4,16,128]{2,1,0:T(8,128)S(1)}, u32[]{:S(2)}, u32[]{:S(2)}) collective-permute-start(f32[4,16,128]{2,1,0:T(8,128)S(1)} %get-tuple-element.88.rest_2_.rest_0_), channel_id=1, source_target_pairs={{0,8},{2,10},{4,12},{6,14},{8,0},{10,2},{12,4},{14,6},{16,24},{18,... | collective-permute-start | bytes 98312 | tf_op jit(solution)/shard_map/ppermute | solution.py:552
  54.8 5.0 %collective-permute-start.15 = (f32[2,16,128]{2,1,0:T(8,128)S(1)}, f32[2,16,128]{2,1,0:T(8,128)S(1)}, u32[]{:S(2)}, u32[]{:S(2)}) collective-permute-start(f32[2,16,128]{2,1,0:T(8,128)S(1)} %get-tuple-element.98.rest_2_.rest_0_), channel_id=1, source_target_pairs={{0,24},{2,26},{4,28},{6,30},{8,16},{10,18},{12,20},{14,22},{16,8},... | collective-permute-start | bytes 49160 | tf_op jit(solution)/shard_map/ppermute | solution.py:557
  59.8 3.7 %collective-permute-start.16 = (f32[1,16,128]{2,1,0:T(8,128)S(1)}, f32[1,16,128]{2,1,0:T(8,128)S(1)}, u32[]{:S(2)}, u32[]{:S(2)}) collective-permute-start(f32[1,16,128]{2,1,0:T(8,128)S(1)} %get-tuple-element.108.rest_0_), channel_id=1, source_target_pairs={{0,4},{2,6},{4,0},{6,2},{8,12},{10,14},{12,8},{14,10},{16,20},{18,... | collective-permute-start | bytes 24584 | tf_op jit(solution)/shard_map/ppermute | solution.py:562
  59.8 3.6 %copy-start.5 = (f32[1,16,128]{2,1,0:T(8,128)S(1)}, f32[1,16,128]{2,1,0:T(8,128)}, u32[]{:S(2)}) copy-start(f32[1,16,128]{2,1,0:T(8,128)} %before.1) | copy-start | bytes 24580
